TPU v7x, 512 devices: a whole 4x4x16 slice. The times are simulated.
512 devices in a mesh: ctx: 32 (over z_lo, x, core), ch: 16 (over z_hi, y).
Axes of the slice: x: 4, y: 4, z: 16 (z_hi: 4, z_lo: 4; z = z_hi * 4 + z_lo), core: 2. Of those that a mesh axis runs over, the one named last changes fastest.
Arguments:
- proj: bfloat16 [3, 4096, 8192], P(None, 'ch', 'ctx'), may hold values from -6 to 6
- short_filter: float32 [3, 4096, 3], P(None, 'ch'), may hold values from -3 to 3
- residues: float32 [4096, 16], P('ch'), may hold values from -1.8 to 1.8
- decays: float32 [4096, 16], P('ch'), may hold values from 6.1035156e-05 to 0.03
- skip: float32 [4096], P('ch'), may hold values from -1 to 1
- w_out: bfloat16 [4096, 4096], P(None, 'ch'), may hold values from -0.09375 to 0.09375
Outputs:
- mixed_out: bfloat16 [8192, 4096], P('ctx', 'ch')
All inputs are finite; a program needn't handle non-finite values.
Results may differ from a plain program's by a relative error of at most 0.015.
Values may be sent and summed in bfloat16 or wider, within the bound.
No kernel may reach another device: no remote copies, remote signals or barrier semaphores. Data moves between devices by JAX's collectives and lax.ppermute only.
A program may use at most 192 MiB of HBM per device.

v0:
```python
import math

import jax
import jax.numpy as jnp
from jax import lax
from jax.sharding import PartitionSpec as P

HIGHEST = lax.Precision.HIGHEST


def shifted(block, axis, distance):
    devices = range(lax.axis_size(axis))
    route = [(i - distance, i) for i in devices if i - distance in devices]
    return lax.ppermute(block, axis, route)


def phase_table(rows, cols, modulus, orient):
    row_ids = jnp.arange(rows, dtype=jnp.int32)[:, None]
    col_ids = jnp.arange(cols, dtype=jnp.int32)[None, :]
    angles = (row_ids * col_ids % modulus).astype(jnp.float32) * (2.0 * math.pi / modulus)
    return (jnp.cos(angles), orient * jnp.sin(angles))


def complex_product(pattern, first_op, second_op):
    first_real, first_imag = first_op
    second_real, second_imag = second_op

    def multiply(left_side, right_side):
        return jnp.einsum(pattern, left_side, right_side, precision=HIGHEST)

    real_out = multiply(first_real, second_real)
    imag_out = None
    if first_imag is not None and second_imag is not None:
        real_out = real_out - multiply(first_imag, second_imag)
    if second_imag is not None:
        imag_out = multiply(first_real, second_imag)
    extra_term = multiply(first_imag, second_real)
    imag_out = extra_term if imag_out is None else imag_out + extra_term
    return (real_out, imag_out)


def transform(real_part, imag_part, orient):
    channels, extent = real_part.shape
    outer = 128
    inner = extent // outer
    shaped_imag = None if imag_part is None else imag_part.reshape(channels, inner, outer)
    section = complex_product(
        "kj,cja->cka",
        phase_table(inner, inner, inner, orient),
        (real_part.reshape(channels, inner, outer), shaped_imag),
    )
    twist_real, twist_imag = phase_table(inner, outer, extent, orient)
    section_real = section[0] * twist_real - section[1] * twist_imag
    section_imag = section[0] * twist_imag + section[1] * twist_real
    final = complex_product(
        "cka,am->ckm", (section_real, section_imag), phase_table(outer, outer, outer, orient)
    )
    return (
        final[0].swapaxes(1, 2).reshape(channels, extent),
        final[1].swapaxes(1, 2).reshape(channels, extent),
    )


def filter_taps(mode_gain, mode_rate, length):
    positions = jnp.arange(length, dtype=jnp.int32).astype(jnp.float32)

    def add_mode(mode, running):
        one_gain = lax.dynamic_slice_in_dim(mode_gain, mode, 1, 1)
        one_rate = lax.dynamic_slice_in_dim(mode_rate, mode, 1, 1)
        return running + one_gain * jnp.exp(-one_rate * positions[None, :])

    initial = jnp.zeros((mode_gain.shape[0], length), jnp.float32)
    return lax.fori_loop(0, mode_gain.shape[1], add_mode, initial)


def group_conv(signal_cols, mode_gain, mode_rate):
    channels, length = signal_cols.shape
    extent = 2 * length
    padding = jnp.zeros((channels, length), jnp.float32)
    sig_real, sig_imag = transform(
        jnp.concatenate([signal_cols.astype(jnp.float32), padding], axis=1), None, -1.0
    )
    taps = filter_taps(mode_gain, mode_rate, length)
    filt_real, filt_imag = transform(jnp.concatenate([taps, padding], axis=1), None, -1.0)
    prod_real = sig_real * filt_real - sig_imag * filt_imag
    prod_imag = sig_real * filt_imag + sig_imag * filt_real
    back_real, back_imag = transform(prod_real, prod_imag, 1.0)
    return back_real[:, :length] / extent


def long_conv(signal_cols, mode_gain, mode_rate):
    channels, length = signal_cols.shape
    group = math.gcd(channels, max(1, channels // 8))
    count = channels // group

    def one_group(operands):
        return group_conv(operands[0], operands[1], operands[2])

    result = lax.map(
        one_group,
        (
            signal_cols.reshape(count, group, length),
            mode_gain.reshape(count, group, mode_gain.shape[1]),
            mode_rate.reshape(count, group, mode_rate.shape[1]),
        ),
    )
    return result.reshape(channels, length)


def per_device(proj, short_filter, residues, decays, skip, w_out):
    width = proj.shape[1]
    length_dev = proj.shape[2]
    earlier = shifted(proj[:, :, length_dev - 2 :], "ctx", 1)
    extended = jnp.concatenate([earlier, proj], axis=2).astype(jnp.float32)
    shortmix = (
        short_filter[:, :, 0:1] * extended[:, :, 2:]
        + short_filter[:, :, 1:2] * extended[:, :, 1:-1]
        + short_filter[:, :, 2:3] * extended[:, :, :-2]
    )
    query = shortmix[0].astype(jnp.bfloat16)
    signal = (shortmix[1] * shortmix[2]).astype(jnp.bfloat16)
    all_gain = residues * jnp.sqrt(-jnp.expm1(-2.0 * decays))
    channels = width // lax.axis_size("ctx")
    offset = lax.axis_index("ctx") * channels
    mode_gain = lax.dynamic_slice_in_dim(all_gain, offset, channels, 0)
    mode_rate = lax.dynamic_slice_in_dim(decays, offset, channels, 0)
    signal_cols = lax.all_to_all(signal, "ctx", split_axis=0, concat_axis=1, tiled=True)
    convolved = long_conv(signal_cols, mode_gain, mode_rate).astype(jnp.bfloat16)
    convolved = lax.all_to_all(convolved, "ctx", split_axis=1, concat_axis=0, tiled=True)
    gated = (
        query.astype(jnp.float32)
        * (convolved.astype(jnp.float32) + skip[:, None] * signal.astype(jnp.float32))
    ).astype(jnp.bfloat16)
    mixed_out = lax.dot_general(
        lax.all_gather(gated, "ch", axis=0, tiled=True),
        w_out,
        (((0,), (0,)), ((), ())),
        preferred_element_type=jnp.float32,
    )
    return mixed_out.astype(jnp.bfloat16)


def solution(mesh):
    in_specs = (
        P(None, "ch", "ctx"),
        P(None, "ch", None),
        P("ch", None),
        P("ch", None),
        P("ch"),
        P(None, "ch"),
    )
    out_specs = P("ctx", "ch")
    return jax.shard_map(
        per_device, mesh=mesh, in_specs=in_specs, out_specs=out_specs, check_vma=False
    )
```

profile of v0, /device:TPU:1, one launch (start us, length us, event | category | flops | bytes accessed | tf_op | source)
XLA Modules:
  0.0 492.2 jit_solution(11115956559206808858)
XLA Ops:
  7.7 4.5 collective-permute-start
  13.1 3.7 collective-permute-done
  16.8 1.3 maximum_convert_fusion
  19.6 7.9 %all-to-all-start = ((bf16[32,8,256]{2,1,0:T(8,128)(2,1)}), bf16[32,8,256]{2,1,0:T(8,128)(2,1)S(1)}, u32[]{:S(2)}, u32[]{:S(2)}) async-start(bf16[32,8,256]{2,1,0:T(8,128)(2,1)} %fusion.217), calls=%async_computation | async-start | bytes 262144 | tf_op jit(solution)/shard_map/all_to_all | solution.py:127
  27.8 8.2 %all-to-all-done = bf16[32,8,256]{2,1,0:T(8,128)(2,1)S(1)} async-done(((bf16[32,8,256]{2,1,0:T(8,128)(2,1)}), bf16[32,8,256]{2,1,0:T(8,128)(2,1)S(1)}, u32[]{:S(2)}, u32[]{:S(2)}) %all-to-all-start) | async-done | bytes 131104 | tf_op jit(solution)/shard_map/all_to_all | solution.py:127
  36.1 338.8 %while.37 = (s32[]{:T(128)}, bf16[8,1,8192]{2,1,0:T(2,128)(2,1)S(1)}, bf16[8,1,8192]{2,0,1:T(8,128)(2,1)S(1)}, f32[8,1,16]{2,1,0:T(1,128)S(1)}, f32[8,1,16]{2,1,...) while((s32[]{:T(128)}, bf16[8,1,8192]{2,1,0:T(2,128)(2,1)S(1)}, ...), condition=%wide.region_3.4_spmd, body=%wide.region_0.3_spmd.sunk | while | flops 460390400 | bytes 4178456 | solution.py:99
  36.1 30.7 %while.38 = (s32[]{:T(128)}, f32[1,8192]{1,0:T(1,128)S(1)}, f32[1,16]{1,0:T(1,128)S(1)}, f32[1,16]{1,0:T(1,128)S(1)}, s32[]{:T(128)}, /*index=5*/s32[]{:T(128)}) while((s32[]{:T(128)}, f32[1,8192]{1,0:T(1,128)S(1)}, f32[1,16]{1,0:T(1,128)S(1)}, f32[1,16]{1,0:T(1,128)S(1)}, s32[]{:T(128)}, /*index=5*/s32[]{:T(128)}) %tuple.82), condition=%wide.region_2.2_spmd.clone, body=%wide.region_1.1_spmd.clone.sunk | while | flops 40964 | bytes 131179 | solution.py:73
  38.6 1.2 fusion.312
  40.5 1.2 fusion.312
  46.3 1.2 fusion.312
  52.0 1.2 fusion.312
  57.8 1.2 fusion.312
  63.6 1.2 fusion.312
  78.4 30.7 %while.38 = (s32[]{:T(128)}, f32[1,8192]{1,0:T(1,128)S(1)}, f32[1,16]{1,0:T(1,128)S(1)}, f32[1,16]{1,0:T(1,128)S(1)}, s32[]{:T(128)}, /*index=5*/s32[]{:T(128)}) while((s32[]{:T(128)}, f32[1,8192]{1,0:T(1,128)S(1)}, f32[1,16]{1,0:T(1,128)S(1)}, f32[1,16]{1,0:T(1,128)S(1)}, s32[]{:T(128)}, /*index=5*/s32[]{:T(128)}) %tuple.82), condition=%wide.region_2.2_spmd.clone, body=%wide.region_1.1_spmd.clone.sunk | while | flops 40964 | bytes 131179 | solution.py:73
  81.0 1.2 fusion.312
  86.7 1.2 fusion.312
  88.6 1.2 fusion.312
  94.4 1.2 fusion.312
  100.2 1.2 fusion.312
  105.9 1.2 fusion.312
  120.8 30.7 %while.38 = (s32[]{:T(128)}, f32[1,8192]{1,0:T(1,128)S(1)}, f32[1,16]{1,0:T(1,128)S(1)}, f32[1,16]{1,0:T(1,128)S(1)}, s32[]{:T(128)}, /*index=5*/s32[]{:T(128)}) while((s32[]{:T(128)}, f32[1,8192]{1,0:T(1,128)S(1)}, f32[1,16]{1,0:T(1,128)S(1)}, f32[1,16]{1,0:T(1,128)S(1)}, s32[]{:T(128)}, /*index=5*/s32[]{:T(128)}) %tuple.82), condition=%wide.region_2.2_spmd.clone, body=%wide.region_1.1_spmd.clone.sunk | while | flops 40964 | bytes 131179 | solution.py:73
  125.2 1.2 fusion.312
  131.0 1.2 fusion.312
  136.8 1.2 fusion.312
  138.7 1.2 fusion.312
  144.4 1.2 fusion.312
  150.2 1.2 fusion.312
  163.1 30.7 %while.38 = (s32[]{:T(128)}, f32[1,8192]{1,0:T(1,128)S(1)}, f32[1,16]{1,0:T(1,128)S(1)}, f32[1,16]{1,0:T(1,128)S(1)}, s32[]{:T(128)}, /*index=5*/s32[]{:T(128)}) while((s32[]{:T(128)}, f32[1,8192]{1,0:T(1,128)S(1)}, f32[1,16]{1,0:T(1,128)S(1)}, f32[1,16]{1,0:T(1,128)S(1)}, s32[]{:T(128)}, /*index=5*/s32[]{:T(128)}) %tuple.82), condition=%wide.region_2.2_spmd.clone, body=%wide.region_1.1_spmd.clone.sunk | while | flops 40964 | bytes 131179 | solution.py:73
  163.8 1.2 fusion.312
  169.5 1.2 fusion.312
  175.3 1.2 fusion.312
  181.0 1.2 fusion.312
  186.8 1.2 fusion.312
  188.7 1.2 fusion.312
  205.5 30.7 %while.38 = (s32[]{:T(128)}, f32[1,8192]{1,0:T(1,128)S(1)}, f32[1,16]{1,0:T(1,128)S(1)}, f32[1,16]{1,0:T(1,128)S(1)}, s32[]{:T(128)}, /*index=5*/s32[]{:T(128)}) while((s32[]{:T(128)}, f32[1,8192]{1,0:T(1,128)S(1)}, f32[1,16]{1,0:T(1,128)S(1)}, f32[1,16]{1,0:T(1,128)S(1)}, s32[]{:T(128)}, /*index=5*/s32[]{:T(128)}) %tuple.82), condition=%wide.region_2.2_spmd.clone, body=%wide.region_1.1_spmd.clone.sunk | while | flops 40964 | bytes 131179 | solution.py:73
  208.0 1.2 fusion.312
  213.8 1.2 fusion.312
  219.6 1.2 fusion.312
  225.3 1.2 fusion.312
  231.1 1.2 fusion.312
  247.8 30.7 %while.38 = (s32[]{:T(128)}, f32[1,8192]{1,0:T(1,128)S(1)}, f32[1,16]{1,0:T(1,128)S(1)}, f32[1,16]{1,0:T(1,128)S(1)}, s32[]{:T(128)}, /*index=5*/s32[]{:T(128)}) while((s32[]{:T(128)}, f32[1,8192]{1,0:T(1,128)S(1)}, f32[1,16]{1,0:T(1,128)S(1)}, f32[1,16]{1,0:T(1,128)S(1)}, s32[]{:T(128)}, /*index=5*/s32[]{:T(128)}) %tuple.82), condition=%wide.region_2.2_spmd.clone, body=%wide.region_1.1_spmd.clone.sunk | while | flops 40964 | bytes 131179 | solution.py:73
  250.4 1.2 fusion.312
  252.3 1.2 fusion.312
  258.1 1.2 fusion.312
  263.8 1.2 fusion.312
  269.6 1.2 fusion.312
  275.4 1.2 fusion.312
  290.2 30.7 %while.38 = (s32[]{:T(128)}, f32[1,8192]{1,0:T(1,128)S(1)}, f32[1,16]{1,0:T(1,128)S(1)}, f32[1,16]{1,0:T(1,128)S(1)}, s32[]{:T(128)}, /*index=5*/s32[]{:T(128)}) while((s32[]{:T(128)}, f32[1,8192]{1,0:T(1,128)S(1)}, f32[1,16]{1,0:T(1,128)S(1)}, f32[1,16]{1,0:T(1,128)S(1)}, s32[]{:T(128)}, /*index=5*/s32[]{:T(128)}) %tuple.82), condition=%wide.region_2.2_spmd.clone, body=%wide.region_1.1_spmd.clone.sunk | while | flops 40964 | bytes 131179 | solution.py:73
  294.7 1.2 fusion.312
  300.4 1.2 fusion.312
  302.4 1.2 fusion.312
  308.1 1.2 fusion.312
  313.9 1.2 fusion.312
  319.6 1.2 fusion.312
  332.6 30.7 %while.38 = (s32[]{:T(128)}, f32[1,8192]{1,0:T(1,128)S(1)}, f32[1,16]{1,0:T(1,128)S(1)}, f32[1,16]{1,0:T(1,128)S(1)}, s32[]{:T(128)}, /*index=5*/s32[]{:T(128)}) while((s32[]{:T(128)}, f32[1,8192]{1,0:T(1,128)S(1)}, f32[1,16]{1,0:T(1,128)S(1)}, f32[1,16]{1,0:T(1,128)S(1)}, s32[]{:T(128)}, /*index=5*/s32[]{:T(128)}) %tuple.82), condition=%wide.region_2.2_spmd.clone, body=%wide.region_1.1_spmd.clone.sunk | while | flops 40964 | bytes 131179 | solution.py:73
  333.2 1.2 fusion.312
  338.9 1.2 fusion.312
  344.7 1.2 fusion.312
  350.5 1.2 fusion.312
  352.4 1.2 fusion.312
  358.2 1.2 fusion.312
  375.6 12.1 %all_to_all.23 = bf16[8,32,256]{2,0,1:T(8,128)(2,1)S(1)} all-to-all(bf16[8,32,256]{2,0,1:T(8,128)(2,1)S(1)} %bitcast.201), channel_id=1, replica_groups=mesh['ctx'=32,'ch'=16] {'ctx'}, dimensions={1} | all-to-all | bytes 262144 | tf_op jit(solution)/shard_map/all_to_all | solution.py:129
  388.6 93.8 %all-gather.2.cloned.1.call-done = bf16[4096,256]{1,0:T(8,128)(2,1)} async-done(((bf16[256,256]{1,0:T(8,128)(2,1)}), bf16[4096,256]{1,0:T(8,128)(2,1)}) %all-gather.2.cloned.1.call-update) | async-done | bytes 2097168 | tf_op jit(solution)/shard_map/all_gather | solution.py:135
  482.4 3.0 convolution_convert_fusion
  (559 shorter events, 283.0 us)
Async XLA Ops:
  6.5 475.9 %copy-start = (bf16[4096,256]{1,0:T(8,128)(2,1)S(1)}, bf16[4096,256]{1,0:T(8,128)(2,1)}, u32[]{:S(2)}) copy-start(bf16[4096,256]{1,0:T(8,128)(2,1)} %param.15) | copy-start | bytes 6291460
  7.7 9.1 %collective-permute-start = (bf16[3,256,2]{2,1,0:T(8,128)(2,1)S(1)}, bf16[3,256,2]{2,1,0:T(8,128)(2,1)S(1)}, u32[]{:S(2)}, u32[]{:S(2)}) collective-permute-start(bf16[3,256,2]{2,1,0:T(8,128)(2,1)S(1)} %slice.39), channel_id=1, source_target_pairs={{0,16},{16,32},{32,48},{48,64},{64,80},{80,96},{96,112},{112,128},... | collective-permute-start | bytes 9224 | tf_op jit(solution)/shard_map/ppermute | solution.py:14
  18.1 9.5 %copy-start.1 = (f32[256,16]{0,1:T(8,128)S(1)}, f32[256,16]{0,1:T(8,128)}, u32[]{:S(2)}) copy-start(f32[256,16]{0,1:T(8,128)} %param.13) | copy-start | bytes 49156
  18.1 9.5 %copy-start.2 = (f32[256,16]{0,1:T(8,128)S(1)}, f32[256,16]{0,1:T(8,128)}, u32[]{:S(2)}) copy-start(f32[256,16]{0,1:T(8,128)} %param.12) | copy-start | bytes 49156
  19.6 16.5 %all-to-all-start = ((bf16[32,8,256]{2,1,0:T(8,128)(2,1)}), bf16[32,8,256]{2,1,0:T(8,128)(2,1)S(1)}, u32[]{:S(2)}, u32[]{:S(2)}) async-start(bf16[32,8,256]{2,1,0:T(8,128)(2,1)} %fusion.217), calls=%async_computation | async-start | bytes 262144 | tf_op jit(solution)/shard_map/all_to_all | solution.py:127
  27.5 454.9 %all-gather.2.cloned.1.call-start = ((), (), s32[]{:S(2)}) async-start(), calls=%async_computation.2 | async-start | bytes 2228224 | tf_op jit(solution)/shard_map/all_gather | solution.py:135
  36.1 351.7 %copy-start.3 = (f32[256]{0:T(256)S(1)}, f32[256]{0:T(256)}, u32[]{:S(2)}) copy-start(f32[256]{0:T(256)} %param.14) | copy-start | bytes 3076
Sparse Core Ops, SparseCore 0:
  388.7 93.6 all-gather.1
where the time goes:
time: 496 us; the launch traced here: 492 us
  other arithmetic  247 us (50%)
  waiting for transfers between devices  106 us (21%)
  matrix products  92 us (19%)
  between operations  13.5 us (3%)
  starting transfers between devices  12.5 us (3%)
  blocking collectives  12.1 us (2%)
  local copies, waits for them, and re-layouts  5.29 us (1%)
    mul x128, other arithmetic, add_mode(): return running + one_gain * jnp.exp(-one_rate * positions[None, :])  155 us
    all_gather x1, waiting for transfers between devices, per_device(): lax.all_gather(gated, 'ch', axis=0, tiled=True)  93.8 us
    dot_general x144, matrix products, multiply(): return jnp.einsum(pattern, left_side, right_side, precision=HIGHEST)  89 us
    dynamic_slice x128, other arithmetic, add_mode(): one_gain = lax.dynamic_slice_in_dim(mode_gain, mode, 1, 1)  78.7 us
    all_to_all x1, blocking collectives, per_device(): lax.all_to_all(convolved, 'ctx', split_axis=1, concat_axis=0, tiled=True)  12.1 us
  transfers between devices with their start and end apart: 3, of which 3 were waited for; matrix products, arithmetic and copies ran while one was open for 0% of the time, Pallas kernels for 0%

commit v1 on v0

v1 whole, which is shorter than its diff:
```python
import functools

import jax
import jax.numpy as jnp
from jax import lax
from jax.experimental import pallas as pl
from jax.experimental.pallas import tpu as pltpu
from jax.sharding import PartitionSpec as P

F32 = jnp.float32
BF16 = jnp.bfloat16
LANES = 128
SUB = 8
VMEM_LIMIT = 48 * 1024 * 1024


def pallas(body, out_shape, scratch=(), **kwargs):
    return pl.pallas_call(
        body,
        out_shape=out_shape,
        scratch_shapes=list(scratch),
        compiler_params=pltpu.CompilerParams(vmem_limit_bytes=VMEM_LIMIT),
        **kwargs,
    )


def edge_kernel(proj_ref, edge_ref):
    rows = [proj_ref[i].astype(F32).T[-2:, :] for i in range(3)]
    rows.append(jnp.zeros((2, proj_ref.shape[1]), F32))
    edge_ref[...] = jnp.concatenate(rows, axis=0).astype(BF16)


def halves(width):
    return [slice(lo, lo + LANES) for lo in range(0, width, LANES)]


def state_kernel(
    proj_ref, halo_ref, filter_ref, decay_ref,
    signal_ref, query_ref, ends_ref, state_ref,
    line_ref, coef_ref, sums_ref,
):
    width, length = proj_ref.shape[1:]
    steps = length // SUB
    modes = decay_ref.shape[1]
    decay = decay_ref[...].T
    coef_ref[...] = decay
    halo = halo_ref[...].astype(F32)
    for i in range(3):
        block = proj_ref[i].astype(F32).T
        for h, cols in enumerate(halves(width)):
            line_ref[i, h, SUB - 2 : SUB, :] = halo[2 * i : 2 * i + 2, cols]
            line_ref[i, h, SUB:, :] = block[:, cols]
    taps = [filter_ref[i].T for i in range(3)]
    chunk_id = lax.broadcasted_iota(jnp.int32, (SUB, LANES), 0).astype(F32)
    for h, cols in enumerate(halves(width)):
        tap = [[jnp.broadcast_to(taps[i][m : m + 1, cols], (SUB, LANES)) for m in range(3)] for i in range(3)]
        rate = [jnp.broadcast_to(coef_ref[m : m + 1, cols], (SUB, LANES)) for m in range(modes)]
        keep = [jnp.exp(-r) for r in rate]
        state = [jnp.zeros((SUB, LANES), F32) for _ in range(modes)]

        def rows(i, at):
            return line_ref[i, h, pl.ds(SUB + at, SUB, stride=steps), :]

        back2 = [rows(i, -2) for i in range(3)]
        back1 = [rows(i, -1) for i in range(3)]
        for p in range(steps):
            here = [rows(i, p) for i in range(3)]
            mix = [tap[i][0] * here[i] + tap[i][1] * back1[i] + tap[i][2] * back2[i] for i in range(3)]
            back2, back1 = back1, here
            signal = (mix[1] * mix[2]).astype(BF16).astype(F32)
            signal_ref[p, :, cols] = signal
            query_ref[p, :, cols] = mix[0].astype(BF16).astype(F32)
            state = [keep[m] * state[m] + signal for m in range(modes)]
        for m in range(modes):
            ends_ref[m, :, cols] = state[m]
            weight = jnp.exp(-rate[m] * (float(steps) * (SUB - 1 - chunk_id)))
            sums_ref[m : m + 1, cols] = jnp.sum(weight * state[m], axis=0, keepdims=True)
    sent = sums_ref[...].astype(BF16)
    for j in range(state_ref.shape[0]):
        state_ref[j] = sent


def gate_kernel(
    place_ref, given_ref, signal_ref, query_ref, ends_ref, decay_ref, residue_ref, skip_ref,
    gated_ref,
    carry_ref, gain_ref, coef_ref, line_ref,
):
    blocks, modes, width = given_ref.shape
    steps = signal_ref.shape[0]
    length = steps * SUB
    place = place_ref[0]
    decay = decay_ref[...].T
    coef_ref[...] = decay
    twice = 2.0 * decay
    series = jnp.ones_like(twice)
    for n in (8, 7, 6, 5, 4, 3, 2):
        series = 1.0 - twice * (1.0 / n) * series
    gain_ref[...] = residue_ref[...].T * jnp.sqrt(twice * series)
    per_block = jnp.exp(-float(length) * decay)
    carry = jnp.zeros_like(decay)
    for j in range(blocks - 1):
        carry = jnp.where(j < place, per_block * carry + given_ref[j].astype(F32), carry)
    carry_ref[...] = carry
    chunk_id = lax.broadcasted_iota(jnp.int32, (SUB, LANES), 0)
    for h, cols in enumerate(halves(width)):
        rate = [jnp.broadcast_to(coef_ref[m : m + 1, cols], (SUB, LANES)) for m in range(modes)]
        state = []
        for m in range(modes):
            enters = jnp.broadcast_to(carry_ref[m : m + 1, cols], (SUB, LANES))
            run = jnp.where(chunk_id == 0, enters, pltpu.roll(ends_ref[m, :, cols], 1, 0))
            for far in (1, 2, 4):
                moved = jnp.where(chunk_id >= far, pltpu.roll(run, far, 0), 0.0)
                run = run + jnp.exp(-float(steps * far) * rate[m]) * moved
            state.append(run)
        keep = [jnp.exp(-r) for r in rate]
        gain = [jnp.broadcast_to(gain_ref[m : m + 1, cols], (SUB, LANES)) for m in range(modes)]
        skip = jnp.broadcast_to(skip_ref[0:1, cols], (SUB, LANES))
        for p in range(steps):
            signal = signal_ref[p, :, cols]
            state = [keep[m] * state[m] + signal for m in range(modes)]
            terms = [gain[m] * state[m] for m in range(modes)]
            while len(terms) > 1:
                terms = [a + b for a, b in zip(terms[::2], terms[1::2])]
            conv = terms[0].astype(BF16).astype(F32)
            line_ref[h, pl.ds(p, SUB, stride=steps), :] = query_ref[p, :, cols] * (conv + skip * signal)
        gated_ref[:, cols] = line_ref[h].astype(BF16)


def mix_kernel(gated_ref, w_ref, out_ref, total_ref):
    step = pl.program_id(0)
    part = sum(
        jnp.dot(gated_ref[0, k], w_ref[k, 0], preferred_element_type=F32)
        for k in range(gated_ref.shape[1])
    )

    @pl.when(step == 0)
    def _():
        total_ref[...] = part

    @pl.when(step > 0)
    def _():
        total_ref[...] += part

    @pl.when(step == pl.num_programs(0) - 1)
    def _():
        out_ref[...] = total_ref[...].astype(BF16)


def per_device(outer, proj, short_filter, residues, decays, skip, w_out):
    _, width, length = proj.shape
    modes = decays.shape[1]
    blocks = lax.axis_size("ctx")
    groups = lax.axis_size("ch")
    inner = groups // outer
    steps = length // SUB
    shape = jax.ShapeDtypeStruct

    edge = pl.pallas_call(
        edge_kernel,
        grid=(1,),
        in_specs=[pl.BlockSpec((3, width, LANES), lambda i: (0, 0, length // LANES - 1))],
        out_specs=pl.BlockSpec((SUB, width), lambda i: (0, 0)),
        out_shape=shape((SUB, width), BF16),
    )(proj)
    halo = lax.ppermute(edge, "ctx", [(i, i + 1) for i in range(blocks - 1)])
    signal, query, ends, state = pallas(
        state_kernel,
        (
            shape((steps, SUB, width), F32),
            shape((steps, SUB, width), F32),
            shape((modes, SUB, width), F32),
            shape((blocks, modes, width), BF16),
        ),
        (
            pltpu.VMEM((3, width // LANES, SUB + length, LANES), F32),
            pltpu.VMEM((modes, width), F32),
            pltpu.VMEM((modes, width), F32),
        ),
    )(proj, halo, short_filter, decays)
    given = lax.all_to_all(state, "ctx", 0, 0)
    place = lax.axis_index("ctx").astype(jnp.int32).reshape(1)
    whole = pl.BlockSpec(memory_space=pltpu.VMEM)
    gated = pallas(
        gate_kernel,
        shape((length, width), BF16),
        (
            pltpu.VMEM((modes, width), F32),
            pltpu.VMEM((modes, width), F32),
            pltpu.VMEM((modes, width), F32),
            pltpu.VMEM((width // LANES, length, LANES), F32),
        ),
        in_specs=[pl.BlockSpec(memory_space=pltpu.SMEM)] + [whole] * 7,
    )(place, given, signal, query, ends, decays, residues, skip.reshape(1, width))
    along_outer = [[a * inner + b for a in range(outer)] for b in range(inner)]
    along_inner = [[a * inner + b for b in range(inner)] for a in range(outer)]
    near = lax.all_gather(gated, "ch", axis_index_groups=along_outer)
    full = lax.all_gather(near, "ch", axis_index_groups=along_inner)
    return pl.pallas_call(
        mix_kernel,
        grid=(inner,),
        in_specs=[
            pl.BlockSpec((1, outer, length, width), lambda i: (i, 0, 0, 0)),
            pl.BlockSpec((outer, 1, width, w_out.shape[1]), lambda i: (0, i, 0, 0)),
        ],
        out_specs=pl.BlockSpec((length, w_out.shape[1]), lambda i: (0, 0)),
        out_shape=shape((length, w_out.shape[1]), BF16),
        scratch_shapes=[pltpu.VMEM((length, w_out.shape[1]), F32)],
        compiler_params=pltpu.CompilerParams(vmem_limit_bytes=VMEM_LIMIT),
    )(full, w_out.reshape(outer, inner, width, w_out.shape[1]))


def solution(mesh):
    groups = mesh.shape["ch"]
    outer = 4 if groups % 4 == 0 else 1
    in_specs = (
        P(None, "ch", "ctx"),
        P(None, "ch", None),
        P("ch", None),
        P("ch", None),
        P("ch"),
        P(None, "ch"),
    )
    return jax.shard_map(
        functools.partial(per_device, outer),
        mesh=mesh,
        in_specs=in_specs,
        out_specs=P("ctx", "ch"),
        check_vma=False,
    )
```

time: 496 us -> 115 us (0.23)
  other arithmetic: 247 us -> 0 us
  matrix products: 92 us -> 0 us
  waiting for transfers between devices: 106 us -> 46.5 us
  blocking collectives: 12.1 us -> 33.3 us
  Pallas kernels: 0 us -> 6.82 us
    mul x128 -> x0, other arithmetic: 155 us -> none  [add_mode(): return running + one_gain * jnp.exp(-one_rate * positions[None, :])]
    dot_general x145 -> x0, matrix products: 92 us -> none  [the longest x144 89 us: multiply(): return jnp.einsum(pattern, left_side, right_side, precision=HIGHEST)]
    dynamic_slice x129 -> x0, other arithmetic: 78.8 us -> none  [the longest x128 78.7 us: add_mode(): one_gain = lax.dynamic_slice_in_dim(mode_gain, mode, 1, 1)]
    all_gather x1, waiting for transfers between devices: 93.8 us -> 32.7 us  [per_device(): full = lax.all_gather(near, 'ch', axis_index_groups=along_inner)]
    all_gather x0 -> x1, blocking collectives: none -> 33.3 us  [per_device(): near = lax.all_gather(gated, 'ch', axis_index_groups=along_outer)]
    all_to_all x1 -> x0, blocking collectives: 12.1 us -> none  [per_device(): lax.all_to_all(convolved, 'ctx', split_axis=1, concat_axis=0, tiled=True)]
    add x129 -> x0, other arithmetic: 10.2 us -> none  [the longest x128 9.36 us: add_mode(): return running + one_gain * jnp.exp(-one_rate * positions[None, :])]
    pallas_call x0 -> x4, Pallas kernels: none -> 6.82 us  [the longest x1 2.16 us: per_device(): pl.pallas_call(mix_kernel, grid=(inner,), in_specs=[pl.BlockSpec((1, oute...]
  transfers between devices with their start and end apart: 3 -> 3, of which waited for: 3 -> 3; matrix products, arithmetic and copies ran while one was open for 0% -> 2% of each run, Pallas kernels for 0% -> 0%
where the time goes in v1:
time: 115 us
  waiting for transfers between devices  46.5 us (40%)
  blocking collectives  33.3 us (29%)
  between operations  13.5 us (12%)
  starting transfers between devices  10.7 us (9%)
  Pallas kernels  6.82 us (6%)
  local copies, waits for them, and re-layouts  4.4 us (4%)
    all_gather x1, blocking collectives, per_device(): near = lax.all_gather(gated, 'ch', axis_index_groups=along_outer)  33.3 us
    all_gather x1, waiting for transfers between devices, per_device(): full = lax.all_gather(near, 'ch', axis_index_groups=along_inner)  32.7 us
    all_to_all x1, waiting for transfers between devices, per_device(): given = lax.all_to_all(state, 'ctx', 0, 0)  10.9 us
    all_to_all x1, starting transfers between devices, per_device(): given = lax.all_to_all(state, 'ctx', 0, 0)  6.13 us
    ppermute x1, starting transfers between devices, per_device(): halo = lax.ppermute(edge, 'ctx', [(i, i + 1) for i in range(blocks - 1)])  4.5 us
    unnamed x13, local copies, waits for them, and re-layouts  4.4 us
    ppermute x1, waiting for transfers between devices, per_device(): halo = lax.ppermute(edge, 'ctx', [(i, i + 1) for i in range(blocks - 1)])  2.79 us
  transfers between devices with their start and end apart: 3, of which 3 were waited for; matrix products, arithmetic and copies ran while one was open for 2% of the time, Pallas kernels for 0%

profile of v1, /device:TPU:1, one launch (start us, length us, event | category | flops | bytes accessed | tf_op | source)
XLA Modules:
  0.0 115.1 jit_solution(16605427265760112199)
XLA Ops:
  6.5 0.0 copy-start.4
  6.5 0.0 copy-start.3
  6.5 1.7 %shard_map.64 = bf16[8,256]{1,0:T(8,128)(2,1)} custom-call(bf16[3,256,256]{2,1,0:T(8,128)(2,1)} %proj_ref.3), custom_call_target="tpu_custom_call" | custom-call | tf_op jit(solution)/shard_map/pallas_call | solution.py:158
  8.2 4.5 %collective-permute-start = (bf16[8,256]{1,0:T(8,128)(2,1)}, bf16[8,256]{1,0:T(8,128)(2,1)S(1)}, u32[]{:S(2)}, u32[]{:S(2)}) collective-permute-start(bf16[8,256]{1,0:T(8,128)(2,1)} %shard_map.64), channel_id=1, source_target_pairs={{0,16},{16,32},{32,48},{48,64},{64,80},{80,96},{96,112},{112,128},... | collective-permute-start | bytes 12296 | tf_op jit(solution)/shard_map/ppermute | solution.py:165
  12.7 0.8 copy.12.decay_ref
  13.5 0.9 copy.11.filter_ref
  14.4 0.0 copy-start
  14.5 2.8 %collective-permute-done.halo_ref = bf16[8,256]{1,0:T(8,128)(2,1)S(1)} collective-permute-done((bf16[8,256]{1,0:T(8,128)(2,1)}, bf16[8,256]{1,0:T(8,128)(2,1)S(1)}, u32[]{:S(2)}, u32[]{:S(2)}) %collective-permute-start) | collective-permute-done | bytes 4128 | tf_op jit(solution)/shard_map/ppermute | solution.py:165
  17.2 0.0 copy-start.2
  17.2 1.0 copy-done.2
  18.2 2.0 %shard_map.65 = (f32[32,8,256]{2,1,0:T(8,128)S(1)}, f32[32,8,256]{2,1,0:T(8,128)S(1)}, f32[16,8,256]{2,1,0:T(8,128)S(1)}, bf16[32,16,256]{2,1,0:T(8,128)(2,1)}) custom-call(bf16[3,256,256]{2,1,0:T(8,128)(2,1)S(1)} %copy-done.2, bf16[8,256]{1,0:T(8,128)(2,1)S(1)} %collective-permute-done.halo_ref, f32[3,256,3]{2,1,0:T(8,128)S(1)} %copy.11.filter_ref, ...), custom_call_target="tpu_custom_call" | custom-call | tf_op jit(solution)/shard_map/pallas_call | solution.py:166
  20.3 6.1 %all-to-all-start = ((bf16[32,16,256]{2,1,0:T(8,128)(2,1)}), bf16[32,16,256]{2,1,0:T(8,128)(2,1)S(1)}, u32[]{:S(2)}, u32[]{:S(2)}) async-start(bf16[32,16,256]{2,1,0:T(8,128)(2,1)} %get-tuple-element.9), calls=%async_computation | async-start | bytes 524288 | tf_op jit(solution)/shard_map/all_to_all | solution.py:180
  26.4 0.0 all-gather.4.cloned.1.call-start
  26.5 0.0 copy-done.4
  26.5 0.1 copy.14.residue_ref
  26.6 10.9 %all-to-all-done.given_ref = bf16[32,16,256]{2,1,0:T(8,128)(2,1)S(1)} async-done(((bf16[32,16,256]{2,1,0:T(8,128)(2,1)}), bf16[32,16,256]{2,1,0:T(8,128)(2,1)S(1)}, u32[]{:S(2)}, u32[]{:S(2)}) %all-to-all-start) | async-done | bytes 262176 | tf_op jit(solution)/shard_map/all_to_all | solution.py:180
  37.5 0.0 copy-done.3
  37.5 0.9 shard_map.66
  38.5 33.3 %all-gather = bf16[1024,256]{1,0:T(8,128)(2,1)} all-gather(bf16[256,256]{1,0:T(8,128)(2,1)S(1)} %shard_map.66), channel_id=2, replica_groups={{0,4,8,12},{1,5,9,13},{2,6,10,14},{3,7,11,15},{16,20,24,28},{17,21,25,2..., dimensions={0}, use_global_device_ids=true | all-gather | bytes 655360 | tf_op jit(solution)/shard_map/all_gather | solution.py:196
  71.7 0.0 all-gather.4.cloned.1.call-update
  71.8 32.7 %all-gather.4.cloned.1.call-done = bf16[16,256,256]{2,1,0:T(8,128)(2,1)} async-done(((bf16[4,256,256]{2,1,0:T(8,128)(2,1)}), bf16[16,256,256]{2,1,0:T(8,128)(2,1)}) %all-gather.4.cloned.1.call-update) | async-done | bytes 2097168 | tf_op jit(solution)/shard_map/all_gather | solution.py:197
  104.5 0.0 copy-done
  104.5 0.0 copy-start.1
  104.5 1.6 %copy-done.1 = bf16[16,256,256]{2,1,0:T(8,128)(2,1)S(1)} copy-done((bf16[16,256,256]{2,1,0:T(8,128)(2,1)S(1)}, bf16[16,256,256]{2,1,0:T(8,128)(2,1)}, u32[]{:S(2)}) %copy-start.1) | copy-done | bytes 2097176
  106.1 2.2 %shard_map.67 = bf16[256,256]{1,0:T(8,128)(2,1)} custom-call(bf16[4,4,256,256]{3,2,1,0:T(8,128)(2,1)S(1)} %bitcast.6, bf16[4,4,256,256]{3,2,1,0:T(8,128)(2,1)S(1)} %bitcast.5), custom_call_target="tpu_custom_call" | custom-call | tf_op jit(solution)/shard_map/pallas_call | solution.py:198
Async XLA Ops:
  6.5 19.9 %copy-start.4 = (f32[256,16]{0,1:T(8,128)S(1)}, f32[256,16]{0,1:T(8,128)}, u32[]{:S(2)}) copy-start(f32[256,16]{0,1:T(8,128)} %param.8) | copy-start | bytes 49156
  6.5 31.0 %copy-start.3 = (f32[256]{0:T(256)S(1)}, f32[256]{0:T(256)}, u32[]{:S(2)}) copy-start(f32[256]{0:T(256)} %param.10) | copy-start | bytes 3076
  8.2 9.0 %collective-permute-start = (bf16[8,256]{1,0:T(8,128)(2,1)}, bf16[8,256]{1,0:T(8,128)(2,1)S(1)}, u32[]{:S(2)}, u32[]{:S(2)}) collective-permute-start(bf16[8,256]{1,0:T(8,128)(2,1)} %shard_map.64), channel_id=1, source_target_pairs={{0,16},{16,32},{32,48},{48,64},{64,80},{80,96},{96,112},{112,128},... | collective-permute-start | bytes 12296 | tf_op jit(solution)/shard_map/ppermute | solution.py:165
  14.4 90.1 %copy-start = (bf16[4096,256]{1,0:T(8,128)(2,1)S(1)}, bf16[4096,256]{1,0:T(8,128)(2,1)}, u32[]{:S(2)}) copy-start(bf16[4096,256]{1,0:T(8,128)(2,1)} %param.11) | copy-start | bytes 6291460
  17.2 1.0 copy-start.2
  20.3 17.2 %all-to-all-start = ((bf16[32,16,256]{2,1,0:T(8,128)(2,1)}), bf16[32,16,256]{2,1,0:T(8,128)(2,1)S(1)}, u32[]{:S(2)}, u32[]{:S(2)}) async-start(bf16[32,16,256]{2,1,0:T(8,128)(2,1)} %get-tuple-element.9), calls=%async_computation | async-start | bytes 524288 | tf_op jit(solution)/shard_map/all_to_all | solution.py:180
  26.4 78.1 %all-gather.4.cloned.1.call-start = ((), (), s32[]{:S(2)}) async-start(), calls=%async_computation.1 | async-start | bytes 2621440 | tf_op jit(solution)/shard_map/all_gather | solution.py:197
  104.5 1.6 %copy-start.1 = (bf16[16,256,256]{2,1,0:T(8,128)(2,1)S(1)}, bf16[16,256,256]{2,1,0:T(8,128)(2,1)}, u32[]{:S(2)}) copy-start(bf16[16,256,256]{2,1,0:T(8,128)(2,1)} %all-gather.4.cloned.1.call-done) | copy-start | bytes 6291460
Sparse Core Ops, SparseCore 0:
  71.9 32.5 all-gather.3

commit v2 on v1

--- a/solution.py
+++ b/solution.py
@@ -37,24 +37,21 @@
 def state_kernel(
     proj_ref, halo_ref, filter_ref, decay_ref,
     signal_ref, query_ref, ends_ref, state_ref,
-    line_ref, coef_ref, sums_ref,
+    line_ref, sums_ref,
 ):
     width, length = proj_ref.shape[1:]
     steps = length // SUB
-    modes = decay_ref.shape[1]
-    decay = decay_ref[...].T
-    coef_ref[...] = decay
+    modes = decay_ref.shape[0]
     halo = halo_ref[...].astype(F32)
     for i in range(3):
         block = proj_ref[i].astype(F32).T
         for h, cols in enumerate(halves(width)):
             line_ref[i, h, SUB - 2 : SUB, :] = halo[2 * i : 2 * i + 2, cols]
             line_ref[i, h, SUB:, :] = block[:, cols]
-    taps = [filter_ref[i].T for i in range(3)]
     chunk_id = lax.broadcasted_iota(jnp.int32, (SUB, LANES), 0).astype(F32)
     for h, cols in enumerate(halves(width)):
-        tap = [[jnp.broadcast_to(taps[i][m : m + 1, cols], (SUB, LANES)) for m in range(3)] for i in range(3)]
-        rate = [jnp.broadcast_to(coef_ref[m : m + 1, cols], (SUB, LANES)) for m in range(modes)]
+        tap = [[jnp.broadcast_to(filter_ref[i, m : m + 1, cols], (SUB, LANES)) for m in range(3)] for i in range(3)]
+        rate = [jnp.broadcast_to(decay_ref[m : m + 1, cols], (SUB, LANES)) for m in range(modes)]
         keep = [jnp.exp(-r) for r in rate]
         state = [jnp.zeros((SUB, LANES), F32) for _ in range(modes)]
 
@@ -83,19 +80,18 @@
 def gate_kernel(
     place_ref, given_ref, signal_ref, query_ref, ends_ref, decay_ref, residue_ref, skip_ref,
     gated_ref,
-    carry_ref, gain_ref, coef_ref, line_ref,
+    carry_ref, gain_ref, line_ref,
 ):
     blocks, modes, width = given_ref.shape
     steps = signal_ref.shape[0]
     length = steps * SUB
     place = place_ref[0]
-    decay = decay_ref[...].T
-    coef_ref[...] = decay
+    decay = decay_ref[...]
     twice = 2.0 * decay
     series = jnp.ones_like(twice)
     for n in (8, 7, 6, 5, 4, 3, 2):
         series = 1.0 - twice * (1.0 / n) * series
-    gain_ref[...] = residue_ref[...].T * jnp.sqrt(twice * series)
+    gain_ref[...] = residue_ref[...] * jnp.sqrt(twice * series)
     per_block = jnp.exp(-float(length) * decay)
     carry = jnp.zeros_like(decay)
     for j in range(blocks - 1):
@@ -103,7 +99,7 @@
     carry_ref[...] = carry
     chunk_id = lax.broadcasted_iota(jnp.int32, (SUB, LANES), 0)
     for h, cols in enumerate(halves(width)):
-        rate = [jnp.broadcast_to(coef_ref[m : m + 1, cols], (SUB, LANES)) for m in range(modes)]
+        rate = [jnp.broadcast_to(decay_ref[m : m + 1, cols], (SUB, LANES)) for m in range(modes)]
         state = []
         for m in range(modes):
             enters = jnp.broadcast_to(carry_ref[m : m + 1, cols], (SUB, LANES))
@@ -126,35 +122,39 @@
         gated_ref[:, cols] = line_ref[h].astype(BF16)
 
 
-def mix_kernel(gated_ref, w_ref, out_ref, total_ref):
-    step = pl.program_id(0)
-    part = sum(
-        jnp.dot(gated_ref[0, k], w_ref[k, 0], preferred_element_type=F32)
-        for k in range(gated_ref.shape[1])
-    )
-
-    @pl.when(step == 0)
-    def _():
-        total_ref[...] = part
-
-    @pl.when(step > 0)
-    def _():
-        total_ref[...] += part
-
-    @pl.when(step == pl.num_programs(0) - 1)
-    def _():
-        out_ref[...] = total_ref[...].astype(BF16)
+def mix_kernel(gated_ref, w_ref, part_ref):
+    for y in range(part_ref.shape[0]):
+        part_ref[y] = sum(
+            jnp.dot(gated_ref[k], w_ref[y, k], preferred_element_type=F32)
+            for k in range(gated_ref.shape[0])
+        ).astype(BF16)
+
+
+def sum_kernel(part_ref, out_ref):
+    total = part_ref[0].astype(F32)
+    for k in range(1, part_ref.shape[0]):
+        total = total + part_ref[k].astype(F32)
+    out_ref[...] = total.astype(BF16)
 
 
 def per_device(outer, proj, short_filter, residues, decays, skip, w_out):
     _, width, length = proj.shape
     modes = decays.shape[1]
+    features = w_out.shape[1]
     blocks = lax.axis_size("ctx")
     groups = lax.axis_size("ch")
     inner = groups // outer
     steps = length // SUB
     shape = jax.ShapeDtypeStruct
 
+    along_outer = [[a * inner + b for a in range(outer)] for b in range(inner)]
+    along_inner = [[a * inner + b for b in range(inner)] for a in range(outer)]
+    decays, residues = decays.T, residues.T
+    short_filter = short_filter.swapaxes(1, 2)
+    w_near = lax.all_to_all(
+        w_out.reshape(outer, inner, width, features).swapaxes(0, 1),
+        "ch", 0, 0, axis_index_groups=along_inner,
+    )
     edge = pl.pallas_call(
         edge_kernel,
         grid=(1,),
@@ -174,7 +174,6 @@
         (
             pltpu.VMEM((3, width // LANES, SUB + length, LANES), F32),
             pltpu.VMEM((modes, width), F32),
-            pltpu.VMEM((modes, width), F32),
         ),
     )(proj, halo, short_filter, decays)
     given = lax.all_to_all(state, "ctx", 0, 0)
@@ -186,27 +185,14 @@
         (
             pltpu.VMEM((modes, width), F32),
             pltpu.VMEM((modes, width), F32),
-            pltpu.VMEM((modes, width), F32),
             pltpu.VMEM((width // LANES, length, LANES), F32),
         ),
         in_specs=[pl.BlockSpec(memory_space=pltpu.SMEM)] + [whole] * 7,
     )(place, given, signal, query, ends, decays, residues, skip.reshape(1, width))
-    along_outer = [[a * inner + b for a in range(outer)] for b in range(inner)]
-    along_inner = [[a * inner + b for b in range(inner)] for a in range(outer)]
     near = lax.all_gather(gated, "ch", axis_index_groups=along_outer)
-    full = lax.all_gather(near, "ch", axis_index_groups=along_inner)
-    return pl.pallas_call(
-        mix_kernel,
-        grid=(inner,),
-        in_specs=[
-            pl.BlockSpec((1, outer, length, width), lambda i: (i, 0, 0, 0)),
-            pl.BlockSpec((outer, 1, width, w_out.shape[1]), lambda i: (0, i, 0, 0)),
-        ],
-        out_specs=pl.BlockSpec((length, w_out.shape[1]), lambda i: (0, 0)),
-        out_shape=shape((length, w_out.shape[1]), BF16),
-        scratch_shapes=[pltpu.VMEM((length, w_out.shape[1]), F32)],
-        compiler_params=pltpu.CompilerParams(vmem_limit_bytes=VMEM_LIMIT),
-    )(full, w_out.reshape(outer, inner, width, w_out.shape[1]))
+    parts = pallas(mix_kernel, shape((inner, length, features), BF16), in_specs=[whole, whole])(near, w_near)
+    parts = lax.all_to_all(parts, "ch", 0, 0, axis_index_groups=along_inner)
+    return pallas(sum_kernel, shape((length, features), BF16), in_specs=[whole])(parts)
 
 
 def solution(mesh):

time: 115 us -> 85.3 us (0.74)
  waiting for transfers between devices: 46.5 us -> 12.5 us
  between operations: 13.5 us -> 0.04 us
  blocking collectives: 33.3 us -> 45.8 us
  starting transfers between devices: 10.7 us -> 14.9 us
    all_gather x1 -> x0, waiting for transfers between devices: 32.7 us -> none  [per_device(): full = lax.all_gather(near, 'ch', axis_index_groups=along_inner)]
    all_to_all x0 -> x1, blocking collectives: none -> 12.7 us  [per_device(): parts = lax.all_to_all(parts, 'ch', 0, 0, axis_index_groups=along_inner)]
    all_to_all x0 -> x1, starting transfers between devices: none -> 4.32 us  [per_device(): lax.all_to_all(w_out.reshape(outer, inner, width, features).swapaxes(0, 1...]
    reshape x0 -> x1, local copies, waits for them, and re-layouts: none -> 3.11 us  [per_device(): w_out.reshape(outer, inner, width, features).swapaxes(0, 1)]
    all_to_all x1, waiting for transfers between devices: 10.9 us -> 8 us  [per_device(): given = lax.all_to_all(state, 'ctx', 0, 0)]
    unnamed x13 -> x12, local copies, waits for them, and re-layouts: 4.4 us -> 2.43 us
    ppermute x1, waiting for transfers between devices: 2.79 us -> 4.51 us  [per_device(): halo = lax.ppermute(edge, 'ctx', [(i, i + 1) for i in range(blocks - 1)])]
  transfers between devices with their start and end apart: 3 -> 3, of which waited for: 3 -> 2; matrix products, arithmetic and copies ran while one was open for 2% -> 4% of each run, Pallas kernels for 0% -> 1%
where the time goes in v2:
time: 85.3 us; the launch traced here: 84.7 us
  blocking collectives  45.8 us (54%)
  starting transfers between devices  14.9 us (17%)
  waiting for transfers between devices  12.5 us (15%)
  Pallas kernels  5.85 us (7%)
  local copies, waits for them, and re-layouts  5.54 us (6%)
    all_gather x1, blocking collectives, per_device(): near = lax.all_gather(gated, 'ch', axis_index_groups=along_outer)  33.2 us
    all_to_all x1, blocking collectives, per_device(): parts = lax.all_to_all(parts, 'ch', 0, 0, axis_index_groups=along_inner)  12.7 us
    all_to_all x1, waiting for transfers between devices, per_device(): given = lax.all_to_all(state, 'ctx', 0, 0)  8 us
    all_to_all x1, starting transfers between devices, per_device(): given = lax.all_to_all(state, 'ctx', 0, 0)  6.13 us
    ppermute x1, waiting for transfers between devices, per_device(): halo = lax.ppermute(edge, 'ctx', [(i, i + 1) for i in range(blocks - 1)])  4.51 us
    ppermute x1, starting transfers between devices, per_device(): halo = lax.ppermute(edge, 'ctx', [(i, i + 1) for i in range(blocks - 1)])  4.5 us
    all_to_all x1, starting transfers between devices, per_device(): lax.all_to_all(w_out.reshape(outer, inner, width, features).swapaxes(0, 1...  4.32 us
    reshape x1, local copies, waits for them, and re-layouts, per_device(): w_out.reshape(outer, inner, width, features).swapaxes(0, 1)  3.11 us
  transfers between devices with their start and end apart: 3, of which 2 were waited for; matrix products, arithmetic and copies ran while one was open for 4% of the time, Pallas kernels for 1%

profile of v2, /device:TPU:1, one launch (start us, length us, event | category | flops | bytes accessed | tf_op | source)
XLA Modules:
  0.0 84.7 jit_solution(6154748915935195189)
XLA Ops:
  0.0 1.7 %shard_map.64 = bf16[8,256]{1,0:T(8,128)(2,1)} custom-call(bf16[3,256,256]{2,1,0:T(8,128)(2,1)} %proj_ref.3), custom_call_target="tpu_custom_call" | custom-call | tf_op jit(solution)/shard_map/pallas_call | solution.py:158
  1.7 4.5 %collective-permute-start = (bf16[8,256]{1,0:T(8,128)(2,1)}, bf16[8,256]{1,0:T(8,128)(2,1)S(1)}, u32[]{:S(2)}, u32[]{:S(2)}) collective-permute-start(bf16[8,256]{1,0:T(8,128)(2,1)} %shard_map.64), channel_id=1, source_target_pairs={{0,16},{16,32},{32,48},{48,64},{64,80},{80,96},{96,112},{112,128},... | collective-permute-start | bytes 12296 | tf_op jit(solution)/shard_map/ppermute | solution.py:165
  6.2 4.5 %collective-permute-done.halo_ref = bf16[8,256]{1,0:T(8,128)(2,1)S(1)} collective-permute-done((bf16[8,256]{1,0:T(8,128)(2,1)}, bf16[8,256]{1,0:T(8,128)(2,1)S(1)}, u32[]{:S(2)}, u32[]{:S(2)}) %collective-permute-start) | collective-permute-done | bytes 4128 | tf_op jit(solution)/shard_map/ppermute | solution.py:165
  10.7 0.0 copy-start
  10.7 1.0 %copy-done = bf16[3,256,256]{2,1,0:T(8,128)(2,1)S(1)} copy-done((bf16[3,256,256]{2,1,0:T(8,128)(2,1)S(1)}, bf16[3,256,256]{2,1,0:T(8,128)(2,1)}, u32[]{:S(2)}) %copy-start) | copy-done | bytes 393240
  11.7 0.0 copy-start.1
  11.7 0.7 copy-done.1
  12.4 0.0 copy-start.4
  12.4 0.7 copy-done.4
  13.1 1.9 %shard_map.65 = (f32[32,8,256]{2,1,0:T(8,128)S(1)}, f32[32,8,256]{2,1,0:T(8,128)S(1)}, f32[16,8,256]{2,1,0:T(8,128)S(1)}, bf16[32,16,256]{2,1,0:T(8,128)(2,1)}) custom-call(bf16[3,256,256]{2,1,0:T(8,128)(2,1)S(1)} %copy-done, bf16[8,256]{1,0:T(8,128)(2,1)S(1)} %collective-permute-done.halo_ref, f32[3,3,256]{2,1,0:T(4,128)S(1)} %bitcast.14, ...), custom_call_target="tpu_custom_call" | custom-call | tf_op jit(solution)/shard_map/pallas_call | solution.py:166
  15.0 6.1 %all-to-all-start = ((bf16[32,16,256]{2,1,0:T(8,128)(2,1)}), bf16[32,16,256]{2,1,0:T(8,128)(2,1)S(1)}, u32[]{:S(2)}, u32[]{:S(2)}) async-start(bf16[32,16,256]{2,1,0:T(8,128)(2,1)} %get-tuple-element.9), calls=%async_computation | async-start | bytes 524288 | tf_op jit(solution)/shard_map/all_to_all | solution.py:179
  21.2 3.1 %copy.9 = bf16[4,4,256,256]{3,2,0,1:T(8,128)(2,1)} copy(bf16[4,4,256,256]{3,2,1,0:T(8,128)(2,1)} %bitcast.17) | data formatting | bytes 4194304 | tf_op jit(solution)/shard_map/reshape | solution.py:155
  24.3 8.0 %all-to-all-done.given_ref = bf16[32,16,256]{2,1,0:T(8,128)(2,1)S(1)} async-done(((bf16[32,16,256]{2,1,0:T(8,128)(2,1)}), bf16[32,16,256]{2,1,0:T(8,128)(2,1)S(1)}, u32[]{:S(2)}, u32[]{:S(2)}) %all-to-all-start) | async-done | bytes 262176 | tf_op jit(solution)/shard_map/all_to_all | solution.py:179
  32.3 0.0 copy-start.2
  32.3 0.0 copy-start.3
  32.3 0.0 copy-start.5
  32.3 4.3 %all-to-all-start.1 = ((bf16[4,4,256,256]{3,2,1,0:T(8,128)(2,1)}), bf16[4,4,256,256]{3,2,1,0:T(8,128)(2,1)S(1)}, u32[]{:S(2)}, u32[]{:S(2)}) async-start(bf16[4,4,256,256]{3,2,1,0:T(8,128)(2,1)} %bitcast.16), calls=%async_computation.1 | async-start | bytes 4194304 | tf_op jit(solution)/shard_map/all_to_all | solution.py:154
  36.6 0.0 copy-done.2
  36.6 0.0 copy-done.3
  36.6 0.0 copy-done.5
  36.6 0.8 shard_map.66
  37.4 33.2 %all-gather = bf16[1024,256]{1,0:T(8,128)(2,1)S(1)} all-gather(bf16[256,256]{1,0:T(8,128)(2,1)S(1)} %shard_map.66), channel_id=2, replica_groups={{0,4,8,12},{1,5,9,13},{2,6,10,14},{3,7,11,15},{16,20,24,28},{17,21,25,2..., dimensions={0}, use_global_device_ids=true | all-gather | bytes 655360 | tf_op jit(solution)/shard_map/all_gather | solution.py:192
  70.6 0.0 all-to-all-done.1.w_ref
  70.6 0.7 shard_map.67
  71.3 12.7 %all_to_all.15.part_ref = bf16[4,256,256]{2,1,0:T(8,128)(2,1)S(1)} all-to-all(bf16[4,256,256]{2,1,0:T(8,128)(2,1)S(1)} %shard_map.67), channel_id=1, replica_groups={{0,1,2,3},{4,5,6,7},{8,9,10,11},{12,13,14,15},{16,17,18,19},{20,21,22,2..., dimensions={0} | all-to-all | bytes 1048576 | tf_op jit(solution)/shard_map/all_to_all | solution.py:194
  84.0 0.7 shard_map.68
Async XLA Ops:
  1.7 9.0 %collective-permute-start = (bf16[8,256]{1,0:T(8,128)(2,1)}, bf16[8,256]{1,0:T(8,128)(2,1)S(1)}, u32[]{:S(2)}, u32[]{:S(2)}) collective-permute-start(bf16[8,256]{1,0:T(8,128)(2,1)} %shard_map.64), channel_id=1, source_target_pairs={{0,16},{16,32},{32,48},{48,64},{64,80},{80,96},{96,112},{112,128},... | collective-permute-start | bytes 12296 | tf_op jit(solution)/shard_map/ppermute | solution.py:165
  10.7 1.0 %copy-start = (bf16[3,256,256]{2,1,0:T(8,128)(2,1)S(1)}, bf16[3,256,256]{2,1,0:T(8,128)(2,1)}, u32[]{:S(2)}) copy-start(bf16[3,256,256]{2,1,0:T(8,128)(2,1)} %proj_ref.3) | copy-start | bytes 1179652
  11.7 0.7 copy-start.1
  12.4 0.7 copy-start.4
  15.0 17.2 %all-to-all-start = ((bf16[32,16,256]{2,1,0:T(8,128)(2,1)}), bf16[32,16,256]{2,1,0:T(8,128)(2,1)S(1)}, u32[]{:S(2)}, u32[]{:S(2)}) async-start(bf16[32,16,256]{2,1,0:T(8,128)(2,1)} %get-tuple-element.9), calls=%async_computation | async-start | bytes 524288 | tf_op jit(solution)/shard_map/all_to_all | solution.py:179
  32.3 4.3 %copy-start.2 = (f32[256,16]{0,1:T(8,128)S(1)}, f32[256,16]{0,1:T(8,128)}, u32[]{:S(2)}) copy-start(f32[256,16]{0,1:T(8,128)} %param.9) | copy-start | bytes 49156
  32.3 4.3 %copy-start.3 = (f32[256,16]{0,1:T(8,128)S(1)}, f32[256,16]{0,1:T(8,128)}, u32[]{:S(2)}) copy-start(f32[256,16]{0,1:T(8,128)} %param.8) | copy-start | bytes 49156
  32.3 4.3 %copy-start.5 = (f32[256]{0:T(256)S(1)}, f32[256]{0:T(256)}, u32[]{:S(2)}) copy-start(f32[256]{0:T(256)} %param.10) | copy-start | bytes 3076
  32.3 38.3 %all-to-all-start.1 = ((bf16[4,4,256,256]{3,2,1,0:T(8,128)(2,1)}), bf16[4,4,256,256]{3,2,1,0:T(8,128)(2,1)S(1)}, u32[]{:S(2)}, u32[]{:S(2)}) async-start(bf16[4,4,256,256]{3,2,1,0:T(8,128)(2,1)} %bitcast.16), calls=%async_computation.1 | async-start | bytes 4194304 | tf_op jit(solution)/shard_map/all_to_all | solution.py:154

commit v3 on v2

v3 whole, which is shorter than its diff:
```python
import functools

import jax
import jax.numpy as jnp
from jax import lax
from jax.experimental import pallas as pl
from jax.experimental.pallas import tpu as pltpu
from jax.sharding import PartitionSpec as P

F32 = jnp.float32
BF16 = jnp.bfloat16
LANES = 128
SUB = 8
VMEM_LIMIT = 16 * 1024 * 1024
VMEM_WHOLE = 63 * 1024 * 1024


def pallas(body, out_shape, scratch=(), vmem=VMEM_LIMIT, **kwargs):
    return pl.pallas_call(
        body,
        out_shape=out_shape,
        scratch_shapes=list(scratch),
        compiler_params=pltpu.CompilerParams(vmem_limit_bytes=vmem),
        **kwargs,
    )


def halves(width):
    return [slice(lo, lo + LANES) for lo in range(0, width, LANES)]


def spread(row):
    return jnp.broadcast_to(row, (SUB, LANES))


def fill_line(line_ref, at, block):
    for h, cols in enumerate(halves(block.shape[1])):
        line_ref[at, h, :SUB, :] = jnp.zeros((SUB, LANES), F32)
        line_ref[at, h, SUB:, :] = block[:, cols]


def short_mix(line_ref, at, h, tap, steps):
    def rows(step):
        return line_ref[at, h, pl.ds(SUB + step, SUB, stride=steps), :]

    back2, back1 = rows(-2), rows(-1)
    for p in range(steps):
        here = rows(p)
        yield tap[0] * here + tap[1] * back1 + tap[2] * back2
        back2, back1 = back1, here


def signal_steps(k_line, v_line, filter_ref, h, cols, steps):
    chunk_id = lax.broadcasted_iota(jnp.int32, (SUB, LANES), 0)
    mixes = [
        short_mix(line_ref, at, h, [spread(filter_ref[i, m : m + 1, cols]) for m in range(3)], steps)
        for i, (line_ref, at) in enumerate((k_line, v_line), start=1)
    ]
    for p, (k, v) in enumerate(zip(*mixes)):
        signal = (k * v).astype(BF16).astype(F32)
        yield jnp.where(chunk_id == 0, 0.0, signal) if p < 2 else signal


def state_kernel(k_ref, v_ref, q_edge_ref, filter_ref, decay_ref, sent_ref, line_ref, sums_ref):
    width, length = k_ref.shape[1:]
    steps = length // SUB
    modes = decay_ref.shape[0]
    blocks = [ref[0].astype(F32).T for ref in (k_ref, v_ref)]
    for i, block in enumerate(blocks):
        fill_line(line_ref, i, block)
    chunk_id = lax.broadcasted_iota(jnp.int32, (SUB, LANES), 0)
    from_end = float(steps) * (SUB - 1 - chunk_id).astype(F32)
    for h, cols in enumerate(halves(width)):
        rate = [spread(decay_ref[m : m + 1, cols]) for m in range(modes)]
        keep = [jnp.exp(-r) for r in rate]
        state = [jnp.zeros((SUB, LANES), F32) for _ in range(modes)]
        for signal in signal_steps((line_ref, 0), (line_ref, 1), filter_ref, h, cols, steps):
            state = [keep[m] * state[m] + signal for m in range(modes)]
        for m in range(modes):
            weight = jnp.exp(-rate[m] * from_end)
            sums_ref[h * modes + m : h * modes + m + 1, :] = jnp.sum(weight * state[m], axis=0, keepdims=True)
    last_q = q_edge_ref[0].astype(F32).T[-2:, :]
    edges = [blocks[0][-2:], blocks[1][-2:], blocks[0][:2], blocks[1][:2]]
    at = 2 * modes
    for h, cols in enumerate(halves(width)):
        for e, edge in enumerate(edges):
            sums_ref[at + h * SUB + 2 * e : at + h * SUB + 2 * e + 2, :] = edge[:, cols]
        sums_ref[at + 2 * SUB + 2 * h : at + 2 * SUB + 2 * h + 2, :] = last_q[:, cols]
    sums_ref[at + 2 * SUB + 4 :, :] = jnp.zeros((4, LANES), F32)
    sent = sums_ref[...].astype(BF16)
    for j in range(sent_ref.shape[0]):
        sent_ref[j] = sent


def prepare_kernel(proj_ref, filter_ref, decay_ref, signal_ref, query_ref, first_ref, ends_ref, line_ref):
    _, width, length = proj_ref.shape
    steps = length // SUB
    modes = decay_ref.shape[0]
    for i in range(3):
        fill_line(line_ref, i, proj_ref[i].astype(F32).T)
    for h, cols in enumerate(halves(width)):
        tap = [spread(filter_ref[0, m : m + 1, cols]) for m in range(3)]
        mixes = list(short_mix(line_ref, 0, h, tap, steps))
        first_ref[0, :, cols], first_ref[1, :, cols] = mixes[:2]
        for p in range(0, steps, 2):
            query_ref[p // 2, :, cols] = jnp.concatenate(mixes[p : p + 2], axis=0).astype(BF16)
        keep = [jnp.exp(-spread(decay_ref[m : m + 1, cols])) for m in range(modes)]
        state = [jnp.zeros((SUB, LANES), F32) for _ in range(modes)]
        pair = []
        for p, signal in enumerate(signal_steps((line_ref, 1), (line_ref, 2), filter_ref, h, cols, steps)):
            pair.append(signal)
            if p % 2:
                signal_ref[p // 2, :, cols] = jnp.concatenate(pair, axis=0).astype(BF16)
                pair = []
            state = [keep[m] * state[m] + signal for m in range(modes)]
        for m in range(modes):
            ends_ref[m, :, cols] = state[m]


def first_signals(taps_k, taps_v, edge, last):
    def mixed(tap, first, before):
        zero = tap[0] * first[0:1] + tap[1] * before[1:2] + tap[2] * before[0:1]
        one = tap[0] * first[1:2] + tap[1] * first[0:1] + tap[2] * before[1:2]
        return zero, one

    k = mixed(taps_k, edge[4:6], last[0:2])
    v = mixed(taps_v, edge[6:8], last[2:4])
    return [(a * b).astype(BF16).astype(F32) for a, b in zip(k, v)]


def gate_kernel(
    place_ref, given_ref, signal_ref, query_ref, first_ref, ends_ref, filter_ref, decay_ref, residue_ref, skip_ref,
    gated_ref,
    line_ref,
):
    blocks = given_ref.shape[0]
    modes, width = decay_ref.shape
    steps = 2 * signal_ref.shape[0]
    length = steps * SUB
    at = 2 * modes
    place = place_ref[0]
    chunk_id = lax.broadcasted_iota(jnp.int32, (SUB, LANES), 0)
    own = given_ref[place].astype(F32)
    before = given_ref[jnp.maximum(place - 1, 0)].astype(F32)
    before = jnp.where(place > 0, before, 0.0)
    for h, cols in enumerate(halves(width)):
        decay = decay_ref[:, cols]
        twice = 2.0 * decay
        series = jnp.ones_like(twice)
        for n in (8, 7, 6, 5, 4, 3, 2):
            series = 1.0 - twice * (1.0 / n) * series
        weight = residue_ref[:, cols] * jnp.sqrt(twice * series)
        taps = [[filter_ref[i, m : m + 1, cols] for m in range(3)] for i in range(3)]
        per_block = jnp.exp(-float(length) * decay)
        age0 = jnp.exp(-float(length - 1) * decay)
        age1 = jnp.exp(-float(length - 2) * decay)
        carry = jnp.zeros_like(decay)
        last = jnp.zeros((SUB, LANES), F32)
        for j in range(blocks - 1):
            there = given_ref[j].astype(F32)
            edge = there[at + h * SUB : at + (h + 1) * SUB]
            zero, one = first_signals(taps[1], taps[2], edge, last)
            gone = there[h * modes : (h + 1) * modes] + age0 * zero + age1 * one
            carry = jnp.where(j < place, per_block * carry + gone, carry)
            last = edge
        rows = slice(at + h * SUB, at + (h + 1) * SUB)
        firsts = first_signals(taps[1], taps[2], own[rows], before[rows])
        q_last = before[at + 2 * SUB + 2 * h : at + 2 * SUB + 2 * h + 2]
        q_more = [taps[0][1] * q_last[1:2] + taps[0][2] * q_last[0:1], taps[0][2] * q_last[1:2]]
        rate = [spread(decay[m : m + 1]) for m in range(modes)]
        keep = [jnp.exp(-r) for r in rate]
        state = []
        for m in range(modes):
            end = ends_ref[m, :, cols]
            more = jnp.exp(-float(steps - 1) * decay[m : m + 1]) * firsts[0]
            more = more + jnp.exp(-float(steps - 2) * decay[m : m + 1]) * firsts[1]
            end = jnp.where(chunk_id == 0, end + spread(more), end)
            run = jnp.where(chunk_id == 0, spread(carry[m : m + 1]), pltpu.roll(end, 1, 0))
            for far in (1, 2, 4):
                moved = jnp.where(chunk_id >= far, pltpu.roll(run, far, 0), 0.0)
                run = run + jnp.exp(-float(steps * far) * rate[m]) * moved
            state.append(run)
        gain = [spread(weight[m : m + 1]) for m in range(modes)]
        skip = spread(skip_ref[0:1, cols])
        for p in range(steps):
            if p % 2 == 0:
                signals = signal_ref[p // 2, :, cols].astype(F32)
                queries = query_ref[p // 2, :, cols].astype(F32)
            signal = signals[p % 2 * SUB : (p % 2 + 1) * SUB]
            query = queries[p % 2 * SUB : (p % 2 + 1) * SUB]
            if p < 2:
                signal = jnp.where(chunk_id == 0, spread(firsts[p]), signal)
                full = (first_ref[p, :, cols] + spread(q_more[p])).astype(BF16).astype(F32)
                query = jnp.where(chunk_id == 0, full, query)
            state = [keep[m] * state[m] + signal for m in range(modes)]
            terms = [gain[m] * state[m] for m in range(modes)]
            while len(terms) > 1:
                terms = [a + b for a, b in zip(terms[::2], terms[1::2])]
            conv = terms[0].astype(BF16).astype(F32)
            line_ref[h, pl.ds(p, SUB, stride=steps), :] = query * (conv + skip * signal)
        gated_ref[:, cols] = line_ref[h].astype(BF16)


def roll_kernel(place_ref, w_ref, *refs):
    outs, sems = refs[:-1], refs[-1]
    inner = w_ref.shape[1]
    copies = [
        pltpu.make_async_copy(w_ref.at[:, lax.rem(place_ref[0] + k, inner)], out, sems.at[k])
        for k, out in enumerate(outs)
    ]
    for copy in copies:
        copy.start()
    for copy in copies:
        copy.wait()


def mix_kernel(place_ref, gated_ref, own_ref, *refs):
    w_refs, part_ref = (own_ref,) + refs[:-1], refs[-1]
    inner = part_ref.shape[0]
    for k, w_ref in enumerate(w_refs):
        part_ref[lax.rem(place_ref[0] - k + inner, inner)] = sum(
            jnp.dot(gated_ref[z], w_ref[z], preferred_element_type=F32)
            for z in range(gated_ref.shape[0])
        ).astype(BF16)


def sum_kernel(part_ref, out_ref):
    total = part_ref[0].astype(F32)
    for k in range(1, part_ref.shape[0]):
        total = total + part_ref[k].astype(F32)
    out_ref[...] = total.astype(BF16)


def per_device(outer, proj, short_filter, residues, decays, skip, w_out):
    _, width, length = proj.shape
    modes = decays.shape[1]
    features = w_out.shape[1]
    blocks = lax.axis_size("ctx")
    groups = lax.axis_size("ch")
    inner = groups // outer
    steps = length // SUB
    shape = jax.ShapeDtypeStruct

    along_outer = [[a * inner + b for a in range(outer)] for b in range(inner)]
    along_inner = [[a * inner + b for b in range(inner)] for a in range(outer)]
    decays, residues = decays.T, residues.T
    short_filter = short_filter.swapaxes(1, 2)
    place = lax.axis_index("ctx").astype(jnp.int32).reshape(1)
    place_y = lax.rem(lax.axis_index("ch"), inner).astype(jnp.int32).reshape(1)
    whole = pl.BlockSpec(memory_space=pltpu.VMEM)
    scalar = pl.BlockSpec(memory_space=pltpu.SMEM)
    far = pl.BlockSpec(memory_space=pl.ANY)

    def full(*dims):
        return pl.BlockSpec(dims, lambda i: (0,) * len(dims))

    def one(i, lanes, at):
        return pl.BlockSpec((1, width, lanes), lambda g: (i, 0, at))

    sent_rows = 2 * modes + 3 * SUB
    sent = pallas(
        state_kernel,
        shape((blocks, sent_rows, LANES), BF16),
        (
            pltpu.VMEM((2, width // LANES, SUB + length, LANES), F32),
            pltpu.VMEM((sent_rows, LANES), F32),
        ),
        vmem=VMEM_WHOLE,
        grid=(1,),
        in_specs=[
            one(1, length, 0),
            one(2, length, 0),
            one(0, LANES, length // LANES - 1),
            full(3, 3, width),
            full(modes, width),
        ],
        out_specs=full(blocks, sent_rows, LANES),
    )(proj, proj, proj, short_filter, decays)
    given = lax.all_to_all(sent, "ctx", 0, 0)
    proj, sent = lax.optimization_barrier((proj, sent))
    signal, query, first, ends = pallas(
        prepare_kernel,
        (
            shape((steps // 2, 2 * SUB, width), BF16),
            shape((steps // 2, 2 * SUB, width), BF16),
            shape((2, SUB, width), F32),
            shape((modes, SUB, width), F32),
        ),
        (pltpu.VMEM((3, width // LANES, SUB + length, LANES), F32),),
        in_specs=[whole] * 3,
        cost_estimate=pl.CostEstimate(flops=4000000, bytes_accessed=1000000, transcendentals=0),
    )(proj, short_filter, decays)
    w_parts = w_out.reshape(outer, inner, width, features)
    place_y, first = lax.optimization_barrier((place_y, first))
    rolled = pallas(
        roll_kernel,
        [shape((outer, width, features), BF16)] * inner,
        (pltpu.SemaphoreType.DMA((inner,)),),
        in_specs=[scalar, whole],
        out_specs=[whole] + [far] * (inner - 1),
    )(place_y, w_parts)
    w_near = [
        lax.ppermute(
            part, "ch",
            [(a * inner + b, a * inner + (b + k + 1) % inner) for a in range(outer) for b in range(inner)],
        )
        for k, part in enumerate(rolled[1:])
    ]
    gated = pallas(
        gate_kernel,
        shape((length, width), BF16),
        (pltpu.VMEM((width // LANES, length, LANES), F32),),
        in_specs=[scalar] + [whole] * 9,
    )(place, given, signal, query, first, ends, short_filter, decays, residues, skip.reshape(1, width))
    near = lax.all_gather(gated, "ch", axis_index_groups=along_outer)
    parts = pallas(
        mix_kernel,
        shape((inner, length, features), BF16),
        in_specs=[scalar] + [whole] * (1 + inner),
    )(place_y, near, rolled[0], *w_near)
    parts = lax.all_to_all(parts, "ch", 0, 0, axis_index_groups=along_inner)
    return pallas(sum_kernel, shape((length, features), BF16), in_specs=[whole])(parts)


def solution(mesh):
    groups = mesh.shape["ch"]
    outer = 4 if groups % 4 == 0 else 1
    in_specs = (
        P(None, "ch", "ctx"),
        P(None, "ch", None),
        P("ch", None),
        P("ch", None),
        P("ch"),
        P(None, "ch"),
    )
    return jax.shard_map(
        functools.partial(per_device, outer),
        mesh=mesh,
        in_specs=in_specs,
        out_specs=P("ctx", "ch"),
        check_vma=False,
    )
```

time: 85.3 us -> 76.2 us (0.89)
  the two profiles are of different devices: /device:TPU:1 before, /device:TPU:2 now
where the time goes in v3:
time: 76.2 us; the launch traced here: 75.8 us
  blocking collectives  45.6 us (60%)
  starting transfers between devices  20.7 us (27%)
  Pallas kernels  7.73 us (10%)
  local copies, waits for them, and re-layouts  1.6 us (2%)
    all_gather x1, blocking collectives, per_device(): near = lax.all_gather(gated, 'ch', axis_index_groups=along_outer)  30.7 us
    all_to_all x1, blocking collectives, per_device(): parts = lax.all_to_all(parts, 'ch', 0, 0, axis_index_groups=along_inner)  14.9 us
    ppermute x3, starting transfers between devices, per_device(): lax.ppermute(part, 'ch', [(a * inner + b, a * inner + (b + k + 1) % inner...  11.2 us
    all_to_all x1, starting transfers between devices, per_device(): given = lax.all_to_all(sent, 'ctx', 0, 0)  9.58 us
    pallas_call x1, Pallas kernels, per_device(): pallas(state_kernel, shape((blocks, sent_rows, LANES), BF16), (pltpu.VMEM...  2.72 us
    unnamed x12, local copies, waits for them, and re-layouts  1.6 us
  transfers between devices with their start and end apart: 4, of which 0 were waited for; matrix products, arithmetic and copies ran while one was open for 0% of the time, Pallas kernels for 5%

profile of v3, /device:TPU:2, one launch (start us, length us, event | category | flops | bytes accessed | tf_op | source)
XLA Modules:
  0.0 75.8 jit_solution(3681251332097396745)
XLA Ops:
  0.0 0.0 copy-start
  0.0 0.0 copy-start.2
  0.0 0.0 copy-start.3
  0.0 2.7 %shard_map.64 = bf16[32,56,128]{2,1,0:T(8,128)(2,1)} custom-call(bf16[3,256,256]{2,1,0:T(8,128)(2,1)} %proj_ref, bf16[3,256,256]{2,1,0:T(8,128)(2,1)} %proj_ref, bf16[3,256,256]{2,1,0:T(8,128)(2,1)} %proj_ref, f32[3,3,256]{2,1,0:T(4,128)} %bitcast.13, f32[16,256]{1,0:T(8,128)} %bitcast.10), custom_call_target="tpu_custom_call" | custom-call | tf_op jit(solution)/shard_map/pallas_call | solution.py:261
  2.7 0.0 copy-start.4
  2.7 0.0 copy-start.5
  2.7 9.6 %all-to-all-start = ((bf16[32,56,128]{2,1,0:T(8,128)(2,1)}), bf16[32,56,128]{2,1,0:T(8,128)(2,1)S(1)}, u32[]{:S(2)}, u32[]{:S(2)}) async-start(bf16[32,56,128]{2,1,0:T(8,128)(2,1)} %shard_map.64), calls=%async_computation | async-start | bytes 917504 | tf_op jit(solution)/shard_map/all_to_all | solution.py:279
  12.3 0.0 copy-done
  12.3 0.0 copy-done.2
  12.3 0.0 copy-done.3
  12.4 1.0 %shard_map.65 = (bf16[16,16,256]{2,1,0:T(8,128)(2,1)S(1)}, bf16[16,16,256]{2,1,0:T(8,128)(2,1)S(1)}, f32[2,8,256]{2,1,0:T(8,128)S(1)}, f32[16,8,256]{2,1,0:T(8,128)S(1)}) custom-call(bf16[3,256,256]{2,1,0:T(8,128)(2,1)S(1)} %copy-done, f32[3,3,256]{2,1,0:T(4,128)S(1)} %bitcast.14, f32[16,256]{1,0:T(8,128)S(1)} %bitcast.11), custom_call_target="tpu_custom_call" | custom-call | flops 4000000 | bytes 1000000 | tf_op jit(solution)/shard_map/pallas_call | solution.py:281
  13.4 0.0 copy-start.1
  13.4 1.6 %copy-done.1 = bf16[4096,256]{1,0:T(8,128)(2,1)S(1)} copy-done((bf16[4096,256]{1,0:T(8,128)(2,1)S(1)}, bf16[4096,256]{1,0:T(8,128)(2,1)}, u32[]{:S(2)}) %copy-start.1) | copy-done | bytes 2097176
  15.0 1.2 %shard_map.67 = (bf16[4,256,256]{2,1,0:T(8,128)(2,1)S(1)}, bf16[4,256,256]{2,1,0:T(8,128)(2,1)}, bf16[4,256,256]{2,1,0:T(8,128)(2,1)}, bf16[4,256,256]{2,1,0:T(8,128)(2,1)}) custom-call(s32[1]{0:T(128)} %bitcast.place_ref, bf16[4,4,256,256]{3,2,1,0:T(8,128)(2,1)S(1)} %bitcast.8), custom_call_target="tpu_custom_call" | custom-call | tf_op jit(solution)/shard_map/pallas_call | solution.py:295
  16.2 3.1 %collective-permute-start = (bf16[4,256,256]{2,1,0:T(8,128)(2,1)}, bf16[4,256,256]{2,1,0:T(8,128)(2,1)S(1)}, u32[]{:S(2)}, u32[]{:S(2)}) collective-permute-start(bf16[4,256,256]{2,1,0:T(8,128)(2,1)} %get-tuple-element.24), channel_id=1, source_target_pairs={{0,1},{1,2},{2,3},{3,0},{4,5},{5,6},{6,7},{7,4},{8,9},{9,10},{10,1... | collective-permute-start | bytes 1572872 | tf_op jit(solution)/shard_map/ppermute | solution.py:303
  19.3 4.8 %collective-permute-start.1 = (bf16[4,256,256]{2,1,0:T(8,128)(2,1)}, bf16[4,256,256]{2,1,0:T(8,128)(2,1)S(1)}, u32[]{:S(2)}, u32[]{:S(2)}) collective-permute-start(bf16[4,256,256]{2,1,0:T(8,128)(2,1)} %get-tuple-element.25), channel_id=1, source_target_pairs={{0,2},{1,3},{2,0},{3,1},{4,6},{5,7},{6,4},{7,5},{8,10},{9,11},{10,... | collective-permute-start | bytes 1572872 | tf_op jit(solution)/shard_map/ppermute | solution.py:303
  24.1 3.3 %collective-permute-start.2 = (bf16[4,256,256]{2,1,0:T(8,128)(2,1)}, bf16[4,256,256]{2,1,0:T(8,128)(2,1)S(1)}, u32[]{:S(2)}, u32[]{:S(2)}) collective-permute-start(bf16[4,256,256]{2,1,0:T(8,128)(2,1)} %get-tuple-element.26), channel_id=1, source_target_pairs={{0,3},{1,0},{2,1},{3,2},{4,7},{5,4},{6,5},{7,6},{8,11},{9,8},{10,9... | collective-permute-start | bytes 1572872 | tf_op jit(solution)/shard_map/ppermute | solution.py:303
  27.4 0.0 all-to-all-done.given_ref
  27.4 0.0 copy-done.4
  27.4 0.0 copy-done.5
  27.4 1.3 %shard_map.66 = bf16[256,256]{1,0:T(8,128)(2,1)S(1)} custom-call(s32[1]{0:T(128)} %bitcast.3.place_ref, bf16[32,56,128]{2,1,0:T(8,128)(2,1)S(1)} %all-to-all-done.given_ref, bf16[16,16,256]{2,1,0:T(8,128)(2,1)S(1)} %get-tuple-element.19.signal_ref, bf16[16,16,256]{2,1,0:T(8,128)(2,1)S(1)} %get-tuple-element.20.query_ref, ...), custom_call_target="tpu_custom_call" | custom-call | tf_op jit(solution)/shard_map/pallas_call | solution.py:309
  28.8 30.7 %all-gather = bf16[1024,256]{1,0:T(8,128)(2,1)S(1)} all-gather(bf16[256,256]{1,0:T(8,128)(2,1)S(1)} %shard_map.66), channel_id=2, replica_groups={{0,4,8,12},{1,5,9,13},{2,6,10,14},{3,7,11,15},{16,20,24,28},{17,21,25,2..., dimensions={0}, use_global_device_ids=true | all-gather | bytes 655360 | tf_op jit(solution)/shard_map/all_gather | solution.py:315
  59.5 0.0 collective-permute-done.refs_0_
  59.5 0.0 collective-permute-done.1.refs_1_
  59.5 0.0 collective-permute-done.2.refs_2_
  59.5 0.7 shard_map.68
  60.2 14.9 %all_to_all.10.part_ref = bf16[4,256,256]{2,1,0:T(8,128)(2,1)S(1)} all-to-all(bf16[4,256,256]{2,1,0:T(8,128)(2,1)S(1)} %shard_map.68), channel_id=1, replica_groups={{0,1,2,3},{4,5,6,7},{8,9,10,11},{12,13,14,15},{16,17,18,19},{20,21,22,2..., dimensions={0} | all-to-all | bytes 1048576 | tf_op jit(solution)/shard_map/all_to_all | solution.py:321
  75.1 0.7 shard_map.69
Async XLA Ops:
  0.0 12.3 %copy-start = (bf16[3,256,256]{2,1,0:T(8,128)(2,1)S(1)}, bf16[3,256,256]{2,1,0:T(8,128)(2,1)}, u32[]{:S(2)}) copy-start(bf16[3,256,256]{2,1,0:T(8,128)(2,1)} %proj_ref) | copy-start | bytes 1179652
  0.0 12.3 %copy-start.2 = (f32[256,16]{0,1:T(8,128)S(1)}, f32[256,16]{0,1:T(8,128)}, u32[]{:S(2)}) copy-start(f32[256,16]{0,1:T(8,128)} %param.9) | copy-start | bytes 49156
  0.0 12.3 %copy-start.3 = (f32[3,256,3]{1,2,0:T(4,128)S(1)}, f32[3,256,3]{1,2,0:T(4,128)}, u32[]{:S(2)}) copy-start(f32[3,256,3]{1,2,0:T(4,128)} %param.7) | copy-start | bytes 27652
  2.7 24.7 %copy-start.4 = (f32[256,16]{0,1:T(8,128)S(1)}, f32[256,16]{0,1:T(8,128)}, u32[]{:S(2)}) copy-start(f32[256,16]{0,1:T(8,128)} %param.8) | copy-start | bytes 49156
  2.7 24.7 %copy-start.5 = (f32[256]{0:T(256)S(1)}, f32[256]{0:T(256)}, u32[]{:S(2)}) copy-start(f32[256]{0:T(256)} %param.10) | copy-start | bytes 3076
  2.7 24.7 %all-to-all-start = ((bf16[32,56,128]{2,1,0:T(8,128)(2,1)}), bf16[32,56,128]{2,1,0:T(8,128)(2,1)S(1)}, u32[]{:S(2)}, u32[]{:S(2)}) async-start(bf16[32,56,128]{2,1,0:T(8,128)(2,1)} %shard_map.64), calls=%async_computation | async-start | bytes 917504 | tf_op jit(solution)/shard_map/all_to_all | solution.py:279
  13.4 1.6 %copy-start.1 = (bf16[4096,256]{1,0:T(8,128)(2,1)S(1)}, bf16[4096,256]{1,0:T(8,128)(2,1)}, u32[]{:S(2)}) copy-start(bf16[4096,256]{1,0:T(8,128)(2,1)} %param.11) | copy-start | bytes 6291460
  16.2 43.3 %collective-permute-start = (bf16[4,256,256]{2,1,0:T(8,128)(2,1)}, bf16[4,256,256]{2,1,0:T(8,128)(2,1)S(1)}, u32[]{:S(2)}, u32[]{:S(2)}) collective-permute-start(bf16[4,256,256]{2,1,0:T(8,128)(2,1)} %get-tuple-element.24), channel_id=1, source_target_pairs={{0,1},{1,2},{2,3},{3,0},{4,5},{5,6},{6,7},{7,4},{8,9},{9,10},{10,1... | collective-permute-start | bytes 1572872 | tf_op jit(solution)/shard_map/ppermute | solution.py:303
  19.3 40.2 %collective-permute-start.1 = (bf16[4,256,256]{2,1,0:T(8,128)(2,1)}, bf16[4,256,256]{2,1,0:T(8,128)(2,1)S(1)}, u32[]{:S(2)}, u32[]{:S(2)}) collective-permute-start(bf16[4,256,256]{2,1,0:T(8,128)(2,1)} %get-tuple-element.25), channel_id=1, source_target_pairs={{0,2},{1,3},{2,0},{3,1},{4,6},{5,7},{6,4},{7,5},{8,10},{9,11},{10,... | collective-permute-start | bytes 1572872 | tf_op jit(solution)/shard_map/ppermute | solution.py:303
  24.1 35.3 %collective-permute-start.2 = (bf16[4,256,256]{2,1,0:T(8,128)(2,1)}, bf16[4,256,256]{2,1,0:T(8,128)(2,1)S(1)}, u32[]{:S(2)}, u32[]{:S(2)}) collective-permute-start(bf16[4,256,256]{2,1,0:T(8,128)(2,1)} %get-tuple-element.26), channel_id=1, source_target_pairs={{0,3},{1,0},{2,1},{3,2},{4,7},{5,4},{6,5},{7,6},{8,11},{9,8},{10,9... | collective-permute-start | bytes 1572872 | tf_op jit(solution)/shard_map/ppermute | solution.py:303

commit v4 on v3

--- a/solution.py
+++ b/solution.py
@@ -12,6 +12,7 @@
 LANES = 128
 SUB = 8
 VMEM_LIMIT = 16 * 1024 * 1024
+VMEM_MOST = 16 * 1024 * 1024
 VMEM_WHOLE = 63 * 1024 * 1024
 
 
@@ -48,6 +49,16 @@
         here = rows(p)
         yield tap[0] * here + tap[1] * back1 + tap[2] * back2
         back2, back1 = back1, here
+
+
+def w_copies(place, w_ref, outs, held_ref, come, go, ahead):
+    inner = w_ref.shape[1]
+    loads = [
+        pltpu.make_async_copy(w_ref.at[:, lax.rem(place + k, inner)], held_ref.at[n], come.at[n])
+        for n, k in enumerate(ahead)
+    ]
+    stores = [pltpu.make_async_copy(held_ref.at[n], out, go.at[n]) for n, out in enumerate(outs)]
+    return loads, stores
 
 
 def signal_steps(k_line, v_line, filter_ref, h, cols, steps):
@@ -61,13 +72,31 @@
         yield jnp.where(chunk_id == 0, 0.0, signal) if p < 2 else signal
 
 
-def state_kernel(k_ref, v_ref, q_edge_ref, filter_ref, decay_ref, sent_ref, line_ref, sums_ref):
-    width, length = k_ref.shape[1:]
+def state_kernel(ahead, place_ref, proj_hbm, filter_hbm, decay_hbm, w_hbm, sent_ref, *refs):
+    w_outs, refs = refs[: len(ahead)], refs[len(ahead) :]
+    kv_ref, q_edge_ref, filter_ref, decay_ref, line_ref, sums_ref, held_ref, sems, come, go = refs
+    _, width, length = kv_ref.shape
     steps = length // SUB
     modes = decay_ref.shape[0]
-    blocks = [ref[0].astype(F32).T for ref in (k_ref, v_ref)]
-    for i, block in enumerate(blocks):
-        fill_line(line_ref, i, block)
+    ends = pl.ds(length - LANES, LANES)
+    pairs = [
+        (proj_hbm.at[1], kv_ref.at[0]),
+        (proj_hbm.at[2], kv_ref.at[1]),
+        (filter_hbm, filter_ref),
+        (decay_hbm, decay_ref),
+        (proj_hbm.at[0, :, ends], q_edge_ref),
+    ]
+    loads = [pltpu.make_async_copy(a, b, sems.at[n]) for n, (a, b) in enumerate(pairs)]
+    w_loads, w_stores = w_copies(place_ref[0], w_hbm, w_outs, held_ref, come, go, ahead)
+    for load in loads + w_loads:
+        load.start()
+    blocks = []
+    for i in range(2):
+        loads[i].wait()
+        blocks.append(kv_ref[i].astype(F32).T)
+        fill_line(line_ref, i, blocks[i])
+    for load in loads[2:]:
+        load.wait()
     chunk_id = lax.broadcasted_iota(jnp.int32, (SUB, LANES), 0)
     from_end = float(steps) * (SUB - 1 - chunk_id).astype(F32)
     for h, cols in enumerate(halves(width)):
@@ -79,7 +108,11 @@
         for m in range(modes):
             weight = jnp.exp(-rate[m] * from_end)
             sums_ref[h * modes + m : h * modes + m + 1, :] = jnp.sum(weight * state[m], axis=0, keepdims=True)
-    last_q = q_edge_ref[0].astype(F32).T[-2:, :]
+        if h == 0:
+            for load, store in zip(w_loads, w_stores):
+                load.wait()
+                store.start()
+    last_q = q_edge_ref[...].astype(F32).T[-2:, :]
     edges = [blocks[0][-2:], blocks[1][-2:], blocks[0][:2], blocks[1][:2]]
     at = 2 * modes
     for h, cols in enumerate(halves(width)):
@@ -90,9 +123,17 @@
     sent = sums_ref[...].astype(BF16)
     for j in range(sent_ref.shape[0]):
         sent_ref[j] = sent
-
-
-def prepare_kernel(proj_ref, filter_ref, decay_ref, signal_ref, query_ref, first_ref, ends_ref, line_ref):
+    for store in w_stores:
+        store.wait()
+
+
+def prepare_kernel(
+    ahead, place_ref, proj_ref, filter_ref, decay_ref, w_hbm, signal_ref, query_ref, first_ref, ends_ref, *refs
+):
+    w_outs, (line_ref, held_ref, come, go) = refs[: len(ahead)], refs[len(ahead) :]
+    w_loads, w_stores = w_copies(place_ref[0], w_hbm, w_outs, held_ref, come, go, ahead)
+    for load in w_loads:
+        load.start()
     _, width, length = proj_ref.shape
     steps = length // SUB
     modes = decay_ref.shape[0]
@@ -115,6 +156,12 @@
             state = [keep[m] * state[m] + signal for m in range(modes)]
         for m in range(modes):
             ends_ref[m, :, cols] = state[m]
+        if h == 0:
+            for load, store in zip(w_loads, w_stores):
+                load.wait()
+                store.start()
+    for store in w_stores:
+        store.wait()
 
 
 def first_signals(taps_k, taps_v, edge, last):
@@ -201,19 +248,6 @@
         gated_ref[:, cols] = line_ref[h].astype(BF16)
 
 
-def roll_kernel(place_ref, w_ref, *refs):
-    outs, sems = refs[:-1], refs[-1]
-    inner = w_ref.shape[1]
-    copies = [
-        pltpu.make_async_copy(w_ref.at[:, lax.rem(place_ref[0] + k, inner)], out, sems.at[k])
-        for k, out in enumerate(outs)
-    ]
-    for copy in copies:
-        copy.start()
-    for copy in copies:
-        copy.wait()
-
-
 def mix_kernel(place_ref, gated_ref, own_ref, *refs):
     w_refs, part_ref = (own_ref,) + refs[:-1], refs[-1]
     inner = part_ref.shape[0]
@@ -251,60 +285,58 @@
     scalar = pl.BlockSpec(memory_space=pltpu.SMEM)
     far = pl.BlockSpec(memory_space=pl.ANY)
 
-    def full(*dims):
-        return pl.BlockSpec(dims, lambda i: (0,) * len(dims))
-
-    def one(i, lanes, at):
-        return pl.BlockSpec((1, width, lanes), lambda g: (i, 0, at))
-
     sent_rows = 2 * modes + 3 * SUB
-    sent = pallas(
-        state_kernel,
-        shape((blocks, sent_rows, LANES), BF16),
+    w_parts = w_out.reshape(outer, inner, width, features)
+    w_block = shape((outer, width, features), BF16)
+    soon, later = (1,), (0, 2, 3)
+    sent, *w_soon = pallas(
+        functools.partial(state_kernel, soon),
+        [shape((blocks, sent_rows, LANES), BF16)] + [w_block] * len(soon),
         (
+            pltpu.VMEM((2, width, length), BF16),
+            pltpu.VMEM((width, LANES), BF16),
+            pltpu.VMEM((3, 3, width), F32),
+            pltpu.VMEM((modes, width), F32),
             pltpu.VMEM((2, width // LANES, SUB + length, LANES), F32),
             pltpu.VMEM((sent_rows, LANES), F32),
+            pltpu.VMEM((len(soon), outer, width, features), BF16),
+            pltpu.SemaphoreType.DMA((5,)),
+            pltpu.SemaphoreType.DMA((len(soon),)),
+            pltpu.SemaphoreType.DMA((len(soon),)),
         ),
         vmem=VMEM_WHOLE,
-        grid=(1,),
-        in_specs=[
-            one(1, length, 0),
-            one(2, length, 0),
-            one(0, LANES, length // LANES - 1),
-            full(3, 3, width),
-            full(modes, width),
-        ],
-        out_specs=full(blocks, sent_rows, LANES),
-    )(proj, proj, proj, short_filter, decays)
+        in_specs=[scalar] + [far] * 4,
+        out_specs=[whole] + [far] * len(soon),
+    )(place_y, proj, short_filter, decays, w_parts)
     given = lax.all_to_all(sent, "ctx", 0, 0)
-    proj, sent = lax.optimization_barrier((proj, sent))
-    signal, query, first, ends = pallas(
-        prepare_kernel,
-        (
+    proj, place_later, sent = lax.optimization_barrier((proj, place_y, sent))
+    signal, query, first, ends, *w_later = pallas(
+        functools.partial(prepare_kernel, later),
+        [
             shape((steps // 2, 2 * SUB, width), BF16),
             shape((steps // 2, 2 * SUB, width), BF16),
             shape((2, SUB, width), F32),
             shape((modes, SUB, width), F32),
+        ]
+        + [w_block] * len(later),
+        (
+            pltpu.VMEM((3, width // LANES, SUB + length, LANES), F32),
+            pltpu.VMEM((len(later), outer, width, features), BF16),
+            pltpu.SemaphoreType.DMA((len(later),)),
+            pltpu.SemaphoreType.DMA((len(later),)),
         ),
-        (pltpu.VMEM((3, width // LANES, SUB + length, LANES), F32),),
-        in_specs=[whole] * 3,
-        cost_estimate=pl.CostEstimate(flops=4000000, bytes_accessed=1000000, transcendentals=0),
-    )(proj, short_filter, decays)
-    w_parts = w_out.reshape(outer, inner, width, features)
-    place_y, first = lax.optimization_barrier((place_y, first))
-    rolled = pallas(
-        roll_kernel,
-        [shape((outer, width, features), BF16)] * inner,
-        (pltpu.SemaphoreType.DMA((inner,)),),
-        in_specs=[scalar, whole],
-        out_specs=[whole] + [far] * (inner - 1),
-    )(place_y, w_parts)
+        vmem=VMEM_MOST,
+        in_specs=[scalar] + [whole] * 3 + [far],
+        out_specs=[whole] * 4 + [far] * len(later),
+        cost_estimate=pl.CostEstimate(flops=4000000, bytes_accessed=4000000, transcendentals=0),
+    )(place_later, proj, short_filter, decays, w_parts)
+    rolled = dict(zip(soon + later, w_soon + w_later))
     w_near = [
         lax.ppermute(
-            part, "ch",
-            [(a * inner + b, a * inner + (b + k + 1) % inner) for a in range(outer) for b in range(inner)],
+            rolled[k], "ch",
+            [(a * inner + b, a * inner + (b + k) % inner) for a in range(outer) for b in range(inner)],
         )
-        for k, part in enumerate(rolled[1:])
+        for k in range(1, inner)
     ]
     gated = pallas(
         gate_kernel,

time: 76.2 us -> 76 us (level)
  the two profiles are of different devices: /device:TPU:2 before, /device:TPU:32 now
where the time goes in v4:
time: 76 us; the launch traced here: 75.7 us
  blocking collectives  46 us (61%)
  starting transfers between devices  20.2 us (27%)
  Pallas kernels  7.69 us (10%)
  local copies, waits for them, and re-layouts  1.61 us (2%)
    all_gather x1, blocking collectives, per_device(): near = lax.all_gather(gated, 'ch', axis_index_groups=along_outer)  30.6 us
    all_to_all x1, blocking collectives, per_device(): parts = lax.all_to_all(parts, 'ch', 0, 0, axis_index_groups=along_inner)  15.4 us
    ppermute x3, starting transfers between devices, per_device(): lax.ppermute(rolled[k], 'ch', [(a * inner + b, a * inner + (b + k) % inne...  11.1 us
    all_to_all x1, starting transfers between devices, per_device(): given = lax.all_to_all(sent, 'ctx', 0, 0)  9.08 us
    pallas_call x1, Pallas kernels, per_device(): pallas(functools.partial(state_kernel, soon), [shape((blocks, sent_rows,...  3.16 us
    pallas_call x1, Pallas kernels, per_device(): pallas(functools.partial(prepare_kernel, later), [shape((steps // 2, 2 *...  1.8 us
    unnamed x12, local copies, waits for them, and re-layouts  1.61 us
  transfers between devices with their start and end apart: 4, of which 0 were waited for; matrix products, arithmetic and copies ran while one was open for 0% of the time, Pallas kernels for 4%

profile of v4, /device:TPU:32, one launch (start us, length us, event | category | flops | bytes accessed | tf_op | source)
XLA Modules:
  0.0 75.7 jit_solution(17963730246625931462)
XLA Ops:
  0.0 0.0 copy-start.1
  0.0 0.0 copy-start.2
  0.0 0.0 copy-start.3
  0.0 3.2 %shard_map.64 = (bf16[32,56,128]{2,1,0:T(8,128)(2,1)}, bf16[4,256,256]{2,1,0:T(8,128)(2,1)}) custom-call(s32[1]{0:T(128)} %bitcast.place_ref, bf16[3,256,256]{2,1,0:T(8,128)(2,1)} %proj_ref, f32[3,3,256]{2,1,0:T(4,128)} %bitcast.14, f32[16,256]{1,0:T(8,128)} %bitcast.11, bf16[4,4,256,256]{3,2,1,0:T(8,128)(2,1)} %bitcast.8), custom_call_target="tpu_custom_call" | custom-call | tf_op jit(solution)/shard_map/pallas_call | solution.py:292
  3.2 0.0 copy-start.4
  3.2 0.0 copy-start.5
  3.2 9.1 %all-to-all-start = ((bf16[32,56,128]{2,1,0:T(8,128)(2,1)}), bf16[32,56,128]{2,1,0:T(8,128)(2,1)S(1)}, u32[]{:S(2)}, u32[]{:S(2)}) async-start(bf16[32,56,128]{2,1,0:T(8,128)(2,1)} %get-tuple-element.16), calls=%async_computation | async-start | bytes 917504 | tf_op jit(solution)/shard_map/all_to_all | solution.py:311
  12.3 3.0 %collective-permute-start = (bf16[4,256,256]{2,1,0:T(8,128)(2,1)}, bf16[4,256,256]{2,1,0:T(8,128)(2,1)S(1)}, u32[]{:S(2)}, u32[]{:S(2)}) collective-permute-start(bf16[4,256,256]{2,1,0:T(8,128)(2,1)} %get-tuple-element.24), channel_id=1, source_target_pairs={{0,1},{1,2},{2,3},{3,0},{4,5},{5,6},{6,7},{7,4},{8,9},{9,10},{10,1... | collective-permute-start | bytes 1572872 | tf_op jit(solution)/shard_map/ppermute | solution.py:335
  15.3 0.0 copy-done.1
  15.4 0.0 copy-done.2
  15.4 0.0 copy-done.3
  15.4 0.0 copy-start
  15.4 1.6 %copy-done = bf16[4096,256]{1,0:T(8,128)(2,1)S(1)} copy-done((bf16[4096,256]{1,0:T(8,128)(2,1)S(1)}, bf16[4096,256]{1,0:T(8,128)(2,1)}, u32[]{:S(2)}) %copy-start) | copy-done | bytes 2097176
  17.0 1.8 %shard_map.65 = (bf16[16,16,256]{2,1,0:T(8,128)(2,1)S(1)}, bf16[16,16,256]{2,1,0:T(8,128)(2,1)S(1)}, f32[2,8,256]{2,1,0:T(8,128)S(1)}, f32[16,8,256]{2,1,0:T(8,1...) custom-call(s32[1]{0:T(128)} %bitcast.place_ref, ...), custom_call_target="tpu_custom_call" | custom-call | flops 4000000 | bytes 4000000 | tf_op jit(solution)/shard_map/pallas_call | solution.py:313
  18.8 4.8 %collective-permute-start.1 = (bf16[4,256,256]{2,1,0:T(8,128)(2,1)}, bf16[4,256,256]{2,1,0:T(8,128)(2,1)S(1)}, u32[]{:S(2)}, u32[]{:S(2)}) collective-permute-start(bf16[4,256,256]{2,1,0:T(8,128)(2,1)} %get-tuple-element.25), channel_id=1, source_target_pairs={{0,2},{1,3},{2,0},{3,1},{4,6},{5,7},{6,4},{7,5},{8,10},{9,11},{10,... | collective-permute-start | bytes 1572872 | tf_op jit(solution)/shard_map/ppermute | solution.py:335
  23.6 3.3 %collective-permute-start.2 = (bf16[4,256,256]{2,1,0:T(8,128)(2,1)}, bf16[4,256,256]{2,1,0:T(8,128)(2,1)S(1)}, u32[]{:S(2)}, u32[]{:S(2)}) collective-permute-start(bf16[4,256,256]{2,1,0:T(8,128)(2,1)} %get-tuple-element.26), channel_id=1, source_target_pairs={{0,3},{1,0},{2,1},{3,2},{4,7},{5,4},{6,5},{7,6},{8,11},{9,8},{10,9... | collective-permute-start | bytes 1572872 | tf_op jit(solution)/shard_map/ppermute | solution.py:335
  26.9 0.0 all-to-all-done.given_ref
  26.9 0.0 copy-done.4
  26.9 0.0 copy-done.5
  26.9 1.3 %shard_map.66 = bf16[256,256]{1,0:T(8,128)(2,1)S(1)} custom-call(s32[1]{0:T(128)} %bitcast.1.place_ref, bf16[32,56,128]{2,1,0:T(8,128)(2,1)S(1)} %all-to-all-done.given_ref, bf16[16,16,256]{2,1,0:T(8,128)(2,1)S(1)} %get-tuple-element.19.signal_ref, bf16[16,16,256]{2,1,0:T(8,128)(2,1)S(1)} %get-tuple-element.20.query_ref, ...), custom_call_target="tpu_custom_call" | custom-call | tf_op jit(solution)/shard_map/pallas_call | solution.py:341
  28.2 30.6 %all-gather = bf16[1024,256]{1,0:T(8,128)(2,1)S(1)} all-gather(bf16[256,256]{1,0:T(8,128)(2,1)S(1)} %shard_map.66), channel_id=2, replica_groups={{0,4,8,12},{1,5,9,13},{2,6,10,14},{3,7,11,15},{16,20,24,28},{17,21,25,2..., dimensions={0}, use_global_device_ids=true | all-gather | bytes 655360 | tf_op jit(solution)/shard_map/all_gather | solution.py:347
  58.8 0.0 collective-permute-done.refs_0_
  58.8 0.0 collective-permute-done.1.refs_1_
  58.8 0.0 collective-permute-done.2.refs_2_
  58.9 0.7 shard_map.67
  59.6 15.4 %all_to_all.10.part_ref = bf16[4,256,256]{2,1,0:T(8,128)(2,1)S(1)} all-to-all(bf16[4,256,256]{2,1,0:T(8,128)(2,1)S(1)} %shard_map.67), channel_id=1, replica_groups={{0,1,2,3},{4,5,6,7},{8,9,10,11},{12,13,14,15},{16,17,18,19},{20,21,22,2..., dimensions={0} | all-to-all | bytes 1048576 | tf_op jit(solution)/shard_map/all_to_all | solution.py:353
  74.9 0.7 shard_map.68
Async XLA Ops:
  0.0 15.3 %copy-start.1 = (bf16[3,256,256]{2,1,0:T(8,128)(2,1)S(1)}, bf16[3,256,256]{2,1,0:T(8,128)(2,1)}, u32[]{:S(2)}) copy-start(bf16[3,256,256]{2,1,0:T(8,128)(2,1)} %proj_ref) | copy-start | bytes 1179652
  0.0 15.4 %copy-start.2 = (f32[256,16]{0,1:T(8,128)S(1)}, f32[256,16]{0,1:T(8,128)}, u32[]{:S(2)}) copy-start(f32[256,16]{0,1:T(8,128)} %param.9) | copy-start | bytes 49156
  0.0 15.4 %copy-start.3 = (f32[3,256,3]{1,2,0:T(4,128)S(1)}, f32[3,256,3]{1,2,0:T(4,128)}, u32[]{:S(2)}) copy-start(f32[3,256,3]{1,2,0:T(4,128)} %param.7) | copy-start | bytes 27652
  3.2 23.7 %copy-start.4 = (f32[256,16]{0,1:T(8,128)S(1)}, f32[256,16]{0,1:T(8,128)}, u32[]{:S(2)}) copy-start(f32[256,16]{0,1:T(8,128)} %param.8) | copy-start | bytes 49156
  3.2 23.7 %copy-start.5 = (f32[256]{0:T(256)S(1)}, f32[256]{0:T(256)}, u32[]{:S(2)}) copy-start(f32[256]{0:T(256)} %param.10) | copy-start | bytes 3076
  3.2 23.7 %all-to-all-start = ((bf16[32,56,128]{2,1,0:T(8,128)(2,1)}), bf16[32,56,128]{2,1,0:T(8,128)(2,1)S(1)}, u32[]{:S(2)}, u32[]{:S(2)}) async-start(bf16[32,56,128]{2,1,0:T(8,128)(2,1)} %get-tuple-element.16), calls=%async_computation | async-start | bytes 917504 | tf_op jit(solution)/shard_map/all_to_all | solution.py:311
  12.3 46.5 %collective-permute-start = (bf16[4,256,256]{2,1,0:T(8,128)(2,1)}, bf16[4,256,256]{2,1,0:T(8,128)(2,1)S(1)}, u32[]{:S(2)}, u32[]{:S(2)}) collective-permute-start(bf16[4,256,256]{2,1,0:T(8,128)(2,1)} %get-tuple-element.24), channel_id=1, source_target_pairs={{0,1},{1,2},{2,3},{3,0},{4,5},{5,6},{6,7},{7,4},{8,9},{9,10},{10,1... | collective-permute-start | bytes 1572872 | tf_op jit(solution)/shard_map/ppermute | solution.py:335
  15.4 1.6 %copy-start = (bf16[4096,256]{1,0:T(8,128)(2,1)S(1)}, bf16[4096,256]{1,0:T(8,128)(2,1)}, u32[]{:S(2)}) copy-start(bf16[4096,256]{1,0:T(8,128)(2,1)} %param.11) | copy-start | bytes 6291460
  18.8 40.1 %collective-permute-start.1 = (bf16[4,256,256]{2,1,0:T(8,128)(2,1)}, bf16[4,256,256]{2,1,0:T(8,128)(2,1)S(1)}, u32[]{:S(2)}, u32[]{:S(2)}) collective-permute-start(bf16[4,256,256]{2,1,0:T(8,128)(2,1)} %get-tuple-element.25), channel_id=1, source_target_pairs={{0,2},{1,3},{2,0},{3,1},{4,6},{5,7},{6,4},{7,5},{8,10},{9,11},{10,... | collective-permute-start | bytes 1572872 | tf_op jit(solution)/shard_map/ppermute | solution.py:335
  23.6 35.3 %collective-permute-start.2 = (bf16[4,256,256]{2,1,0:T(8,128)(2,1)}, bf16[4,256,256]{2,1,0:T(8,128)(2,1)S(1)}, u32[]{:S(2)}, u32[]{:S(2)}) collective-permute-start(bf16[4,256,256]{2,1,0:T(8,128)(2,1)} %get-tuple-element.26), channel_id=1, source_target_pairs={{0,3},{1,0},{2,1},{3,2},{4,7},{5,4},{6,5},{7,6},{8,11},{9,8},{10,9... | collective-permute-start | bytes 1572872 | tf_op jit(solution)/shard_map/ppermute | solution.py:335

commit v5 on v3

--- a/solution.py
+++ b/solution.py
@@ -61,11 +61,15 @@
         yield jnp.where(chunk_id == 0, 0.0, signal) if p < 2 else signal
 
 
-def state_kernel(k_ref, v_ref, q_edge_ref, filter_ref, decay_ref, sent_ref, line_ref, sums_ref):
+def state_kernel(
+    q_ref, k_ref, v_ref, filter_ref, decay_ref,
+    sent_ref, signal_ref, query_ref, first_ref, ends_ref,
+    line_ref, sums_ref,
+):
     width, length = k_ref.shape[1:]
     steps = length // SUB
     modes = decay_ref.shape[0]
-    blocks = [ref[0].astype(F32).T for ref in (k_ref, v_ref)]
+    blocks = [ref[0].astype(F32).T for ref in (q_ref, k_ref, v_ref)]
     for i, block in enumerate(blocks):
         fill_line(line_ref, i, block)
     chunk_id = lax.broadcasted_iota(jnp.int32, (SUB, LANES), 0)
@@ -73,38 +77,6 @@
     for h, cols in enumerate(halves(width)):
         rate = [spread(decay_ref[m : m + 1, cols]) for m in range(modes)]
         keep = [jnp.exp(-r) for r in rate]
-        state = [jnp.zeros((SUB, LANES), F32) for _ in range(modes)]
-        for signal in signal_steps((line_ref, 0), (line_ref, 1), filter_ref, h, cols, steps):
-            state = [keep[m] * state[m] + signal for m in range(modes)]
-        for m in range(modes):
-            weight = jnp.exp(-rate[m] * from_end)
-            sums_ref[h * modes + m : h * modes + m + 1, :] = jnp.sum(weight * state[m], axis=0, keepdims=True)
-    last_q = q_edge_ref[0].astype(F32).T[-2:, :]
-    edges = [blocks[0][-2:], blocks[1][-2:], blocks[0][:2], blocks[1][:2]]
-    at = 2 * modes
-    for h, cols in enumerate(halves(width)):
-        for e, edge in enumerate(edges):
-            sums_ref[at + h * SUB + 2 * e : at + h * SUB + 2 * e + 2, :] = edge[:, cols]
-        sums_ref[at + 2 * SUB + 2 * h : at + 2 * SUB + 2 * h + 2, :] = last_q[:, cols]
-    sums_ref[at + 2 * SUB + 4 :, :] = jnp.zeros((4, LANES), F32)
-    sent = sums_ref[...].astype(BF16)
-    for j in range(sent_ref.shape[0]):
-        sent_ref[j] = sent
-
-
-def prepare_kernel(proj_ref, filter_ref, decay_ref, signal_ref, query_ref, first_ref, ends_ref, line_ref):
-    _, width, length = proj_ref.shape
-    steps = length // SUB
-    modes = decay_ref.shape[0]
-    for i in range(3):
-        fill_line(line_ref, i, proj_ref[i].astype(F32).T)
-    for h, cols in enumerate(halves(width)):
-        tap = [spread(filter_ref[0, m : m + 1, cols]) for m in range(3)]
-        mixes = list(short_mix(line_ref, 0, h, tap, steps))
-        first_ref[0, :, cols], first_ref[1, :, cols] = mixes[:2]
-        for p in range(0, steps, 2):
-            query_ref[p // 2, :, cols] = jnp.concatenate(mixes[p : p + 2], axis=0).astype(BF16)
-        keep = [jnp.exp(-spread(decay_ref[m : m + 1, cols])) for m in range(modes)]
         state = [jnp.zeros((SUB, LANES), F32) for _ in range(modes)]
         pair = []
         for p, signal in enumerate(signal_steps((line_ref, 1), (line_ref, 2), filter_ref, h, cols, steps)):
@@ -115,6 +87,23 @@
             state = [keep[m] * state[m] + signal for m in range(modes)]
         for m in range(modes):
             ends_ref[m, :, cols] = state[m]
+            weight = jnp.exp(-rate[m] * from_end)
+            sums_ref[h * modes + m : h * modes + m + 1, :] = jnp.sum(weight * state[m], axis=0, keepdims=True)
+        tap = [spread(filter_ref[0, m : m + 1, cols]) for m in range(3)]
+        mixes = list(short_mix(line_ref, 0, h, tap, steps))
+        first_ref[0, :, cols], first_ref[1, :, cols] = mixes[:2]
+        for p in range(0, steps, 2):
+            query_ref[p // 2, :, cols] = jnp.concatenate(mixes[p : p + 2], axis=0).astype(BF16)
+    edges = [blocks[1][-2:], blocks[2][-2:], blocks[1][:2], blocks[2][:2]]
+    at = 2 * modes
+    for h, cols in enumerate(halves(width)):
+        for e, edge in enumerate(edges):
+            sums_ref[at + h * SUB + 2 * e : at + h * SUB + 2 * e + 2, :] = edge[:, cols]
+        sums_ref[at + 2 * SUB + 2 * h : at + 2 * SUB + 2 * h + 2, :] = blocks[0][-2:, cols]
+    sums_ref[at + 2 * SUB + 4 :, :] = jnp.zeros((4, LANES), F32)
+    sent = sums_ref[...].astype(BF16)
+    for j in range(sent_ref.shape[0]):
+        sent_ref[j] = sent
 
 
 def first_signals(taps_k, taps_v, edge, last):
@@ -258,47 +247,40 @@
         return pl.BlockSpec((1, width, lanes), lambda g: (i, 0, at))
 
     sent_rows = 2 * modes + 3 * SUB
-    sent = pallas(
+    sent, signal, query, first, ends = pallas(
         state_kernel,
-        shape((blocks, sent_rows, LANES), BF16),
         (
-            pltpu.VMEM((2, width // LANES, SUB + length, LANES), F32),
-            pltpu.VMEM((sent_rows, LANES), F32),
-        ),
-        vmem=VMEM_WHOLE,
-        grid=(1,),
-        in_specs=[
-            one(1, length, 0),
-            one(2, length, 0),
-            one(0, LANES, length // LANES - 1),
-            full(3, 3, width),
-            full(modes, width),
-        ],
-        out_specs=full(blocks, sent_rows, LANES),
-    )(proj, proj, proj, short_filter, decays)
-    given = lax.all_to_all(sent, "ctx", 0, 0)
-    proj, sent = lax.optimization_barrier((proj, sent))
-    signal, query, first, ends = pallas(
-        prepare_kernel,
-        (
+            shape((blocks, sent_rows, LANES), BF16),
             shape((steps // 2, 2 * SUB, width), BF16),
             shape((steps // 2, 2 * SUB, width), BF16),
             shape((2, SUB, width), F32),
             shape((modes, SUB, width), F32),
         ),
-        (pltpu.VMEM((3, width // LANES, SUB + length, LANES), F32),),
-        in_specs=[whole] * 3,
-        cost_estimate=pl.CostEstimate(flops=4000000, bytes_accessed=1000000, transcendentals=0),
-    )(proj, short_filter, decays)
+        (
+            pltpu.VMEM((3, width // LANES, SUB + length, LANES), F32),
+            pltpu.VMEM((sent_rows, LANES), F32),
+        ),
+        vmem=VMEM_WHOLE,
+        grid=(1,),
+        in_specs=[one(i, length, 0) for i in range(3)] + [full(3, 3, width), full(modes, width)],
+        out_specs=[
+            full(blocks, sent_rows, LANES),
+            full(steps // 2, 2 * SUB, width),
+            full(steps // 2, 2 * SUB, width),
+            full(2, SUB, width),
+            full(modes, SUB, width),
+        ],
+    )(proj, proj, proj, short_filter, decays)
+    given = lax.all_to_all(sent, "ctx", 0, 0)
     w_parts = w_out.reshape(outer, inner, width, features)
-    place_y, first = lax.optimization_barrier((place_y, first))
+    place_after, sent = lax.optimization_barrier((place_y, sent))
     rolled = pallas(
         roll_kernel,
         [shape((outer, width, features), BF16)] * inner,
         (pltpu.SemaphoreType.DMA((inner,)),),
         in_specs=[scalar, whole],
         out_specs=[whole] + [far] * (inner - 1),
-    )(place_y, w_parts)
+    )(place_after, w_parts)
     w_near = [
         lax.ppermute(
             part, "ch",

time: 76.2 us -> 76.2 us (level)
  the two profiles are of different devices: /device:TPU:2 before, /device:TPU:32 now
where the time goes in v5:
time: 76.2 us; the launch traced here: 75.8 us
  blocking collectives  46.5 us (61%)
  starting transfers between devices  20.3 us (27%)
  Pallas kernels  6.94 us (9%)
  local copies, waits for them, and re-layouts  1.62 us (2%)
    all_gather x1, blocking collectives, per_device(): near = lax.all_gather(gated, 'ch', axis_index_groups=along_outer)  30.8 us
    all_to_all x1, blocking collectives, per_device(): parts = lax.all_to_all(parts, 'ch', 0, 0, axis_index_groups=along_inner)  15.7 us
    ppermute x3, starting transfers between devices, per_device(): lax.ppermute(part, 'ch', [(a * inner + b, a * inner + (b + k + 1) % inner...  11.1 us
    all_to_all x1, starting transfers between devices, per_device(): given = lax.all_to_all(sent, 'ctx', 0, 0)  9.21 us
    pallas_call x1, Pallas kernels, per_device(): pallas(state_kernel, (shape((blocks, sent_rows, LANES), BF16), shape((ste...  3.15 us
    unnamed x18, local copies, waits for them, and re-layouts  1.62 us
  transfers between devices with their start and end apart: 4, of which 1 were waited for; matrix products, arithmetic and copies ran while one was open for 0% of the time, Pallas kernels for 3%

profile of v5, /device:TPU:32, one launch (start us, length us, event | category | flops | bytes accessed | tf_op | source)
XLA Modules:
  0.0 75.8 jit_solution(16262094521500264939)
XLA Ops:
  0.0 0.0 copy-start.4
  0.0 0.0 copy-start.5
  0.0 0.0 copy-start.6
  0.0 0.0 copy-start.8
  0.0 3.2 %shard_map.64 = (bf16[32,56,128]{2,1,0:T(8,128)(2,1)}, bf16[16,16,256]{2,1,0:T(8,128)(2,1)}, bf16[16,16,256]{2,1,0:T(8,128)(2,1)}, f32[2,8,256]{2,1,0:T(8,128)}, f32[16,8,256]{2,1,0:T(8,128)}) custom-call(bf16[3,256,256]{2,1,0:T(8,128)(2,1)} %v_ref.1, bf16[3,256,256]{2,1,0:T(8,128)(2,1)} %v_ref.1, bf16[3,256,256]{2,1,0:T(8,128)(2,1)} %v_ref.1, ...), custom_call_target="tpu_custom_call" | custom-call | tf_op jit(solution)/shard_map/pallas_call | solution.py:250
  3.2 0.0 copy-start.1
  3.2 0.0 copy-start.2
  3.2 0.0 copy-start.3
  3.2 0.0 copy-start.7
  3.2 9.2 %all-to-all-start = ((bf16[32,56,128]{2,1,0:T(8,128)(2,1)}), bf16[32,56,128]{2,1,0:T(8,128)(2,1)S(1)}, u32[]{:S(2)}, u32[]{:S(2)}) async-start(bf16[32,56,128]{2,1,0:T(8,128)(2,1)} %get-tuple-element.15), calls=%async_computation | async-start | bytes 917504 | tf_op jit(solution)/shard_map/all_to_all | solution.py:274
  12.4 0.0 copy-start
  12.4 1.6 %copy-done = bf16[4096,256]{1,0:T(8,128)(2,1)S(1)} copy-done((bf16[4096,256]{1,0:T(8,128)(2,1)S(1)}, bf16[4096,256]{1,0:T(8,128)(2,1)}, u32[]{:S(2)}) %copy-start) | copy-done | bytes 2097176
  14.0 1.1 %shard_map.66 = (bf16[4,256,256]{2,1,0:T(8,128)(2,1)S(1)}, bf16[4,256,256]{2,1,0:T(8,128)(2,1)}, bf16[4,256,256]{2,1,0:T(8,128)(2,1)}, bf16[4,256,256]{2,1,0:T(8,128)(2,1)S(1)}) custom-call(s32[1]{0:T(128)} %bitcast.place_ref, bf16[4,4,256,256]{3,2,1,0:T(8,128)(2,1)S(1)} %bitcast.8), custom_call_target="tpu_custom_call" | custom-call | tf_op jit(solution)/shard_map/pallas_call | solution.py:277
  15.1 3.0 %collective-permute-start = (bf16[4,256,256]{2,1,0:T(8,128)(2,1)}, bf16[4,256,256]{2,1,0:T(8,128)(2,1)S(1)}, u32[]{:S(2)}, u32[]{:S(2)}) collective-permute-start(bf16[4,256,256]{2,1,0:T(8,128)(2,1)} %get-tuple-element.22), channel_id=1, source_target_pairs={{0,1},{1,2},{2,3},{3,0},{4,5},{5,6},{6,7},{7,4},{8,9},{9,10},{10,1... | collective-permute-start | bytes 1572872 | tf_op jit(solution)/shard_map/ppermute | solution.py:285
  18.1 4.8 %collective-permute-start.1 = (bf16[4,256,256]{2,1,0:T(8,128)(2,1)}, bf16[4,256,256]{2,1,0:T(8,128)(2,1)S(1)}, u32[]{:S(2)}, u32[]{:S(2)}) collective-permute-start(bf16[4,256,256]{2,1,0:T(8,128)(2,1)} %get-tuple-element.23), channel_id=1, source_target_pairs={{0,2},{1,3},{2,0},{3,1},{4,6},{5,7},{6,4},{7,5},{8,10},{9,11},{10,... | collective-permute-start | bytes 1572872 | tf_op jit(solution)/shard_map/ppermute | solution.py:285
  22.9 3.3 %collective-permute-start.2 = (bf16[4,256,256]{2,1,0:T(8,128)(2,1)S(1)}, bf16[4,256,256]{2,1,0:T(8,128)(2,1)S(1)}, u32[]{:S(2)}, u32[]{:S(2)}) collective-permute-start(bf16[4,256,256]{2,1,0:T(8,128)(2,1)S(1)} %get-tuple-element.24), channel_id=1, source_target_pairs={{0,3},{1,0},{2,1},{3,2},{4,7},{5,4},{6,5},{7,6},{8,11},{9,8},{10,9... | collective-permute-start | bytes 1572872 | tf_op jit(solution)/shard_map/ppermute | solution.py:285
  26.2 0.3 all-to-all-done.given_ref
  26.5 0.0 copy-done.4
  26.5 0.0 copy-done.5
  26.5 0.0 copy-done.6
  26.6 0.0 copy-done.8
  26.6 0.0 copy-done.1
  26.6 0.0 copy-done.2
  26.6 0.0 copy-done.3
  26.6 0.0 copy-done.7
  26.6 1.3 %shard_map.65 = bf16[256,256]{1,0:T(8,128)(2,1)S(1)} custom-call(s32[1]{0:T(128)} %bitcast.1.place_ref, bf16[32,56,128]{2,1,0:T(8,128)(2,1)S(1)} %all-to-all-done.given_ref, bf16[16,16,256]{2,1,0:T(8,128)(2,1)S(1)} %copy-done.1, bf16[16,16,256]{2,1,0:T(8,128)(2,1)S(1)} %copy-done.2, f32[2,8,256]{2,1,0:T(8,128)S(1)} %copy-done.7, ...), custom_call_target="tpu_custom_call" | custom-call | tf_op jit(solution)/shard_map/pallas_call | solution.py:291
  27.9 30.8 %all-gather = bf16[1024,256]{1,0:T(8,128)(2,1)S(1)} all-gather(bf16[256,256]{1,0:T(8,128)(2,1)S(1)} %shard_map.65), channel_id=2, replica_groups={{0,4,8,12},{1,5,9,13},{2,6,10,14},{3,7,11,15},{16,20,24,28},{17,21,25,2..., dimensions={0}, use_global_device_ids=true | all-gather | bytes 655360 | tf_op jit(solution)/shard_map/all_gather | solution.py:297
  58.7 0.0 collective-permute-done.refs_0_
  58.7 0.0 collective-permute-done.1.refs_1_
  58.7 0.0 collective-permute-done.2.refs_2_
  58.7 0.7 shard_map.67
  59.4 15.7 %all_to_all.10.part_ref = bf16[4,256,256]{2,1,0:T(8,128)(2,1)S(1)} all-to-all(bf16[4,256,256]{2,1,0:T(8,128)(2,1)S(1)} %shard_map.67), channel_id=1, replica_groups={{0,1,2,3},{4,5,6,7},{8,9,10,11},{12,13,14,15},{16,17,18,19},{20,21,22,2..., dimensions={0} | all-to-all | bytes 1048576 | tf_op jit(solution)/shard_map/all_to_all | solution.py:303
  75.1 0.7 shard_map.68
Async XLA Ops:
  0.0 26.5 %copy-start.4 = (f32[256,16]{0,1:T(8,128)S(1)}, f32[256,16]{0,1:T(8,128)}, u32[]{:S(2)}) copy-start(f32[256,16]{0,1:T(8,128)} %param.9) | copy-start | bytes 49156
  0.0 26.5 %copy-start.5 = (f32[3,256,3]{1,2,0:T(4,128)S(1)}, f32[3,256,3]{1,2,0:T(4,128)}, u32[]{:S(2)}) copy-start(f32[3,256,3]{1,2,0:T(4,128)} %param.7) | copy-start | bytes 27652
  0.0 26.5 %copy-start.6 = (f32[256,16]{0,1:T(8,128)S(1)}, f32[256,16]{0,1:T(8,128)}, u32[]{:S(2)}) copy-start(f32[256,16]{0,1:T(8,128)} %param.8) | copy-start | bytes 49156
  0.0 26.5 %copy-start.8 = (f32[256]{0:T(256)S(1)}, f32[256]{0:T(256)}, u32[]{:S(2)}) copy-start(f32[256]{0:T(256)} %param.10) | copy-start | bytes 3076
  3.2 23.4 %copy-start.1 = (bf16[16,16,256]{2,1,0:T(8,128)(2,1)S(1)}, bf16[16,16,256]{2,1,0:T(8,128)(2,1)}, u32[]{:S(2)}) copy-start(bf16[16,16,256]{2,1,0:T(8,128)(2,1)} %get-tuple-element.16.signal_ref) | copy-start | bytes 393220
  3.2 23.4 %copy-start.2 = (bf16[16,16,256]{2,1,0:T(8,128)(2,1)S(1)}, bf16[16,16,256]{2,1,0:T(8,128)(2,1)}, u32[]{:S(2)}) copy-start(bf16[16,16,256]{2,1,0:T(8,128)(2,1)} %get-tuple-element.17.query_ref) | copy-start | bytes 393220
  3.2 23.4 %copy-start.3 = (f32[16,8,256]{2,1,0:T(8,128)S(1)}, f32[16,8,256]{2,1,0:T(8,128)}, u32[]{:S(2)}) copy-start(f32[16,8,256]{2,1,0:T(8,128)} %get-tuple-element.19.ends_ref) | copy-start | bytes 393220
  3.2 23.4 %copy-start.7 = (f32[2,8,256]{2,1,0:T(8,128)S(1)}, f32[2,8,256]{2,1,0:T(8,128)}, u32[]{:S(2)}) copy-start(f32[2,8,256]{2,1,0:T(8,128)} %get-tuple-element.18.first_ref) | copy-start | bytes 49156
  3.2 23.3 %all-to-all-start = ((bf16[32,56,128]{2,1,0:T(8,128)(2,1)}), bf16[32,56,128]{2,1,0:T(8,128)(2,1)S(1)}, u32[]{:S(2)}, u32[]{:S(2)}) async-start(bf16[32,56,128]{2,1,0:T(8,128)(2,1)} %get-tuple-element.15), calls=%async_computation | async-start | bytes 917504 | tf_op jit(solution)/shard_map/all_to_all | solution.py:274
  12.4 1.6 %copy-start = (bf16[4096,256]{1,0:T(8,128)(2,1)S(1)}, bf16[4096,256]{1,0:T(8,128)(2,1)}, u32[]{:S(2)}) copy-start(bf16[4096,256]{1,0:T(8,128)(2,1)} %param.11) | copy-start | bytes 6291460
  15.1 43.6 %collective-permute-start = (bf16[4,256,256]{2,1,0:T(8,128)(2,1)}, bf16[4,256,256]{2,1,0:T(8,128)(2,1)S(1)}, u32[]{:S(2)}, u32[]{:S(2)}) collective-permute-start(bf16[4,256,256]{2,1,0:T(8,128)(2,1)} %get-tuple-element.22), channel_id=1, source_target_pairs={{0,1},{1,2},{2,3},{3,0},{4,5},{5,6},{6,7},{7,4},{8,9},{9,10},{10,1... | collective-permute-start | bytes 1572872 | tf_op jit(solution)/shard_map/ppermute | solution.py:285
  18.1 40.6 %collective-permute-start.1 = (bf16[4,256,256]{2,1,0:T(8,128)(2,1)}, bf16[4,256,256]{2,1,0:T(8,128)(2,1)S(1)}, u32[]{:S(2)}, u32[]{:S(2)}) collective-permute-start(bf16[4,256,256]{2,1,0:T(8,128)(2,1)} %get-tuple-element.23), channel_id=1, source_target_pairs={{0,2},{1,3},{2,0},{3,1},{4,6},{5,7},{6,4},{7,5},{8,10},{9,11},{10,... | collective-permute-start | bytes 1572872 | tf_op jit(solution)/shard_map/ppermute | solution.py:285
  22.9 35.8 %collective-permute-start.2 = (bf16[4,256,256]{2,1,0:T(8,128)(2,1)S(1)}, bf16[4,256,256]{2,1,0:T(8,128)(2,1)S(1)}, u32[]{:S(2)}, u32[]{:S(2)}) collective-permute-start(bf16[4,256,256]{2,1,0:T(8,128)(2,1)S(1)} %get-tuple-element.24), channel_id=1, source_target_pairs={{0,3},{1,0},{2,1},{3,2},{4,7},{5,4},{6,5},{7,6},{8,11},{9,8},{10,9... | collective-permute-start | bytes 1572872 | tf_op jit(solution)/shard_map/ppermute | solution.py:285

commit v6 on v5

--- a/solution.py
+++ b/solution.py
@@ -192,11 +192,15 @@
 
 def roll_kernel(place_ref, w_ref, *refs):
     outs, sems = refs[:-1], refs[-1]
-    inner = w_ref.shape[1]
-    copies = [
-        pltpu.make_async_copy(w_ref.at[:, lax.rem(place_ref[0] + k, inner)], out, sems.at[k])
-        for k, out in enumerate(outs)
-    ]
+    outer, inner = w_ref.shape[:2]
+    most, start = outer - 1, place_ref[1]
+    copies = []
+    for k, out in enumerate(outs):
+        y = lax.rem(place_ref[0] + k, inner)
+        copies.append(
+            pltpu.make_async_copy(w_ref.at[pl.ds(start, most), y], out.at[pl.ds(0, most)], sems.at[k, 0])
+        )
+        copies.append(pltpu.make_async_copy(w_ref.at[lax.rem(start + most, outer), y], out.at[most], sems.at[k, 1]))
     for copy in copies:
         copy.start()
     for copy in copies:
@@ -230,8 +234,20 @@
     steps = length // SUB
     shape = jax.ShapeDtypeStruct
 
-    along_outer = [[a * inner + b for a in range(outer)] for b in range(inner)]
     along_inner = [[a * inner + b for b in range(inner)] for a in range(outer)]
+    from_zero = ([0, 1], [2, 3]), ([0, 3], [1, 2])
+    from_one = ([1, 2], [3, 0]), ([1, 0], [2, 3])
+    turns = (from_one, from_zero)
+
+    def rings(turn):
+        return [
+            [i * groups + a * inner + b for a in pair]
+            for i in range(blocks)
+            for b in range(inner)
+            for pair in turns[i % 2][turn]
+        ]
+
+    odd = lax.rem(lax.axis_index("ctx"), 2)
     decays, residues = decays.T, residues.T
     short_filter = short_filter.swapaxes(1, 2)
     place = lax.axis_index("ctx").astype(jnp.int32).reshape(1)
@@ -273,14 +289,15 @@
     )(proj, proj, proj, short_filter, decays)
     given = lax.all_to_all(sent, "ctx", 0, 0)
     w_parts = w_out.reshape(outer, inner, width, features)
-    place_after, sent = lax.optimization_barrier((place_y, sent))
+    spots = jnp.stack([place_y[0], 1 - odd]).astype(jnp.int32)
+    spots, sent = lax.optimization_barrier((spots, sent))
     rolled = pallas(
         roll_kernel,
         [shape((outer, width, features), BF16)] * inner,
-        (pltpu.SemaphoreType.DMA((inner,)),),
+        (pltpu.SemaphoreType.DMA((inner, 2)),),
         in_specs=[scalar, whole],
         out_specs=[whole] + [far] * (inner - 1),
-    )(place_after, w_parts)
+    )(spots, w_parts)
     w_near = [
         lax.ppermute(
             part, "ch",
@@ -294,7 +311,8 @@
         (pltpu.VMEM((width // LANES, length, LANES), F32),),
         in_specs=[scalar] + [whole] * 9,
     )(place, given, signal, query, first, ends, short_filter, decays, residues, skip.reshape(1, width))
-    near = lax.all_gather(gated, "ch", axis_index_groups=along_outer)
+    near = lax.all_gather(gated, ("ctx", "ch"), axis_index_groups=rings(0))
+    near = lax.all_gather(near, ("ctx", "ch"), axis_index_groups=rings(1)).reshape(outer, length, width)
     parts = pallas(
         mix_kernel,
         shape((inner, length, features), BF16),

time: 76.2 us -> 75.1 us (0.986)
  the two profiles are of different devices: /device:TPU:32 before, /device:TPU:64 now
where the time goes in v6:
time: 75.1 us; the launch traced here: 74.8 us
  blocking collectives  45.3 us (60%)
  starting transfers between devices  19.9 us (26%)
  Pallas kernels  7.74 us (10%)
  local copies, waits for them, and re-layouts  1.62 us (2%)
    all_gather x1, blocking collectives, per_device(): lax.all_gather(near, ('ctx', 'ch'), axis_index_groups=rings(1))  18.7 us
    all_gather x1, blocking collectives, per_device(): near = lax.all_gather(gated, ('ctx', 'ch'), axis_index_groups=rings(0))  14.3 us
    all_to_all x1, blocking collectives, per_device(): parts = lax.all_to_all(parts, 'ch', 0, 0, axis_index_groups=along_inner)  12.3 us
    ppermute x3, starting transfers between devices, per_device(): lax.ppermute(part, 'ch', [(a * inner + b, a * inner + (b + k + 1) % inner...  11.1 us
    all_to_all x1, starting transfers between devices, per_device(): given = lax.all_to_all(sent, 'ctx', 0, 0)  8.81 us
    pallas_call x1, Pallas kernels, per_device(): pallas(state_kernel, (shape((blocks, sent_rows, LANES), BF16), shape((ste...  3.15 us
    pallas_call x1, Pallas kernels, per_device(): pallas(roll_kernel, [shape((outer, width, features), BF16)] * inner, (plt...  1.84 us
    unnamed x18, local copies, waits for them, and re-layouts  1.62 us
  transfers between devices with their start and end apart: 4, of which 0 were waited for; matrix products, arithmetic and copies ran while one was open for 0% of the time, Pallas kernels for 4%

profile of v6, /device:TPU:64, one launch (start us, length us, event | category | flops | bytes accessed | tf_op | source)
XLA Modules:
  0.0 74.8 jit_solution(14566217606166526669)
XLA Ops:
  0.0 0.0 copy-start.4
  0.0 0.0 copy-start.5
  0.0 0.0 copy-start.6
  0.0 0.0 copy-start.8
  0.0 3.2 %shard_map.64 = (bf16[32,56,128]{2,1,0:T(8,128)(2,1)}, bf16[16,16,256]{2,1,0:T(8,128)(2,1)}, bf16[16,16,256]{2,1,0:T(8,128)(2,1)}, f32[2,8,256]{2,1,0:T(8,128)}, f32[16,8,256]{2,1,0:T(8,128)}) custom-call(bf16[3,256,256]{2,1,0:T(8,128)(2,1)} %v_ref.1, bf16[3,256,256]{2,1,0:T(8,128)(2,1)} %v_ref.1, bf16[3,256,256]{2,1,0:T(8,128)(2,1)} %v_ref.1, ...), custom_call_target="tpu_custom_call" | custom-call | tf_op jit(solution)/shard_map/pallas_call | solution.py:266
  3.2 0.0 copy-start.1
  3.2 0.0 copy-start.2
  3.2 0.0 copy-start.3
  3.2 0.0 copy-start.7
  3.2 8.8 %all-to-all-start = ((bf16[32,56,128]{2,1,0:T(8,128)(2,1)}), bf16[32,56,128]{2,1,0:T(8,128)(2,1)S(1)}, u32[]{:S(2)}, u32[]{:S(2)}) async-start(bf16[32,56,128]{2,1,0:T(8,128)(2,1)} %get-tuple-element.15), calls=%async_computation | async-start | bytes 917504 | tf_op jit(solution)/shard_map/all_to_all | solution.py:290
  12.0 0.1 pad_add_fusion.place_ref
  12.1 0.0 copy-start
  12.1 1.6 %copy-done = bf16[4096,256]{1,0:T(8,128)(2,1)S(1)} copy-done((bf16[4096,256]{1,0:T(8,128)(2,1)S(1)}, bf16[4096,256]{1,0:T(8,128)(2,1)}, u32[]{:S(2)}) %copy-start) | copy-done | bytes 2097176
  13.7 1.8 %shard_map.66 = (bf16[4,256,256]{2,1,0:T(8,128)(2,1)S(1)}, bf16[4,256,256]{2,1,0:T(8,128)(2,1)}, bf16[4,256,256]{2,1,0:T(8,128)(2,1)}, bf16[4,256,256]{2,1,0:T(8,128)(2,1)S(1)}) custom-call(s32[2]{0:T(128)S(1)} %pad_add_fusion.place_ref, bf16[4,4,256,256]{3,2,1,0:T(8,128)(2,1)S(1)} %bitcast.9), custom_call_target="tpu_custom_call" | custom-call | tf_op jit(solution)/shard_map/pallas_call | solution.py:294
  15.5 3.0 %collective-permute-start = (bf16[4,256,256]{2,1,0:T(8,128)(2,1)}, bf16[4,256,256]{2,1,0:T(8,128)(2,1)S(1)}, u32[]{:S(2)}, u32[]{:S(2)}) collective-permute-start(bf16[4,256,256]{2,1,0:T(8,128)(2,1)} %get-tuple-element.22), channel_id=1, source_target_pairs={{0,1},{1,2},{2,3},{3,0},{4,5},{5,6},{6,7},{7,4},{8,9},{9,10},{10,1... | collective-permute-start | bytes 1572872 | tf_op jit(solution)/shard_map/ppermute | solution.py:302
  18.5 4.8 %collective-permute-start.1 = (bf16[4,256,256]{2,1,0:T(8,128)(2,1)}, bf16[4,256,256]{2,1,0:T(8,128)(2,1)S(1)}, u32[]{:S(2)}, u32[]{:S(2)}) collective-permute-start(bf16[4,256,256]{2,1,0:T(8,128)(2,1)} %get-tuple-element.23), channel_id=1, source_target_pairs={{0,2},{1,3},{2,0},{3,1},{4,6},{5,7},{6,4},{7,5},{8,10},{9,11},{10,... | collective-permute-start | bytes 1572872 | tf_op jit(solution)/shard_map/ppermute | solution.py:302
  23.4 3.3 %collective-permute-start.2 = (bf16[4,256,256]{2,1,0:T(8,128)(2,1)S(1)}, bf16[4,256,256]{2,1,0:T(8,128)(2,1)S(1)}, u32[]{:S(2)}, u32[]{:S(2)}) collective-permute-start(bf16[4,256,256]{2,1,0:T(8,128)(2,1)S(1)} %get-tuple-element.24), channel_id=1, source_target_pairs={{0,3},{1,0},{2,1},{3,2},{4,7},{5,4},{6,5},{7,6},{8,11},{9,8},{10,9... | collective-permute-start | bytes 1572872 | tf_op jit(solution)/shard_map/ppermute | solution.py:302
  26.6 0.0 all-to-all-done.given_ref
  26.6 0.0 copy-done.4
  26.6 0.0 copy-done.5
  26.6 0.0 copy-done.6
  26.7 0.0 copy-done.8
  26.7 0.0 copy-done.1
  26.7 0.0 copy-done.2
  26.7 0.0 copy-done.3
  26.7 0.0 copy-done.7
  26.7 1.3 %shard_map.65 = bf16[256,256]{1,0:T(8,128)(2,1)S(1)} custom-call(s32[1]{0:T(128)} %bitcast.1.place_ref, bf16[32,56,128]{2,1,0:T(8,128)(2,1)S(1)} %all-to-all-done.given_ref, bf16[16,16,256]{2,1,0:T(8,128)(2,1)S(1)} %copy-done.1, bf16[16,16,256]{2,1,0:T(8,128)(2,1)S(1)} %copy-done.2, f32[2,8,256]{2,1,0:T(8,128)S(1)} %copy-done.7, ...), custom_call_target="tpu_custom_call" | custom-call | tf_op jit(solution)/shard_map/pallas_call | solution.py:308
  28.0 14.3 %all-gather = bf16[512,256]{1,0:T(8,128)(2,1)S(1)} all-gather(bf16[256,256]{1,0:T(8,128)(2,1)S(1)} %shard_map.65), channel_id=2, replica_groups={{4,8},{12,0},{5,9},{13,1},{6,10},{14,2},{7,11},{15,3},{16,20},{24,28},{..., dimensions={0}, use_global_device_ids=true | all-gather | bytes 393216 | tf_op jit(solution)/shard_map/all_gather | solution.py:314
  42.3 18.7 %all-gather.1.gated_ref = bf16[4,256,256]{2,1,0:T(8,128)(2,1)S(1)} all-gather(bf16[2,256,256]{2,1,0:T(8,128)(2,1)S(1)} %bitcast.16), channel_id=3, replica_groups={{4,0},{8,12},{5,1},{9,13},{6,2},{10,14},{7,3},{11,15},{16,28},{20,24},{..., dimensions={0}, use_global_device_ids=true | all-gather | bytes 786432 | tf_op jit(solution)/shard_map/all_gather | solution.py:315
  61.0 0.0 collective-permute-done.refs_0_
  61.0 0.0 collective-permute-done.1.refs_1_
  61.0 0.0 collective-permute-done.2.refs_2_
  61.0 0.7 shard_map.67
  61.8 12.3 %all_to_all.10.part_ref = bf16[4,256,256]{2,1,0:T(8,128)(2,1)S(1)} all-to-all(bf16[4,256,256]{2,1,0:T(8,128)(2,1)S(1)} %shard_map.67), channel_id=1, replica_groups={{0,1,2,3},{4,5,6,7},{8,9,10,11},{12,13,14,15},{16,17,18,19},{20,21,22,2..., dimensions={0} | all-to-all | bytes 1048576 | tf_op jit(solution)/shard_map/all_to_all | solution.py:321
  74.0 0.7 shard_map.68
Async XLA Ops:
  0.0 26.6 %copy-start.4 = (f32[256,16]{0,1:T(8,128)S(1)}, f32[256,16]{0,1:T(8,128)}, u32[]{:S(2)}) copy-start(f32[256,16]{0,1:T(8,128)} %param.9) | copy-start | bytes 49156
  0.0 26.6 %copy-start.5 = (f32[3,256,3]{1,2,0:T(4,128)S(1)}, f32[3,256,3]{1,2,0:T(4,128)}, u32[]{:S(2)}) copy-start(f32[3,256,3]{1,2,0:T(4,128)} %param.7) | copy-start | bytes 27652
  0.0 26.6 %copy-start.6 = (f32[256,16]{0,1:T(8,128)S(1)}, f32[256,16]{0,1:T(8,128)}, u32[]{:S(2)}) copy-start(f32[256,16]{0,1:T(8,128)} %param.8) | copy-start | bytes 49156
  0.0 26.6 %copy-start.8 = (f32[256]{0:T(256)S(1)}, f32[256]{0:T(256)}, u32[]{:S(2)}) copy-start(f32[256]{0:T(256)} %param.10) | copy-start | bytes 3076
  3.2 23.5 %copy-start.1 = (bf16[16,16,256]{2,1,0:T(8,128)(2,1)S(1)}, bf16[16,16,256]{2,1,0:T(8,128)(2,1)}, u32[]{:S(2)}) copy-start(bf16[16,16,256]{2,1,0:T(8,128)(2,1)} %get-tuple-element.16.signal_ref) | copy-start | bytes 393220
  3.2 23.5 %copy-start.2 = (bf16[16,16,256]{2,1,0:T(8,128)(2,1)S(1)}, bf16[16,16,256]{2,1,0:T(8,128)(2,1)}, u32[]{:S(2)}) copy-start(bf16[16,16,256]{2,1,0:T(8,128)(2,1)} %get-tuple-element.17.query_ref) | copy-start | bytes 393220
  3.2 23.5 %copy-start.3 = (f32[16,8,256]{2,1,0:T(8,128)S(1)}, f32[16,8,256]{2,1,0:T(8,128)}, u32[]{:S(2)}) copy-start(f32[16,8,256]{2,1,0:T(8,128)} %get-tuple-element.19.ends_ref) | copy-start | bytes 393220
  3.2 23.5 %copy-start.7 = (f32[2,8,256]{2,1,0:T(8,128)S(1)}, f32[2,8,256]{2,1,0:T(8,128)}, u32[]{:S(2)}) copy-start(f32[2,8,256]{2,1,0:T(8,128)} %get-tuple-element.18.first_ref) | copy-start | bytes 49156
  3.2 23.4 %all-to-all-start = ((bf16[32,56,128]{2,1,0:T(8,128)(2,1)}), bf16[32,56,128]{2,1,0:T(8,128)(2,1)S(1)}, u32[]{:S(2)}, u32[]{:S(2)}) async-start(bf16[32,56,128]{2,1,0:T(8,128)(2,1)} %get-tuple-element.15), calls=%async_computation | async-start | bytes 917504 | tf_op jit(solution)/shard_map/all_to_all | solution.py:290
  12.1 1.6 %copy-start = (bf16[4096,256]{1,0:T(8,128)(2,1)S(1)}, bf16[4096,256]{1,0:T(8,128)(2,1)}, u32[]{:S(2)}) copy-start(bf16[4096,256]{1,0:T(8,128)(2,1)} %param.11) | copy-start | bytes 6291460
  15.5 45.5 %collective-permute-start = (bf16[4,256,256]{2,1,0:T(8,128)(2,1)}, bf16[4,256,256]{2,1,0:T(8,128)(2,1)S(1)}, u32[]{:S(2)}, u32[]{:S(2)}) collective-permute-start(bf16[4,256,256]{2,1,0:T(8,128)(2,1)} %get-tuple-element.22), channel_id=1, source_target_pairs={{0,1},{1,2},{2,3},{3,0},{4,5},{5,6},{6,7},{7,4},{8,9},{9,10},{10,1... | collective-permute-start | bytes 1572872 | tf_op jit(solution)/shard_map/ppermute | solution.py:302
  18.5 42.5 %collective-permute-start.1 = (bf16[4,256,256]{2,1,0:T(8,128)(2,1)}, bf16[4,256,256]{2,1,0:T(8,128)(2,1)S(1)}, u32[]{:S(2)}, u32[]{:S(2)}) collective-permute-start(bf16[4,256,256]{2,1,0:T(8,128)(2,1)} %get-tuple-element.23), channel_id=1, source_target_pairs={{0,2},{1,3},{2,0},{3,1},{4,6},{5,7},{6,4},{7,5},{8,10},{9,11},{10,... | collective-permute-start | bytes 1572872 | tf_op jit(solution)/shard_map/ppermute | solution.py:302
  23.4 37.7 %collective-permute-start.2 = (bf16[4,256,256]{2,1,0:T(8,128)(2,1)S(1)}, bf16[4,256,256]{2,1,0:T(8,128)(2,1)S(1)}, u32[]{:S(2)}, u32[]{:S(2)}) collective-permute-start(bf16[4,256,256]{2,1,0:T(8,128)(2,1)S(1)} %get-tuple-element.24), channel_id=1, source_target_pairs={{0,3},{1,0},{2,1},{3,2},{4,7},{5,4},{6,5},{7,6},{8,11},{9,8},{10,9... | collective-permute-start | bytes 1572872 | tf_op jit(solution)/shard_map/ppermute | solution.py:302

commit v7 on v6

--- a/solution.py
+++ b/solution.py
@@ -69,7 +69,7 @@
     width, length = k_ref.shape[1:]
     steps = length // SUB
     modes = decay_ref.shape[0]
-    blocks = [ref[0].astype(F32).T for ref in (q_ref, k_ref, v_ref)]
+    blocks = [ref[0].T.astype(F32) for ref in (q_ref, k_ref, v_ref)]
     for i, block in enumerate(blocks):
         fill_line(line_ref, i, block)
     chunk_id = lax.broadcasted_iota(jnp.int32, (SUB, LANES), 0)
@@ -98,7 +98,9 @@
     at = 2 * modes
     for h, cols in enumerate(halves(width)):
         for e, edge in enumerate(edges):
-            sums_ref[at + h * SUB + 2 * e : at + h * SUB + 2 * e + 2, :] = edge[:, cols]
+            for r in range(2):
+                row = at + 2 * (2 * e + r) + h
+                sums_ref[row : row + 1, :] = edge[r : r + 1, cols]
         sums_ref[at + 2 * SUB + 2 * h : at + 2 * SUB + 2 * h + 2, :] = blocks[0][-2:, cols]
     sums_ref[at + 2 * SUB + 4 :, :] = jnp.zeros((4, LANES), F32)
     sent = sums_ref[...].astype(BF16)
@@ -107,14 +109,16 @@
 
 
 def first_signals(taps_k, taps_v, edge, last):
-    def mixed(tap, first, before):
-        zero = tap[0] * first[0:1] + tap[1] * before[1:2] + tap[2] * before[0:1]
-        one = tap[0] * first[1:2] + tap[1] * first[0:1] + tap[2] * before[1:2]
+    def item(rows, n):
+        return rows[2 * n : 2 * n + 2]
+
+    def mixed(tap, n):
+        before2, before1, here, after = item(last, n), item(last, n + 1), item(edge, n + 4), item(edge, n + 5)
+        zero = tap[0] * here + tap[1] * before1 + tap[2] * before2
+        one = tap[0] * after + tap[1] * here + tap[2] * before1
         return zero, one
 
-    k = mixed(taps_k, edge[4:6], last[0:2])
-    v = mixed(taps_v, edge[6:8], last[2:4])
-    return [(a * b).astype(BF16).astype(F32) for a, b in zip(k, v)]
+    return [(a * b).astype(BF16).astype(F32) for a, b in zip(mixed(taps_k, 0), mixed(taps_v, 2))]
 
 
 def gate_kernel(
@@ -132,30 +136,33 @@
     own = given_ref[place].astype(F32)
     before = given_ref[jnp.maximum(place - 1, 0)].astype(F32)
     before = jnp.where(place > 0, before, 0.0)
-    for h, cols in enumerate(halves(width)):
+    parts = halves(width)
+    rows = slice(at, at + 2 * SUB)
+    both = [[jnp.concatenate([filter_ref[i, m : m + 1, cols] for cols in parts], 0) for m in range(3)] for i in (1, 2)]
+    ages = [[jnp.exp(-float(length - n) * decay_ref[:, cols]) for cols in parts] for n in range(3)]
+    carries = [jnp.zeros((modes, LANES), F32) for _ in parts]
+    last = jnp.zeros((2 * SUB, LANES), F32)
+    for j in range(blocks - 1):
+        there = given_ref[j].astype(F32)
+        edge = there[rows]
+        zero, one = first_signals(*both, edge, last)
+        for h in range(2):
+            gone = there[h * modes : (h + 1) * modes] + ages[1][h] * zero[h : h + 1] + ages[2][h] * one[h : h + 1]
+            carries[h] = jnp.where(j < place, ages[0][h] * carries[h] + gone, carries[h])
+        last = edge
+    own_first = first_signals(*both, own[rows], before[rows])
+    for h, cols in enumerate(parts):
         decay = decay_ref[:, cols]
         twice = 2.0 * decay
         series = jnp.ones_like(twice)
         for n in (8, 7, 6, 5, 4, 3, 2):
             series = 1.0 - twice * (1.0 / n) * series
         weight = residue_ref[:, cols] * jnp.sqrt(twice * series)
-        taps = [[filter_ref[i, m : m + 1, cols] for m in range(3)] for i in range(3)]
-        per_block = jnp.exp(-float(length) * decay)
-        age0 = jnp.exp(-float(length - 1) * decay)
-        age1 = jnp.exp(-float(length - 2) * decay)
-        carry = jnp.zeros_like(decay)
-        last = jnp.zeros((SUB, LANES), F32)
-        for j in range(blocks - 1):
-            there = given_ref[j].astype(F32)
-            edge = there[at + h * SUB : at + (h + 1) * SUB]
-            zero, one = first_signals(taps[1], taps[2], edge, last)
-            gone = there[h * modes : (h + 1) * modes] + age0 * zero + age1 * one
-            carry = jnp.where(j < place, per_block * carry + gone, carry)
-            last = edge
-        rows = slice(at + h * SUB, at + (h + 1) * SUB)
-        firsts = first_signals(taps[1], taps[2], own[rows], before[rows])
+        carry = carries[h]
+        firsts = [f[h : h + 1] for f in own_first]
+        tap = [filter_ref[0, m : m + 1, cols] for m in range(3)]
         q_last = before[at + 2 * SUB + 2 * h : at + 2 * SUB + 2 * h + 2]
-        q_more = [taps[0][1] * q_last[1:2] + taps[0][2] * q_last[0:1], taps[0][2] * q_last[1:2]]
+        q_more = [tap[1] * q_last[1:2] + tap[2] * q_last[0:1], tap[2] * q_last[1:2]]
         rate = [spread(decay[m : m + 1]) for m in range(modes)]
         keep = [jnp.exp(-r) for r in rate]
         state = []

time: 75.1 us -> 74.9 us (level)
  no operation moved by 1% of the time
where the time goes in v7:
time: 74.9 us; the launch traced here: 74.5 us
  blocking collectives  45.3 us (60%)
  starting transfers between devices  19.9 us (27%)
  Pallas kernels  7.53 us (10%)
  local copies, waits for them, and re-layouts  1.62 us (2%)
    all_gather x1, blocking collectives, per_device(): lax.all_gather(near, ('ctx', 'ch'), axis_index_groups=rings(1))  18.7 us
    all_gather x1, blocking collectives, per_device(): near = lax.all_gather(gated, ('ctx', 'ch'), axis_index_groups=rings(0))  14.3 us
    all_to_all x1, blocking collectives, per_device(): parts = lax.all_to_all(parts, 'ch', 0, 0, axis_index_groups=along_inner)  12.3 us
    ppermute x3, starting transfers between devices, per_device(): lax.ppermute(part, 'ch', [(a * inner + b, a * inner + (b + k + 1) % inner...  11.1 us
    all_to_all x1, starting transfers between devices, per_device(): given = lax.all_to_all(sent, 'ctx', 0, 0)  8.81 us
    pallas_call x1, Pallas kernels, per_device(): pallas(state_kernel, (shape((blocks, sent_rows, LANES), BF16), shape((ste...  3.12 us
    pallas_call x1, Pallas kernels, per_device(): pallas(roll_kernel, [shape((outer, width, features), BF16)] * inner, (plt...  1.84 us
    unnamed x18, local copies, waits for them, and re-layouts  1.62 us
  transfers between devices with their start and end apart: 4, of which 0 were waited for; matrix products, arithmetic and copies ran while one was open for 0% of the time, Pallas kernels for 4%

profile of v7, /device:TPU:64, one launch (start us, length us, event | category | flops | bytes accessed | tf_op | source)
XLA Modules:
  0.0 74.5 jit_solution(11634464501884710451)
XLA Ops:
  0.0 0.0 copy-start.4
  0.0 0.0 copy-start.5
  0.0 0.0 copy-start.6
  0.0 0.0 copy-start.8
  0.0 3.1 %shard_map.64 = (bf16[32,56,128]{2,1,0:T(8,128)(2,1)}, bf16[16,16,256]{2,1,0:T(8,128)(2,1)}, bf16[16,16,256]{2,1,0:T(8,128)(2,1)}, f32[2,8,256]{2,1,0:T(8,128)}, f32[16,8,256]{2,1,0:T(8,128)}) custom-call(bf16[3,256,256]{2,1,0:T(8,128)(2,1)} %v_ref.1, bf16[3,256,256]{2,1,0:T(8,128)(2,1)} %v_ref.1, bf16[3,256,256]{2,1,0:T(8,128)(2,1)} %v_ref.1, ...), custom_call_target="tpu_custom_call" | custom-call | tf_op jit(solution)/shard_map/pallas_call | solution.py:273
  3.1 0.0 copy-start.1
  3.1 0.0 copy-start.2
  3.1 0.0 copy-start.3
  3.1 0.0 copy-start.7
  3.2 8.8 %all-to-all-start = ((bf16[32,56,128]{2,1,0:T(8,128)(2,1)}), bf16[32,56,128]{2,1,0:T(8,128)(2,1)S(1)}, u32[]{:S(2)}, u32[]{:S(2)}) async-start(bf16[32,56,128]{2,1,0:T(8,128)(2,1)} %get-tuple-element.15), calls=%async_computation | async-start | bytes 917504 | tf_op jit(solution)/shard_map/all_to_all | solution.py:297
  12.0 0.1 pad_add_fusion.place_ref
  12.1 0.0 copy-start
  12.1 1.6 %copy-done = bf16[4096,256]{1,0:T(8,128)(2,1)S(1)} copy-done((bf16[4096,256]{1,0:T(8,128)(2,1)S(1)}, bf16[4096,256]{1,0:T(8,128)(2,1)}, u32[]{:S(2)}) %copy-start) | copy-done | bytes 2097176
  13.6 1.8 %shard_map.66 = (bf16[4,256,256]{2,1,0:T(8,128)(2,1)S(1)}, bf16[4,256,256]{2,1,0:T(8,128)(2,1)}, bf16[4,256,256]{2,1,0:T(8,128)(2,1)}, bf16[4,256,256]{2,1,0:T(8,128)(2,1)S(1)}) custom-call(s32[2]{0:T(128)S(1)} %pad_add_fusion.place_ref, bf16[4,4,256,256]{3,2,1,0:T(8,128)(2,1)S(1)} %bitcast.9), custom_call_target="tpu_custom_call" | custom-call | tf_op jit(solution)/shard_map/pallas_call | solution.py:301
  15.5 3.0 %collective-permute-start = (bf16[4,256,256]{2,1,0:T(8,128)(2,1)}, bf16[4,256,256]{2,1,0:T(8,128)(2,1)S(1)}, u32[]{:S(2)}, u32[]{:S(2)}) collective-permute-start(bf16[4,256,256]{2,1,0:T(8,128)(2,1)} %get-tuple-element.22), channel_id=1, source_target_pairs={{0,1},{1,2},{2,3},{3,0},{4,5},{5,6},{6,7},{7,4},{8,9},{9,10},{10,1... | collective-permute-start | bytes 1572872 | tf_op jit(solution)/shard_map/ppermute | solution.py:309
  18.5 4.8 %collective-permute-start.1 = (bf16[4,256,256]{2,1,0:T(8,128)(2,1)}, bf16[4,256,256]{2,1,0:T(8,128)(2,1)S(1)}, u32[]{:S(2)}, u32[]{:S(2)}) collective-permute-start(bf16[4,256,256]{2,1,0:T(8,128)(2,1)} %get-tuple-element.23), channel_id=1, source_target_pairs={{0,2},{1,3},{2,0},{3,1},{4,6},{5,7},{6,4},{7,5},{8,10},{9,11},{10,... | collective-permute-start | bytes 1572872 | tf_op jit(solution)/shard_map/ppermute | solution.py:309
  23.3 3.3 %collective-permute-start.2 = (bf16[4,256,256]{2,1,0:T(8,128)(2,1)S(1)}, bf16[4,256,256]{2,1,0:T(8,128)(2,1)S(1)}, u32[]{:S(2)}, u32[]{:S(2)}) collective-permute-start(bf16[4,256,256]{2,1,0:T(8,128)(2,1)S(1)} %get-tuple-element.24), channel_id=1, source_target_pairs={{0,3},{1,0},{2,1},{3,2},{4,7},{5,4},{6,5},{7,6},{8,11},{9,8},{10,9... | collective-permute-start | bytes 1572872 | tf_op jit(solution)/shard_map/ppermute | solution.py:309
  26.6 0.0 all-to-all-done.given_ref
  26.6 0.0 copy-done.4
  26.6 0.0 copy-done.5
  26.6 0.0 copy-done.6
  26.6 0.0 copy-done.8
  26.6 0.0 copy-done.1
  26.6 0.0 copy-done.2
  26.7 0.0 copy-done.3
  26.7 0.0 copy-done.7
  26.7 1.1 %shard_map.65 = bf16[256,256]{1,0:T(8,128)(2,1)S(1)} custom-call(s32[1]{0:T(128)} %bitcast.1.place_ref, bf16[32,56,128]{2,1,0:T(8,128)(2,1)S(1)} %all-to-all-done.given_ref, bf16[16,16,256]{2,1,0:T(8,128)(2,1)S(1)} %copy-done.1, bf16[16,16,256]{2,1,0:T(8,128)(2,1)S(1)} %copy-done.2, f32[2,8,256]{2,1,0:T(8,128)S(1)} %copy-done.7, ...), custom_call_target="tpu_custom_call" | custom-call | tf_op jit(solution)/shard_map/pallas_call | solution.py:315
  27.8 14.3 %all-gather = bf16[512,256]{1,0:T(8,128)(2,1)S(1)} all-gather(bf16[256,256]{1,0:T(8,128)(2,1)S(1)} %shard_map.65), channel_id=2, replica_groups={{4,8},{12,0},{5,9},{13,1},{6,10},{14,2},{7,11},{15,3},{16,20},{24,28},{..., dimensions={0}, use_global_device_ids=true | all-gather | bytes 393216 | tf_op jit(solution)/shard_map/all_gather | solution.py:321
  42.1 18.7 %all-gather.1.gated_ref = bf16[4,256,256]{2,1,0:T(8,128)(2,1)S(1)} all-gather(bf16[2,256,256]{2,1,0:T(8,128)(2,1)S(1)} %bitcast.16), channel_id=3, replica_groups={{4,0},{8,12},{5,1},{9,13},{6,2},{10,14},{7,3},{11,15},{16,28},{20,24},{..., dimensions={0}, use_global_device_ids=true | all-gather | bytes 786432 | tf_op jit(solution)/shard_map/all_gather | solution.py:322
  60.8 0.0 collective-permute-done.refs_0_
  60.8 0.0 collective-permute-done.1.refs_1_
  60.8 0.0 collective-permute-done.2.refs_2_
  60.8 0.7 shard_map.67
  61.5 12.3 %all_to_all.10.part_ref = bf16[4,256,256]{2,1,0:T(8,128)(2,1)S(1)} all-to-all(bf16[4,256,256]{2,1,0:T(8,128)(2,1)S(1)} %shard_map.67), channel_id=1, replica_groups={{0,1,2,3},{4,5,6,7},{8,9,10,11},{12,13,14,15},{16,17,18,19},{20,21,22,2..., dimensions={0} | all-to-all | bytes 1048576 | tf_op jit(solution)/shard_map/all_to_all | solution.py:328
  73.8 0.7 shard_map.68
Async XLA Ops:
  0.0 26.6 %copy-start.4 = (f32[256,16]{0,1:T(8,128)S(1)}, f32[256,16]{0,1:T(8,128)}, u32[]{:S(2)}) copy-start(f32[256,16]{0,1:T(8,128)} %param.9) | copy-start | bytes 49156
  0.0 26.6 %copy-start.5 = (f32[3,256,3]{1,2,0:T(4,128)S(1)}, f32[3,256,3]{1,2,0:T(4,128)}, u32[]{:S(2)}) copy-start(f32[3,256,3]{1,2,0:T(4,128)} %param.7) | copy-start | bytes 27652
  0.0 26.6 %copy-start.6 = (f32[256,16]{0,1:T(8,128)S(1)}, f32[256,16]{0,1:T(8,128)}, u32[]{:S(2)}) copy-start(f32[256,16]{0,1:T(8,128)} %param.8) | copy-start | bytes 49156
  0.0 26.6 %copy-start.8 = (f32[256]{0:T(256)S(1)}, f32[256]{0:T(256)}, u32[]{:S(2)}) copy-start(f32[256]{0:T(256)} %param.10) | copy-start | bytes 3076
  3.1 23.5 %copy-start.1 = (bf16[16,16,256]{2,1,0:T(8,128)(2,1)S(1)}, bf16[16,16,256]{2,1,0:T(8,128)(2,1)}, u32[]{:S(2)}) copy-start(bf16[16,16,256]{2,1,0:T(8,128)(2,1)} %get-tuple-element.16.signal_ref) | copy-start | bytes 393220
  3.1 23.5 %copy-start.2 = (bf16[16,16,256]{2,1,0:T(8,128)(2,1)S(1)}, bf16[16,16,256]{2,1,0:T(8,128)(2,1)}, u32[]{:S(2)}) copy-start(bf16[16,16,256]{2,1,0:T(8,128)(2,1)} %get-tuple-element.17.query_ref) | copy-start | bytes 393220
  3.1 23.5 %copy-start.3 = (f32[16,8,256]{2,1,0:T(8,128)S(1)}, f32[16,8,256]{2,1,0:T(8,128)}, u32[]{:S(2)}) copy-start(f32[16,8,256]{2,1,0:T(8,128)} %get-tuple-element.19.ends_ref) | copy-start | bytes 393220
  3.1 23.5 %copy-start.7 = (f32[2,8,256]{2,1,0:T(8,128)S(1)}, f32[2,8,256]{2,1,0:T(8,128)}, u32[]{:S(2)}) copy-start(f32[2,8,256]{2,1,0:T(8,128)} %get-tuple-element.18.first_ref) | copy-start | bytes 49156
  3.2 23.4 %all-to-all-start = ((bf16[32,56,128]{2,1,0:T(8,128)(2,1)}), bf16[32,56,128]{2,1,0:T(8,128)(2,1)S(1)}, u32[]{:S(2)}, u32[]{:S(2)}) async-start(bf16[32,56,128]{2,1,0:T(8,128)(2,1)} %get-tuple-element.15), calls=%async_computation | async-start | bytes 917504 | tf_op jit(solution)/shard_map/all_to_all | solution.py:297
  12.1 1.6 %copy-start = (bf16[4096,256]{1,0:T(8,128)(2,1)S(1)}, bf16[4096,256]{1,0:T(8,128)(2,1)}, u32[]{:S(2)}) copy-start(bf16[4096,256]{1,0:T(8,128)(2,1)} %param.11) | copy-start | bytes 6291460
  15.5 45.3 %collective-permute-start = (bf16[4,256,256]{2,1,0:T(8,128)(2,1)}, bf16[4,256,256]{2,1,0:T(8,128)(2,1)S(1)}, u32[]{:S(2)}, u32[]{:S(2)}) collective-permute-start(bf16[4,256,256]{2,1,0:T(8,128)(2,1)} %get-tuple-element.22), channel_id=1, source_target_pairs={{0,1},{1,2},{2,3},{3,0},{4,5},{5,6},{6,7},{7,4},{8,9},{9,10},{10,1... | collective-permute-start | bytes 1572872 | tf_op jit(solution)/shard_map/ppermute | solution.py:309
  18.5 42.3 %collective-permute-start.1 = (bf16[4,256,256]{2,1,0:T(8,128)(2,1)}, bf16[4,256,256]{2,1,0:T(8,128)(2,1)S(1)}, u32[]{:S(2)}, u32[]{:S(2)}) collective-permute-start(bf16[4,256,256]{2,1,0:T(8,128)(2,1)} %get-tuple-element.23), channel_id=1, source_target_pairs={{0,2},{1,3},{2,0},{3,1},{4,6},{5,7},{6,4},{7,5},{8,10},{9,11},{10,... | collective-permute-start | bytes 1572872 | tf_op jit(solution)/shard_map/ppermute | solution.py:309
  23.3 37.5 %collective-permute-start.2 = (bf16[4,256,256]{2,1,0:T(8,128)(2,1)S(1)}, bf16[4,256,256]{2,1,0:T(8,128)(2,1)S(1)}, u32[]{:S(2)}, u32[]{:S(2)}) collective-permute-start(bf16[4,256,256]{2,1,0:T(8,128)(2,1)S(1)} %get-tuple-element.24), channel_id=1, source_target_pairs={{0,3},{1,0},{2,1},{3,2},{4,7},{5,4},{6,5},{7,6},{8,11},{9,8},{10,9... | collective-permute-start | bytes 1572872 | tf_op jit(solution)/shard_map/ppermute | solution.py:309

commit v8 on v7

--- a/solution.py
+++ b/solution.py
@@ -163,18 +163,21 @@
         tap = [filter_ref[0, m : m + 1, cols] for m in range(3)]
         q_last = before[at + 2 * SUB + 2 * h : at + 2 * SUB + 2 * h + 2]
         q_more = [tap[1] * q_last[1:2] + tap[2] * q_last[0:1], tap[2] * q_last[1:2]]
-        rate = [spread(decay[m : m + 1]) for m in range(modes)]
-        keep = [jnp.exp(-r) for r in rate]
+        one_step = jnp.exp(-decay)
+        one_chunk = jnp.exp(-float(steps) * decay)
+        chunks = {1: one_chunk, 2: one_chunk * one_chunk}
+        chunks[4] = chunks[2] * chunks[2]
+        aged = [jnp.exp(-float(steps - 1 - n) * decay) for n in range(2)]
+        keep = [spread(one_step[m : m + 1]) for m in range(modes)]
         state = []
         for m in range(modes):
             end = ends_ref[m, :, cols]
-            more = jnp.exp(-float(steps - 1) * decay[m : m + 1]) * firsts[0]
-            more = more + jnp.exp(-float(steps - 2) * decay[m : m + 1]) * firsts[1]
+            more = aged[0][m : m + 1] * firsts[0] + aged[1][m : m + 1] * firsts[1]
             end = jnp.where(chunk_id == 0, end + spread(more), end)
             run = jnp.where(chunk_id == 0, spread(carry[m : m + 1]), pltpu.roll(end, 1, 0))
             for far in (1, 2, 4):
                 moved = jnp.where(chunk_id >= far, pltpu.roll(run, far, 0), 0.0)
-                run = run + jnp.exp(-float(steps * far) * rate[m]) * moved
+                run = run + spread(chunks[far][m : m + 1]) * moved
             state.append(run)
         gain = [spread(weight[m : m + 1]) for m in range(modes)]
         skip = spread(skip_ref[0:1, cols])

time: 74.9 us -> 74.9 us (level)
  no operation moved by 1% of the time
where the time goes in v8:
time: 74.9 us; the launch traced here: 74.5 us
  blocking collectives  45.3 us (60%)
  starting transfers between devices  19.9 us (27%)
  Pallas kernels  7.5 us (10%)
  local copies, waits for them, and re-layouts  1.62 us (2%)
    all_gather x1, blocking collectives, per_device(): lax.all_gather(near, ('ctx', 'ch'), axis_index_groups=rings(1))  18.7 us
    all_gather x1, blocking collectives, per_device(): near = lax.all_gather(gated, ('ctx', 'ch'), axis_index_groups=rings(0))  14.3 us
    all_to_all x1, blocking collectives, per_device(): parts = lax.all_to_all(parts, 'ch', 0, 0, axis_index_groups=along_inner)  12.3 us
    ppermute x3, starting transfers between devices, per_device(): lax.ppermute(part, 'ch', [(a * inner + b, a * inner + (b + k + 1) % inner...  11.1 us
    all_to_all x1, starting transfers between devices, per_device(): given = lax.all_to_all(sent, 'ctx', 0, 0)  8.81 us
    pallas_call x1, Pallas kernels, per_device(): pallas(state_kernel, (shape((blocks, sent_rows, LANES), BF16), shape((ste...  3.12 us
    pallas_call x1, Pallas kernels, per_device(): pallas(roll_kernel, [shape((outer, width, features), BF16)] * inner, (plt...  1.84 us
    unnamed x18, local copies, waits for them, and re-layouts  1.62 us
  transfers between devices with their start and end apart: 4, of which 0 were waited for; matrix products, arithmetic and copies ran while one was open for 0% of the time, Pallas kernels for 4%

profile of v8, /device:TPU:64, one launch (start us, length us, event | category | flops | bytes accessed | tf_op | source)
XLA Modules:
  0.0 74.5 jit_solution(9055694881818199138)
XLA Ops:
  0.0 0.0 copy-start.4
  0.0 0.0 copy-start.5
  0.0 0.0 copy-start.6
  0.0 0.0 copy-start.8
  0.0 3.1 %shard_map.64 = (bf16[32,56,128]{2,1,0:T(8,128)(2,1)}, bf16[16,16,256]{2,1,0:T(8,128)(2,1)}, bf16[16,16,256]{2,1,0:T(8,128)(2,1)}, f32[2,8,256]{2,1,0:T(8,128)}, f32[16,8,256]{2,1,0:T(8,128)}) custom-call(bf16[3,256,256]{2,1,0:T(8,128)(2,1)} %v_ref.1, bf16[3,256,256]{2,1,0:T(8,128)(2,1)} %v_ref.1, bf16[3,256,256]{2,1,0:T(8,128)(2,1)} %v_ref.1, ...), custom_call_target="tpu_custom_call" | custom-call | tf_op jit(solution)/shard_map/pallas_call | solution.py:276
  3.1 0.0 copy-start.1
  3.1 0.0 copy-start.2
  3.1 0.0 copy-start.3
  3.1 0.0 copy-start.7
  3.2 8.8 %all-to-all-start = ((bf16[32,56,128]{2,1,0:T(8,128)(2,1)}), bf16[32,56,128]{2,1,0:T(8,128)(2,1)S(1)}, u32[]{:S(2)}, u32[]{:S(2)}) async-start(bf16[32,56,128]{2,1,0:T(8,128)(2,1)} %get-tuple-element.15), calls=%async_computation | async-start | bytes 917504 | tf_op jit(solution)/shard_map/all_to_all | solution.py:300
  12.0 0.1 pad_add_fusion.place_ref
  12.1 0.0 copy-start
  12.1 1.6 %copy-done = bf16[4096,256]{1,0:T(8,128)(2,1)S(1)} copy-done((bf16[4096,256]{1,0:T(8,128)(2,1)S(1)}, bf16[4096,256]{1,0:T(8,128)(2,1)}, u32[]{:S(2)}) %copy-start) | copy-done | bytes 2097176
  13.6 1.8 %shard_map.66 = (bf16[4,256,256]{2,1,0:T(8,128)(2,1)S(1)}, bf16[4,256,256]{2,1,0:T(8,128)(2,1)}, bf16[4,256,256]{2,1,0:T(8,128)(2,1)}, bf16[4,256,256]{2,1,0:T(8,128)(2,1)S(1)}) custom-call(s32[2]{0:T(128)S(1)} %pad_add_fusion.place_ref, bf16[4,4,256,256]{3,2,1,0:T(8,128)(2,1)S(1)} %bitcast.9), custom_call_target="tpu_custom_call" | custom-call | tf_op jit(solution)/shard_map/pallas_call | solution.py:304
  15.5 3.0 %collective-permute-start = (bf16[4,256,256]{2,1,0:T(8,128)(2,1)}, bf16[4,256,256]{2,1,0:T(8,128)(2,1)S(1)}, u32[]{:S(2)}, u32[]{:S(2)}) collective-permute-start(bf16[4,256,256]{2,1,0:T(8,128)(2,1)} %get-tuple-element.22), channel_id=1, source_target_pairs={{0,1},{1,2},{2,3},{3,0},{4,5},{5,6},{6,7},{7,4},{8,9},{9,10},{10,1... | collective-permute-start | bytes 1572872 | tf_op jit(solution)/shard_map/ppermute | solution.py:312
  18.5 4.8 %collective-permute-start.1 = (bf16[4,256,256]{2,1,0:T(8,128)(2,1)}, bf16[4,256,256]{2,1,0:T(8,128)(2,1)S(1)}, u32[]{:S(2)}, u32[]{:S(2)}) collective-permute-start(bf16[4,256,256]{2,1,0:T(8,128)(2,1)} %get-tuple-element.23), channel_id=1, source_target_pairs={{0,2},{1,3},{2,0},{3,1},{4,6},{5,7},{6,4},{7,5},{8,10},{9,11},{10,... | collective-permute-start | bytes 1572872 | tf_op jit(solution)/shard_map/ppermute | solution.py:312
  23.3 3.3 %collective-permute-start.2 = (bf16[4,256,256]{2,1,0:T(8,128)(2,1)S(1)}, bf16[4,256,256]{2,1,0:T(8,128)(2,1)S(1)}, u32[]{:S(2)}, u32[]{:S(2)}) collective-permute-start(bf16[4,256,256]{2,1,0:T(8,128)(2,1)S(1)} %get-tuple-element.24), channel_id=1, source_target_pairs={{0,3},{1,0},{2,1},{3,2},{4,7},{5,4},{6,5},{7,6},{8,11},{9,8},{10,9... | collective-permute-start | bytes 1572872 | tf_op jit(solution)/shard_map/ppermute | solution.py:312
  26.6 0.0 all-to-all-done.given_ref
  26.6 0.0 copy-done.4
  26.6 0.0 copy-done.5
  26.6 0.0 copy-done.6
  26.6 0.0 copy-done.8
  26.6 0.0 copy-done.1
  26.6 0.0 copy-done.2
  26.7 0.0 copy-done.3
  26.7 0.0 copy-done.7
  26.7 1.1 %shard_map.65 = bf16[256,256]{1,0:T(8,128)(2,1)S(1)} custom-call(s32[1]{0:T(128)} %bitcast.1.place_ref, bf16[32,56,128]{2,1,0:T(8,128)(2,1)S(1)} %all-to-all-done.given_ref, bf16[16,16,256]{2,1,0:T(8,128)(2,1)S(1)} %copy-done.1, bf16[16,16,256]{2,1,0:T(8,128)(2,1)S(1)} %copy-done.2, f32[2,8,256]{2,1,0:T(8,128)S(1)} %copy-done.7, ...), custom_call_target="tpu_custom_call" | custom-call | tf_op jit(solution)/shard_map/pallas_call | solution.py:318
  27.8 14.3 %all-gather = bf16[512,256]{1,0:T(8,128)(2,1)S(1)} all-gather(bf16[256,256]{1,0:T(8,128)(2,1)S(1)} %shard_map.65), channel_id=2, replica_groups={{4,8},{12,0},{5,9},{13,1},{6,10},{14,2},{7,11},{15,3},{16,20},{24,28},{..., dimensions={0}, use_global_device_ids=true | all-gather | bytes 393216 | tf_op jit(solution)/shard_map/all_gather | solution.py:324
  42.1 18.7 %all-gather.1.gated_ref = bf16[4,256,256]{2,1,0:T(8,128)(2,1)S(1)} all-gather(bf16[2,256,256]{2,1,0:T(8,128)(2,1)S(1)} %bitcast.16), channel_id=3, replica_groups={{4,0},{8,12},{5,1},{9,13},{6,2},{10,14},{7,3},{11,15},{16,28},{20,24},{..., dimensions={0}, use_global_device_ids=true | all-gather | bytes 786432 | tf_op jit(solution)/shard_map/all_gather | solution.py:325
  60.8 0.0 collective-permute-done.refs_0_
  60.8 0.0 collective-permute-done.1.refs_1_
  60.8 0.0 collective-permute-done.2.refs_2_
  60.8 0.7 shard_map.67
  61.5 12.3 %all_to_all.10.part_ref = bf16[4,256,256]{2,1,0:T(8,128)(2,1)S(1)} all-to-all(bf16[4,256,256]{2,1,0:T(8,128)(2,1)S(1)} %shard_map.67), channel_id=1, replica_groups={{0,1,2,3},{4,5,6,7},{8,9,10,11},{12,13,14,15},{16,17,18,19},{20,21,22,2..., dimensions={0} | all-to-all | bytes 1048576 | tf_op jit(solution)/shard_map/all_to_all | solution.py:331
  73.8 0.7 shard_map.68
Async XLA Ops:
  0.0 26.6 %copy-start.4 = (f32[256,16]{0,1:T(8,128)S(1)}, f32[256,16]{0,1:T(8,128)}, u32[]{:S(2)}) copy-start(f32[256,16]{0,1:T(8,128)} %param.9) | copy-start | bytes 49156
  0.0 26.6 %copy-start.5 = (f32[3,256,3]{1,2,0:T(4,128)S(1)}, f32[3,256,3]{1,2,0:T(4,128)}, u32[]{:S(2)}) copy-start(f32[3,256,3]{1,2,0:T(4,128)} %param.7) | copy-start | bytes 27652
  0.0 26.6 %copy-start.6 = (f32[256,16]{0,1:T(8,128)S(1)}, f32[256,16]{0,1:T(8,128)}, u32[]{:S(2)}) copy-start(f32[256,16]{0,1:T(8,128)} %param.8) | copy-start | bytes 49156
  0.0 26.6 %copy-start.8 = (f32[256]{0:T(256)S(1)}, f32[256]{0:T(256)}, u32[]{:S(2)}) copy-start(f32[256]{0:T(256)} %param.10) | copy-start | bytes 3076
  3.1 23.5 %copy-start.1 = (bf16[16,16,256]{2,1,0:T(8,128)(2,1)S(1)}, bf16[16,16,256]{2,1,0:T(8,128)(2,1)}, u32[]{:S(2)}) copy-start(bf16[16,16,256]{2,1,0:T(8,128)(2,1)} %get-tuple-element.16.signal_ref) | copy-start | bytes 393220
  3.1 23.5 %copy-start.2 = (bf16[16,16,256]{2,1,0:T(8,128)(2,1)S(1)}, bf16[16,16,256]{2,1,0:T(8,128)(2,1)}, u32[]{:S(2)}) copy-start(bf16[16,16,256]{2,1,0:T(8,128)(2,1)} %get-tuple-element.17.query_ref) | copy-start | bytes 393220
  3.1 23.5 %copy-start.3 = (f32[16,8,256]{2,1,0:T(8,128)S(1)}, f32[16,8,256]{2,1,0:T(8,128)}, u32[]{:S(2)}) copy-start(f32[16,8,256]{2,1,0:T(8,128)} %get-tuple-element.19.ends_ref) | copy-start | bytes 393220
  3.1 23.5 %copy-start.7 = (f32[2,8,256]{2,1,0:T(8,128)S(1)}, f32[2,8,256]{2,1,0:T(8,128)}, u32[]{:S(2)}) copy-start(f32[2,8,256]{2,1,0:T(8,128)} %get-tuple-element.18.first_ref) | copy-start | bytes 49156
  3.2 23.4 %all-to-all-start = ((bf16[32,56,128]{2,1,0:T(8,128)(2,1)}), bf16[32,56,128]{2,1,0:T(8,128)(2,1)S(1)}, u32[]{:S(2)}, u32[]{:S(2)}) async-start(bf16[32,56,128]{2,1,0:T(8,128)(2,1)} %get-tuple-element.15), calls=%async_computation | async-start | bytes 917504 | tf_op jit(solution)/shard_map/all_to_all | solution.py:300
  12.1 1.6 %copy-start = (bf16[4096,256]{1,0:T(8,128)(2,1)S(1)}, bf16[4096,256]{1,0:T(8,128)(2,1)}, u32[]{:S(2)}) copy-start(bf16[4096,256]{1,0:T(8,128)(2,1)} %param.11) | copy-start | bytes 6291460
  15.5 45.3 %collective-permute-start = (bf16[4,256,256]{2,1,0:T(8,128)(2,1)}, bf16[4,256,256]{2,1,0:T(8,128)(2,1)S(1)}, u32[]{:S(2)}, u32[]{:S(2)}) collective-permute-start(bf16[4,256,256]{2,1,0:T(8,128)(2,1)} %get-tuple-element.22), channel_id=1, source_target_pairs={{0,1},{1,2},{2,3},{3,0},{4,5},{5,6},{6,7},{7,4},{8,9},{9,10},{10,1... | collective-permute-start | bytes 1572872 | tf_op jit(solution)/shard_map/ppermute | solution.py:312
  18.5 42.3 %collective-permute-start.1 = (bf16[4,256,256]{2,1,0:T(8,128)(2,1)}, bf16[4,256,256]{2,1,0:T(8,128)(2,1)S(1)}, u32[]{:S(2)}, u32[]{:S(2)}) collective-permute-start(bf16[4,256,256]{2,1,0:T(8,128)(2,1)} %get-tuple-element.23), channel_id=1, source_target_pairs={{0,2},{1,3},{2,0},{3,1},{4,6},{5,7},{6,4},{7,5},{8,10},{9,11},{10,... | collective-permute-start | bytes 1572872 | tf_op jit(solution)/shard_map/ppermute | solution.py:312
  23.3 37.5 %collective-permute-start.2 = (bf16[4,256,256]{2,1,0:T(8,128)(2,1)S(1)}, bf16[4,256,256]{2,1,0:T(8,128)(2,1)S(1)}, u32[]{:S(2)}, u32[]{:S(2)}) collective-permute-start(bf16[4,256,256]{2,1,0:T(8,128)(2,1)S(1)} %get-tuple-element.24), channel_id=1, source_target_pairs={{0,3},{1,0},{2,1},{3,2},{4,7},{5,4},{6,5},{7,6},{8,11},{9,8},{10,9... | collective-permute-start | bytes 1572872 | tf_op jit(solution)/shard_map/ppermute | solution.py:312

commit v9 on v8

--- a/solution.py
+++ b/solution.py
@@ -76,7 +76,8 @@
     from_end = float(steps) * (SUB - 1 - chunk_id).astype(F32)
     for h, cols in enumerate(halves(width)):
         rate = [spread(decay_ref[m : m + 1, cols]) for m in range(modes)]
-        keep = [jnp.exp(-r) for r in rate]
+        one_step = jnp.exp(-decay_ref[:, cols])
+        keep = [spread(one_step[m : m + 1]) for m in range(modes)]
         state = [jnp.zeros((SUB, LANES), F32) for _ in range(modes)]
         pair = []
         for p, signal in enumerate(signal_steps((line_ref, 1), (line_ref, 2), filter_ref, h, cols, steps)):

time: 74.9 us -> 74.9 us (level)
  no operation moved by 1% of the time
where the time goes in v9:
time: 74.9 us; the launch traced here: 74.5 us
  blocking collectives  45.3 us (60%)
  starting transfers between devices  19.9 us (27%)
  Pallas kernels  7.51 us (10%)
  local copies, waits for them, and re-layouts  1.62 us (2%)
    all_gather x1, blocking collectives, per_device(): lax.all_gather(near, ('ctx', 'ch'), axis_index_groups=rings(1))  18.7 us
    all_gather x1, blocking collectives, per_device(): near = lax.all_gather(gated, ('ctx', 'ch'), axis_index_groups=rings(0))  14.3 us
    all_to_all x1, blocking collectives, per_device(): parts = lax.all_to_all(parts, 'ch', 0, 0, axis_index_groups=along_inner)  12.3 us
    ppermute x3, starting transfers between devices, per_device(): lax.ppermute(part, 'ch', [(a * inner + b, a * inner + (b + k + 1) % inner...  11.1 us
    all_to_all x1, starting transfers between devices, per_device(): given = lax.all_to_all(sent, 'ctx', 0, 0)  8.81 us
    pallas_call x1, Pallas kernels, per_device(): pallas(state_kernel, (shape((blocks, sent_rows, LANES), BF16), shape((ste...  3.13 us
    pallas_call x1, Pallas kernels, per_device(): pallas(roll_kernel, [shape((outer, width, features), BF16)] * inner, (plt...  1.84 us
    unnamed x18, local copies, waits for them, and re-layouts  1.62 us
  transfers between devices with their start and end apart: 4, of which 0 were waited for; matrix products, arithmetic and copies ran while one was open for 0% of the time, Pallas kernels for 4%

profile of v9, /device:TPU:64, one launch (start us, length us, event | category | flops | bytes accessed | tf_op | source)
XLA Modules:
  0.0 74.5 jit_solution(272838918240008199)
XLA Ops:
  0.0 0.0 copy-start.4
  0.0 0.0 copy-start.5
  0.0 0.0 copy-start.6
  0.0 0.0 copy-start.8
  0.0 3.1 %shard_map.64 = (bf16[32,56,128]{2,1,0:T(8,128)(2,1)}, bf16[16,16,256]{2,1,0:T(8,128)(2,1)}, bf16[16,16,256]{2,1,0:T(8,128)(2,1)}, f32[2,8,256]{2,1,0:T(8,128)}, f32[16,8,256]{2,1,0:T(8,128)}) custom-call(bf16[3,256,256]{2,1,0:T(8,128)(2,1)} %v_ref.1, bf16[3,256,256]{2,1,0:T(8,128)(2,1)} %v_ref.1, bf16[3,256,256]{2,1,0:T(8,128)(2,1)} %v_ref.1, ...), custom_call_target="tpu_custom_call" | custom-call | tf_op jit(solution)/shard_map/pallas_call | solution.py:277
  3.1 0.0 copy-start.1
  3.1 0.0 copy-start.2
  3.2 0.0 copy-start.3
  3.2 0.0 copy-start.7
  3.2 8.8 %all-to-all-start = ((bf16[32,56,128]{2,1,0:T(8,128)(2,1)}), bf16[32,56,128]{2,1,0:T(8,128)(2,1)S(1)}, u32[]{:S(2)}, u32[]{:S(2)}) async-start(bf16[32,56,128]{2,1,0:T(8,128)(2,1)} %get-tuple-element.15), calls=%async_computation | async-start | bytes 917504 | tf_op jit(solution)/shard_map/all_to_all | solution.py:301
  12.0 0.1 pad_add_fusion.place_ref
  12.1 0.0 copy-start
  12.1 1.6 %copy-done = bf16[4096,256]{1,0:T(8,128)(2,1)S(1)} copy-done((bf16[4096,256]{1,0:T(8,128)(2,1)S(1)}, bf16[4096,256]{1,0:T(8,128)(2,1)}, u32[]{:S(2)}) %copy-start) | copy-done | bytes 2097176
  13.7 1.8 %shard_map.66 = (bf16[4,256,256]{2,1,0:T(8,128)(2,1)S(1)}, bf16[4,256,256]{2,1,0:T(8,128)(2,1)}, bf16[4,256,256]{2,1,0:T(8,128)(2,1)}, bf16[4,256,256]{2,1,0:T(8,128)(2,1)S(1)}) custom-call(s32[2]{0:T(128)S(1)} %pad_add_fusion.place_ref, bf16[4,4,256,256]{3,2,1,0:T(8,128)(2,1)S(1)} %bitcast.9), custom_call_target="tpu_custom_call" | custom-call | tf_op jit(solution)/shard_map/pallas_call | solution.py:305
  15.5 3.0 %collective-permute-start = (bf16[4,256,256]{2,1,0:T(8,128)(2,1)}, bf16[4,256,256]{2,1,0:T(8,128)(2,1)S(1)}, u32[]{:S(2)}, u32[]{:S(2)}) collective-permute-start(bf16[4,256,256]{2,1,0:T(8,128)(2,1)} %get-tuple-element.22), channel_id=1, source_target_pairs={{0,1},{1,2},{2,3},{3,0},{4,5},{5,6},{6,7},{7,4},{8,9},{9,10},{10,1... | collective-permute-start | bytes 1572872 | tf_op jit(solution)/shard_map/ppermute | solution.py:313
  18.5 4.8 %collective-permute-start.1 = (bf16[4,256,256]{2,1,0:T(8,128)(2,1)}, bf16[4,256,256]{2,1,0:T(8,128)(2,1)S(1)}, u32[]{:S(2)}, u32[]{:S(2)}) collective-permute-start(bf16[4,256,256]{2,1,0:T(8,128)(2,1)} %get-tuple-element.23), channel_id=1, source_target_pairs={{0,2},{1,3},{2,0},{3,1},{4,6},{5,7},{6,4},{7,5},{8,10},{9,11},{10,... | collective-permute-start | bytes 1572872 | tf_op jit(solution)/shard_map/ppermute | solution.py:313
  23.3 3.3 %collective-permute-start.2 = (bf16[4,256,256]{2,1,0:T(8,128)(2,1)S(1)}, bf16[4,256,256]{2,1,0:T(8,128)(2,1)S(1)}, u32[]{:S(2)}, u32[]{:S(2)}) collective-permute-start(bf16[4,256,256]{2,1,0:T(8,128)(2,1)S(1)} %get-tuple-element.24), channel_id=1, source_target_pairs={{0,3},{1,0},{2,1},{3,2},{4,7},{5,4},{6,5},{7,6},{8,11},{9,8},{10,9... | collective-permute-start | bytes 1572872 | tf_op jit(solution)/shard_map/ppermute | solution.py:313
  26.6 0.0 all-to-all-done.given_ref
  26.6 0.0 copy-done.4
  26.6 0.0 copy-done.5
  26.6 0.0 copy-done.6
  26.6 0.0 copy-done.8
  26.6 0.0 copy-done.1
  26.7 0.0 copy-done.2
  26.7 0.0 copy-done.3
  26.7 0.0 copy-done.7
  26.7 1.1 %shard_map.65 = bf16[256,256]{1,0:T(8,128)(2,1)S(1)} custom-call(s32[1]{0:T(128)} %bitcast.1.place_ref, bf16[32,56,128]{2,1,0:T(8,128)(2,1)S(1)} %all-to-all-done.given_ref, bf16[16,16,256]{2,1,0:T(8,128)(2,1)S(1)} %copy-done.1, bf16[16,16,256]{2,1,0:T(8,128)(2,1)S(1)} %copy-done.2, f32[2,8,256]{2,1,0:T(8,128)S(1)} %copy-done.7, ...), custom_call_target="tpu_custom_call" | custom-call | tf_op jit(solution)/shard_map/pallas_call | solution.py:319
  27.8 14.3 %all-gather = bf16[512,256]{1,0:T(8,128)(2,1)S(1)} all-gather(bf16[256,256]{1,0:T(8,128)(2,1)S(1)} %shard_map.65), channel_id=2, replica_groups={{4,8},{12,0},{5,9},{13,1},{6,10},{14,2},{7,11},{15,3},{16,20},{24,28},{..., dimensions={0}, use_global_device_ids=true | all-gather | bytes 393216 | tf_op jit(solution)/shard_map/all_gather | solution.py:325
  42.1 18.7 %all-gather.1.gated_ref = bf16[4,256,256]{2,1,0:T(8,128)(2,1)S(1)} all-gather(bf16[2,256,256]{2,1,0:T(8,128)(2,1)S(1)} %bitcast.16), channel_id=3, replica_groups={{4,0},{8,12},{5,1},{9,13},{6,2},{10,14},{7,3},{11,15},{16,28},{20,24},{..., dimensions={0}, use_global_device_ids=true | all-gather | bytes 786432 | tf_op jit(solution)/shard_map/all_gather | solution.py:326
  60.8 0.0 collective-permute-done.refs_0_
  60.8 0.0 collective-permute-done.1.refs_1_
  60.8 0.0 collective-permute-done.2.refs_2_
  60.8 0.7 shard_map.67
  61.5 12.3 %all_to_all.10.part_ref = bf16[4,256,256]{2,1,0:T(8,128)(2,1)S(1)} all-to-all(bf16[4,256,256]{2,1,0:T(8,128)(2,1)S(1)} %shard_map.67), channel_id=1, replica_groups={{0,1,2,3},{4,5,6,7},{8,9,10,11},{12,13,14,15},{16,17,18,19},{20,21,22,2..., dimensions={0} | all-to-all | bytes 1048576 | tf_op jit(solution)/shard_map/all_to_all | solution.py:332
  73.8 0.7 shard_map.68
Async XLA Ops:
  0.0 26.6 %copy-start.4 = (f32[256,16]{0,1:T(8,128)S(1)}, f32[256,16]{0,1:T(8,128)}, u32[]{:S(2)}) copy-start(f32[256,16]{0,1:T(8,128)} %param.9) | copy-start | bytes 49156
  0.0 26.6 %copy-start.5 = (f32[3,256,3]{1,2,0:T(4,128)S(1)}, f32[3,256,3]{1,2,0:T(4,128)}, u32[]{:S(2)}) copy-start(f32[3,256,3]{1,2,0:T(4,128)} %param.7) | copy-start | bytes 27652
  0.0 26.6 %copy-start.6 = (f32[256,16]{0,1:T(8,128)S(1)}, f32[256,16]{0,1:T(8,128)}, u32[]{:S(2)}) copy-start(f32[256,16]{0,1:T(8,128)} %param.8) | copy-start | bytes 49156
  0.0 26.6 %copy-start.8 = (f32[256]{0:T(256)S(1)}, f32[256]{0:T(256)}, u32[]{:S(2)}) copy-start(f32[256]{0:T(256)} %param.10) | copy-start | bytes 3076
  3.1 23.5 %copy-start.1 = (bf16[16,16,256]{2,1,0:T(8,128)(2,1)S(1)}, bf16[16,16,256]{2,1,0:T(8,128)(2,1)}, u32[]{:S(2)}) copy-start(bf16[16,16,256]{2,1,0:T(8,128)(2,1)} %get-tuple-element.16.signal_ref) | copy-start | bytes 393220
  3.1 23.5 %copy-start.2 = (bf16[16,16,256]{2,1,0:T(8,128)(2,1)S(1)}, bf16[16,16,256]{2,1,0:T(8,128)(2,1)}, u32[]{:S(2)}) copy-start(bf16[16,16,256]{2,1,0:T(8,128)(2,1)} %get-tuple-element.17.query_ref) | copy-start | bytes 393220
  3.2 23.5 %copy-start.3 = (f32[16,8,256]{2,1,0:T(8,128)S(1)}, f32[16,8,256]{2,1,0:T(8,128)}, u32[]{:S(2)}) copy-start(f32[16,8,256]{2,1,0:T(8,128)} %get-tuple-element.19.ends_ref) | copy-start | bytes 393220
  3.2 23.5 %copy-start.7 = (f32[2,8,256]{2,1,0:T(8,128)S(1)}, f32[2,8,256]{2,1,0:T(8,128)}, u32[]{:S(2)}) copy-start(f32[2,8,256]{2,1,0:T(8,128)} %get-tuple-element.18.first_ref) | copy-start | bytes 49156
  3.2 23.4 %all-to-all-start = ((bf16[32,56,128]{2,1,0:T(8,128)(2,1)}), bf16[32,56,128]{2,1,0:T(8,128)(2,1)S(1)}, u32[]{:S(2)}, u32[]{:S(2)}) async-start(bf16[32,56,128]{2,1,0:T(8,128)(2,1)} %get-tuple-element.15), calls=%async_computation | async-start | bytes 917504 | tf_op jit(solution)/shard_map/all_to_all | solution.py:301
  12.1 1.6 %copy-start = (bf16[4096,256]{1,0:T(8,128)(2,1)S(1)}, bf16[4096,256]{1,0:T(8,128)(2,1)}, u32[]{:S(2)}) copy-start(bf16[4096,256]{1,0:T(8,128)(2,1)} %param.11) | copy-start | bytes 6291460
  15.5 45.3 %collective-permute-start = (bf16[4,256,256]{2,1,0:T(8,128)(2,1)}, bf16[4,256,256]{2,1,0:T(8,128)(2,1)S(1)}, u32[]{:S(2)}, u32[]{:S(2)}) collective-permute-start(bf16[4,256,256]{2,1,0:T(8,128)(2,1)} %get-tuple-element.22), channel_id=1, source_target_pairs={{0,1},{1,2},{2,3},{3,0},{4,5},{5,6},{6,7},{7,4},{8,9},{9,10},{10,1... | collective-permute-start | bytes 1572872 | tf_op jit(solution)/shard_map/ppermute | solution.py:313
  18.5 42.3 %collective-permute-start.1 = (bf16[4,256,256]{2,1,0:T(8,128)(2,1)}, bf16[4,256,256]{2,1,0:T(8,128)(2,1)S(1)}, u32[]{:S(2)}, u32[]{:S(2)}) collective-permute-start(bf16[4,256,256]{2,1,0:T(8,128)(2,1)} %get-tuple-element.23), channel_id=1, source_target_pairs={{0,2},{1,3},{2,0},{3,1},{4,6},{5,7},{6,4},{7,5},{8,10},{9,11},{10,... | collective-permute-start | bytes 1572872 | tf_op jit(solution)/shard_map/ppermute | solution.py:313
  23.3 37.5 %collective-permute-start.2 = (bf16[4,256,256]{2,1,0:T(8,128)(2,1)S(1)}, bf16[4,256,256]{2,1,0:T(8,128)(2,1)S(1)}, u32[]{:S(2)}, u32[]{:S(2)}) collective-permute-start(bf16[4,256,256]{2,1,0:T(8,128)(2,1)S(1)} %get-tuple-element.24), channel_id=1, source_target_pairs={{0,3},{1,0},{2,1},{3,2},{4,7},{5,4},{6,5},{7,6},{8,11},{9,8},{10,9... | collective-permute-start | bytes 1572872 | tf_op jit(solution)/shard_map/ppermute | solution.py:313
